TPU v7x, 512 devices: a whole 4x4x16 slice. The times are simulated.
512 devices in a mesh: tm: 32 (over x, z_lo), space: 16 (over y, z_hi, core).
Axes of the slice: x: 4, y: 4, z: 16 (z_hi: 2, z_lo: 8; z = z_hi * 8 + z_lo), core: 2. Of those that a mesh axis runs over, the one named last changes fastest.
Arguments:
- u_old: float32 [32, 5, 256, 16, 128], P('tm', None, 'space'), may hold values from -2.5 to 2.5
- u_init: float32 [256, 16, 128], P('space'), may hold values from -2.5 to 2.5
Outputs:
- u_new: float32 [32, 5, 256, 16, 128], P('tm', None, 'space')
All inputs are finite; a program needn't handle non-finite values.
Results may differ from a plain program's by a relative error of at most 0.0003.
Values sent between devices are 32-bit elements; how exact they have to be, the bound alone decides.
No kernel may reach another device: no remote copies, remote signals or barrier semaphores. Data moves between devices by JAX's collectives and lax.ppermute only.
A program may use at most 64 MiB of HBM per device.

v0:
```python
import math

import jax
import jax.numpy as jnp
from jax import lax
from jax.sharding import Mesh
from jax.sharding import PartitionSpec as P

SPACE = ("space_0", "space_1", "space_2")


step_length = 0.4
diffusion = 1.0
reaction = 1.0


def passed_along(value, axis, steps):
    count = lax.axis_size(axis)
    leading, last = (max(0, -steps), min(count, count - steps))
    return lax.ppermute(value, axis, [(source, source + steps) for source in range(leading, last)])


def padded_2(x, sides, width):
    for axis, dim in sides:
        count, length = (lax.axis_size(axis), x.shape[dim])
        up = [(i, (i + 1) % count) for i in range(count)]
        down = [(j, i) for i, j in up]
        last = lax.slice_in_dim(x, length - width, length, axis=dim)
        leading = lax.slice_in_dim(x, 0, width, axis=dim)
        before = lax.ppermute(last, axis, up)
        after = lax.ppermute(leading, axis, down)
        x = jnp.concatenate([before, x, after], axis=dim)
    return x


def split_up(x, dim, count):
    before, after = (x.shape[:dim], x.shape[dim + 1 :])
    return jnp.moveaxis(x.reshape(*before, count, -1, *after), dim, 0)


def laid_out(parts, dim):
    parts = jnp.moveaxis(parts, 0, dim)
    lengths = parts.shape
    return parts.reshape(*lengths[:dim], lengths[dim] * lengths[dim + 1], *lengths[dim + 2 :])


def turned_blocks(parts, axes, sequence):
    lengths = [lax.axis_size(a) for a in axes]
    parts = parts.reshape(*lengths, *parts.shape[1:])
    for k in sequence:
        parts = lax.all_to_all(parts, axes[k], split_axis=k, concat_axis=k, tiled=True)
    return parts.reshape(-1, *parts.shape[len(axes) :])


def core_and_chips(x, groups, sequence, split_dim, concat_dim):
    count = lax.axis_size(groups[0]) * lax.axis_size(groups[1])
    parts = split_up(x, split_dim, count)
    return laid_out(turned_blocks(parts, groups, sequence), concat_dim)


def copy_for_each(x, axis):
    copies = jnp.broadcast_to(x, (lax.axis_size(axis), *x.shape))
    return lax.all_to_all(copies, axis, split_axis=0, concat_axis=0, tiled=True)


def collected_together(x, axis):
    leaves = jax.tree.leaves(x)
    sequence = sorted(range(len(leaves)), key=lambda k: -leaves[k].size)
    width = (1, *leaves[sequence[0]].shape)[-1]
    lines = [
        jnp.pad(leaves[k].reshape(-1), (0, -leaves[k].size % width)).reshape(-1, width)
        for k in sequence
    ]
    both, at, found = (copy_for_each(jnp.concatenate(lines), axis), 0, {})
    for k, line in zip(sequence, lines):
        piece = both[:, at : at + len(line)].reshape(len(both), -1)
        found[k] = piece[:, : leaves[k].size].reshape(-1, *leaves[k].shape)
        at += len(line)
    numbers = iter(range(len(leaves)))
    return jax.tree.map(lambda _: found[next(numbers)], x)


def combined_pairwise(pieces, combine):
    while len(jax.tree.leaves(pieces)[0]) > 1:
        pieces = jax.vmap(combine)(
            *(jax.tree.map(lambda part: part[side::2], pieces) for side in (0, 1))
        )
    return jax.tree.map(lambda part: part[0], pieces)


def carried_in(x, axis, combine, identity):
    count, index = (lax.axis_size(axis), lax.axis_index(axis))
    passed = jnp.arange(count) < index

    def kept(part, zero, own):
        part = jnp.where(
            passed.reshape(-1, *(1 for _ in own.shape)), part, jnp.asarray(zero, own.dtype)
        )
        return part

    pieces = collected_together(x, axis)
    return combined_pairwise(jax.tree.map(kept, pieces, identity, x), combine)


def basis_coefficients(nodes, chosen):
    polynomial = [1.0]
    for other, point in enumerate(nodes):
        if other == chosen:
            continue
        divisor = nodes[chosen] - point
        widened = [0.0] * (len(polynomial) + 1)
        for power, value in enumerate(polynomial):
            widened[power + 1] += value / divisor
            widened[power] -= value * point / divisor
        polynomial = widened
    return polynomial


def basis_value(nodes, chosen, where):
    result = 1.0
    for other, point in enumerate(nodes):
        if other != chosen:
            result *= (where - point) / (nodes[chosen] - point)
    return result


def node_tables():
    root = math.sqrt(3.0 / 7.0)
    fine_tau = [0.0, (1.0 - root) / 2.0, 0.5, (1.0 + root) / 2.0, 1.0]
    coarse_tau = [0.0, 0.5, 1.0]
    integ = []
    for j in range(4):
        row_values = []
        for k in range(5):
            polynomial = basis_coefficients(fine_tau, k)
            total = 0.0
            for power, value in enumerate(polynomial):
                total += (
                    value
                    * (fine_tau[j + 1] ** (power + 1) - fine_tau[j] ** (power + 1))
                    / (power + 1)
                )
            row_values.append(total)
        integ.append(row_values)
    interp = [[basis_value(coarse_tau, c, fine_tau[m]) for c in range(3)] for m in range(5)]
    spacing = [float(fine_tau[j + 1] - fine_tau[j]) for j in range(4)]
    return (jnp.asarray(integ, jnp.float32), spacing, jnp.asarray(interp, jnp.float32))


def hartley(length):
    counter = jnp.arange(length, dtype=jnp.int32)
    product = counter[:, None] * counter[None, :] % length
    phase = 2.0 * jnp.pi * product.astype(jnp.float32) / length
    return (jnp.cos(phase) + jnp.sin(phase)) / math.sqrt(length)


def local_force(padded):
    field = padded[:, 1:-1]
    near = padded[:, 2:] + padded[:, :-2] + jnp.roll(field, 1, 2) + jnp.roll(field, -1, 2)
    near = near + jnp.roll(field, 1, 3) + jnp.roll(field, -1, 3)
    return diffusion * (near - 6.0 * field) + reaction * (field - field * field * field)


def inner_planes(field, margin):
    return field[margin : field.shape[0] - margin]


def restrict(field):
    depth, rows, cols = field.shape
    return (
        field.reshape(depth // 2, 2, rows // 2, 2, cols // 2, 2)
        .mean(axis=(1, 3, 5))
        .reshape(depth // 2, rows * cols // 4)
    )


def compose(earlier, later):
    return (later[0] * earlier[0], later[0] * earlier[1] + later[1])


def shards(u_old, u_init):
    integ, spacing, interp = node_tables()
    highest = lax.Precision.HIGHEST
    depth, rows, cols = u_init.shape
    fine_old = u_old[0]
    previous = passed_along(fine_old[4], "tm", 1)
    position = lax.axis_index("tm")
    start = jnp.where(position == 0, u_init, previous)
    states = [start]
    forces = []
    together = jnp.concatenate([start[None], fine_old], 0)
    wide = padded_2(together, ((SPACE, 1),), 5)
    fold_wide = local_force(wide[1:])
    iold_wide = step_length * jnp.einsum("jk,kzxy->jzxy", integ, fold_wide, precision=highest)
    current = wide[0]
    for section in range(4):
        force_now = local_force(current[None])[0]
        forces.append(inner_planes(force_now, 4 - section))
        following = (
            inner_planes(current, 1)
            + step_length
            * spacing[section]
            * (force_now - inner_planes(fold_wide[section], section))
            + inner_planes(iold_wide[section], section)
        )
        states.append(inner_planes(following, 4 - section))
        current = following
    forces.append(local_force(current[None])[0])
    inew = step_length * jnp.einsum("jk,kzxy->jzxy", integ, jnp.stack(forces), precision=highest)
    stacked = jnp.stack(
        [
            restrict(states[0]),
            restrict(states[2]),
            restrict(states[4]),
            restrict(inew[0] + inew[1]),
            restrict(inew[2] + inew[3]),
            restrict(u_init),
        ]
    )
    planes_c = depth // 2
    rows_c = rows // 2
    cols_c = cols // 2
    depth_c = planes_c * lax.axis_size(SPACE)
    table_xy = jnp.kron(hartley(rows_c), hartley(cols_c))
    table_z = hartley(depth_c)
    spectral_xy = jnp.einsum("fzc,cd->fzd", stacked, table_xy, precision=highest)
    wave_z = jnp.arange(depth_c, dtype=jnp.int32)
    wave_xy = jnp.arange(rows_c * cols_c, dtype=jnp.int32)
    angle_z = 2.0 * jnp.cos(2.0 * jnp.pi * wave_z.astype(jnp.float32) / depth_c)
    angle_x = 2.0 * jnp.cos(2.0 * jnp.pi * (wave_xy // cols_c).astype(jnp.float32) / rows_c)
    angle_y = 2.0 * jnp.cos(2.0 * jnp.pi * (wave_xy % cols_c).astype(jnp.float32) / cols_c)
    eigen_all = 0.25 * (angle_z[:, None] + angle_x[None, :] + angle_y[None, :] - 6.0)
    place = lax.axis_index(SPACE)
    columns = core_and_chips(spectral_xy, (("space_0", "space_1"), "space_2"), (1, 0), 2, 1)
    spectra = jnp.einsum("qz,fzc->fqc", table_z, columns, precision=highest)
    width = columns.shape[2]
    eigen = lax.dynamic_slice_in_dim(eigen_all, place * width, width, 1)
    pieces = [spectra[k] for k in range(6)]
    damping = 0.5 * step_length * diffusion * eigen
    denom = 1.0 - damping
    lifted0 = pieces[3] - damping * pieces[1]
    lifted1 = pieces[4] - damping * pieces[2]
    slope = 1.0 / (denom * denom)
    offset = (lifted0 / denom + lifted1) / denom
    before_slope, before_offset = carried_in(
        (slope, offset), "tm", compose, (jnp.ones_like(slope), jnp.zeros_like(offset))
    )
    begin = before_slope * pieces[5] + before_offset
    middle = (begin + lifted0) / denom
    finish = (middle + lifted1) / denom
    delta = jnp.stack([begin - pieces[0], middle - pieces[1], finish - pieces[2]])
    planar = jnp.einsum("zq,fqc->fzc", table_z, delta, precision=highest)
    returned = lax.all_to_all(planar, SPACE, split_axis=1, concat_axis=2, tiled=True)
    real_space = jnp.einsum("fzc,cd->fzd", returned, table_xy, precision=highest)
    coarse_grid = real_space.reshape(3, planes_c, rows_c, cols_c)
    timed = jnp.einsum("mc,czxy->mzxy", interp, coarse_grid, precision=highest)
    upper = jnp.repeat(jnp.repeat(jnp.repeat(timed, 2, 1), 2, 2), 2, 3)
    return (jnp.stack(states) + upper)[None]


def solution(mesh):
    finer = Mesh(
        mesh.devices.reshape(mesh.shape["tm"], 4, 2, 2), ("tm", "space_0", "space_1", "space_2")
    )
    in_specs = (P("tm", None, SPACE, None, None), P(SPACE, None, None))
    out_specs = P("tm", None, SPACE, None, None)
    return jax.shard_map(
        shards, mesh=finer, in_specs=in_specs, out_specs=out_specs, check_vma=False
    )
```

profile of v0, /device:TPU:1, one launch (start us, length us, event | category | flops | bytes accessed | tf_op | source)
XLA Modules:
  0.0 267.7 jit_solution(8408288563641661195)
XLA Ops:
  0.9 4.4 %collective-permute-start = (f32[16,16,128]{2,1,0:T(8,128)S(1)}, f32[16,16,128]{2,1,0:T(8,128)S(1)}, u32[]{:S(2)}, u32[]{:S(2)}) collective-permute-start(f32[16,16,128]{2,1,0:T(8,128)S(1)} %slice_bitcast_fusion.2), channel_id=1, source_target_pairs={{0,16},{16,32},{32,48},{48,64},{64,80},{80,96},{96,112},{112,128},... | collective-permute-start | bytes 393224 | tf_op jit(solution)/shard_map/ppermute | solution.py:20
  5.5 10.5 %reshape.343 = f32[8,2,8,2,64,2]{5,4,3,2,1,0:T(8,128)} reshape(f32[16,16,128]{2,1,0:T(8,128)} %param.5) | data formatting | bytes 262144 | tf_op jit(solution)/shard_map/reshape | solution.py:171
  16.0 4.0 %reduce_sum.59 = f32[8,8,64]{2,1,0:T(8,128)S(1)} reduce(f32[8,2,8,2,64,2]{5,4,3,2,1,0:T(8,128)} %reshape.343, f32[]{:T(128)} %constant.162.clone.1), dimensions={1,3,5}, to_apply=%region_5.6 | reduce | flops 28672 | bytes 147460 | tf_op jit(solution)/shard_map/reduce_sum | solution.py:172
  24.3 9.7 %reshape.340 = f32[8,2,8,2,64,2]{5,4,3,2,1,0:T(8,128)} reshape(f32[16,16,128]{2,1,0:T(8,128)S(1)} %get-tuple-element.20) | data formatting | bytes 262144 | tf_op jit(solution)/shard_map/reshape | solution.py:171
  34.1 15.4 %collective-permute-start.1 = (f32[6,5,16,128]{3,2,1,0:T(8,128)S(1)}, f32[6,5,16,128]{3,2,1,0:T(8,128)S(1)}, u32[]{:S(2)}, u32[]{:S(2)}) collective-permute-start(f32[6,5,16,128]{3,2,1,0:T(8,128)S(1)} %get-tuple-element.35), channel_id=1, source_target_pairs={{0,1},{1,2},{2,3},{3,4},{4,5},{5,6},{6,7},{7,8},{8,9},{9,10},{10,1... | collective-permute-start | bytes 737288 | tf_op jit(solution)/shard_map/ppermute | solution.py:30
  51.6 4.0 %reduce_sum.54 = f32[8,8,64]{2,1,0:T(8,128)S(1)} reduce(f32[8,2,8,2,64,2]{5,4,3,2,1,0:T(8,128)} %reshape.340, f32[]{:T(128)} %constant.162.clone.1), dimensions={1,3,5}, to_apply=%region_0.1 | reduce | flops 28672 | bytes 147460 | tf_op jit(solution)/shard_map/reduce_sum | solution.py:172
  55.7 13.5 %collective-permute-done.1 = f32[6,5,16,128]{3,2,1,0:T(8,128)S(1)} collective-permute-done((f32[6,5,16,128]{3,2,1,0:T(8,128)S(1)}, f32[6,5,16,128]{3,2,1,0:T(8,128)S(1)}, u32[]{:S(2)}, u32[]{:S(2)}) %collective-permute-start.1) | collective-permute-done | bytes 245792 | tf_op jit(solution)/shard_map/ppermute | solution.py:30
  69.2 7.4 %collective-permute-done.2 = f32[6,5,16,128]{3,2,1,0:T(8,128)S(1)} collective-permute-done((f32[6,5,16,128]{3,2,1,0:T(8,128)S(1)}, f32[6,5,16,128]{3,2,1,0:T(8,128)S(1)}, u32[]{:S(2)}, u32[]{:S(2)}) %collective-permute-start.2) | collective-permute-done | bytes 245792 | tf_op jit(solution)/shard_map/ppermute | solution.py:31
  85.1 10.0 %add.346 = f32[8,2,8,2,64,2]{5,4,3,2,1,0:T(8,128)} reshape(f32[16,16,128]{2,1,0:T(8,128)S(1)} %get-tuple-element.6) | data formatting | bytes 262144 | tf_op jit(solution)/shard_map/add | solution.py:215
  95.1 4.0 %reduce_sum.57 = f32[8,8,64]{2,1,0:T(8,128)S(1)} reduce(f32[8,2,8,2,64,2]{5,4,3,2,1,0:T(8,128)} %add.346, f32[]{:T(128)} %constant.162.clone.1), dimensions={1,3,5}, to_apply=%region_3.4 | reduce | flops 28672 | bytes 147460 | tf_op jit(solution)/shard_map/reduce_sum | solution.py:172
  99.2 9.7 %reshape.342 = f32[8,2,8,2,64,2]{5,4,3,2,1,0:T(8,128)} reshape(f32[1,16,16,128]{3,2,1,0:T(8,128)S(1)} %get-tuple-element.66) | data formatting | bytes 262144 | tf_op jit(solution)/shard_map/reshape | solution.py:171
  109.0 4.0 %reduce_sum.56 = f32[8,8,64]{2,1,0:T(8,128)S(1)} reduce(f32[8,2,8,2,64,2]{5,4,3,2,1,0:T(8,128)} %reshape.342, f32[]{:T(128)} %constant.162.clone.1), dimensions={1,3,5}, to_apply=%region_2.3 | reduce | flops 28672 | bytes 147460 | tf_op jit(solution)/shard_map/reduce_sum | solution.py:172
  113.1 9.7 %reshape.341 = f32[8,2,8,2,64,2]{5,4,3,2,1,0:T(8,128)} reshape(f32[1,16,16,128]{3,2,1,0:T(8,128)S(1)} %slice.664) | data formatting | bytes 262144 | tf_op jit(solution)/shard_map/reshape | solution.py:171
  122.8 4.0 %reduce_sum.55 = f32[8,8,64]{2,1,0:T(8,128)S(1)} reduce(f32[8,2,8,2,64,2]{5,4,3,2,1,0:T(8,128)} %reshape.341, f32[]{:T(128)} %constant.162.clone.1), dimensions={1,3,5}, to_apply=%region_1.2 | reduce | flops 28672 | bytes 147460 | tf_op jit(solution)/shard_map/reduce_sum | solution.py:172
  126.9 9.7 %add.348 = f32[8,2,8,2,64,2]{5,4,3,2,1,0:T(8,128)} reshape(f32[16,16,128]{2,1,0:T(8,128)S(1)} %get-tuple-element.5) | data formatting | bytes 262144 | tf_op jit(solution)/shard_map/add | solution.py:216
  136.6 4.0 %reduce_sum.58 = f32[8,8,64]{2,1,0:T(8,128)S(1)} reduce(f32[8,2,8,2,64,2]{5,4,3,2,1,0:T(8,128)} %add.348, f32[]{:T(128)} %constant.162.clone.1), dimensions={1,3,5}, to_apply=%region_4.5 | reduce | flops 28672 | bytes 147460 | tf_op jit(solution)/shard_map/reduce_sum | solution.py:172
  143.6 3.5 %all_to_all.33 = f32[2,1,12288]{2,1,0:T(1,128)S(1)} all-to-all(f32[2,1,12288]{2,1,0:T(1,128)S(1)} %reshape.389), channel_id=1, replica_groups=mesh['tm'=32,'space_0'=4,'space_1'=2,'space_2'=2] {'space_2'}, dimensions={0} | all-to-all | bytes 196608 | tf_op jit(solution)/shard_map/all_to_all | solution.py:51
  149.6 8.5 %all-to-all-start.1 = ((f32[8,1,3072]{2,1,0:T(1,128)}), f32[8,1,3072]{2,1,0:T(1,128)S(1)}, u32[]{:S(2)}, u32[]{:S(2)}) async-start(f32[8,1,3072]{2,1,0:T(1,128)} %reshape.391), calls=%async_computation.1 | async-start | bytes 196608 | tf_op jit(solution)/shard_map/all_to_all | solution.py:51
  158.4 13.8 %all-to-all-done.1 = f32[8,1,3072]{2,1,0:T(1,128)S(1)} async-done(((f32[8,1,3072]{2,1,0:T(1,128)}), f32[8,1,3072]{2,1,0:T(1,128)S(1)}, u32[]{:S(2)}, u32[]{:S(2)}) %all-to-all-start.1) | async-done | bytes 98336 | tf_op jit(solution)/shard_map/all_to_all | solution.py:51
  175.3 7.4 %all-to-all-start.2 = ((f32[32,256,32]{1,2,0:T(8,128)}), f32[32,256,32]{1,2,0:T(8,128)S(1)}, u32[]{:S(2)}, u32[]{:S(2)}) async-start(f32[32,256,32]{1,2,0:T(8,128)} %broadcast_in_dim.60), calls=%async_computation.2 | async-start | bytes 2097152 | tf_op jit(solution)/shard_map/all_to_all | solution.py:63
  184.7 48.1 %all-to-all-done.2 = f32[32,256,32]{1,2,0:T(8,128)S(1)} async-done(((f32[32,256,32]{1,2,0:T(8,128)}), f32[32,256,32]{1,2,0:T(8,128)S(1)}, u32[]{:S(2)}, u32[]{:S(2)}) %all-to-all-start.2) | async-done | bytes 1048608 | tf_op jit(solution)/shard_map/all_to_all | solution.py:63
  234.8 7.0 %all-to-all-start.3 = ((f32[16,1,768]{2,1,0:T(1,128)}), f32[16,1,768]{2,1,0:T(1,128)S(1)}, u32[]{:S(2)}, u32[]{:S(2)}) async-start(f32[16,1,768]{2,1,0:T(1,128)} %reshape.393), calls=%async_computation.3 | async-start | bytes 98304 | tf_op jit(solution)/shard_map/all_to_all | solution.py:253
  242.6 13.9 %all-to-all-done.3 = f32[16,1,768]{2,1,0:T(1,128)S(1)} async-done(((f32[16,1,768]{2,1,0:T(1,128)}), f32[16,1,768]{2,1,0:T(1,128)S(1)}, u32[]{:S(2)}, u32[]{:S(2)}) %all-to-all-start.3) | async-done | bytes 49184 | tf_op jit(solution)/shard_map/all_to_all | solution.py:253
  263.5 3.3 %copy.110 = f32[1,5,16,16,128]{4,3,2,1,0:T(8,128)S(1)} copy(f32[1,5,16,16,128]{3,2,4,1,0:T(8,128)} %bitcast.144) | data formatting | bytes 1310720 | tf_op jit(solution)/shard_map/reshape | solution.py:257
  (124 shorter events, 37.4 us)
Async XLA Ops:
  0.9 22.7 %collective-permute-start = (f32[16,16,128]{2,1,0:T(8,128)S(1)}, f32[16,16,128]{2,1,0:T(8,128)S(1)}, u32[]{:S(2)}, u32[]{:S(2)}) collective-permute-start(f32[16,16,128]{2,1,0:T(8,128)S(1)} %slice_bitcast_fusion.2), channel_id=1, source_target_pairs={{0,16},{16,32},{32,48},{48,64},{64,80},{80,96},{96,112},{112,128},... | collective-permute-start | bytes 393224 | tf_op jit(solution)/shard_map/ppermute | solution.py:20
  21.7 2.0 copy-start.2
  24.3 9.7 %copy-start = (f32[1,5,16,16,128]{4,3,2,1,0:T(8,128)S(1)}, f32[1,5,16,16,128]{4,3,2,1,0:T(8,128)}, u32[]{:S(2)}) copy-start(f32[1,5,16,16,128]{4,3,2,1,0:T(8,128)} %param.4) | copy-start | bytes 1966084
  34.1 35.1 %collective-permute-start.1 = (f32[6,5,16,128]{3,2,1,0:T(8,128)S(1)}, f32[6,5,16,128]{3,2,1,0:T(8,128)S(1)}, u32[]{:S(2)}, u32[]{:S(2)}) collective-permute-start(f32[6,5,16,128]{3,2,1,0:T(8,128)S(1)} %get-tuple-element.35), channel_id=1, source_target_pairs={{0,1},{1,2},{2,3},{3,4},{4,5},{5,6},{6,7},{7,8},{8,9},{9,10},{10,1... | collective-permute-start | bytes 737288 | tf_op jit(solution)/shard_map/ppermute | solution.py:30
  49.5 27.1 %collective-permute-start.2 = (f32[6,5,16,128]{3,2,1,0:T(8,128)S(1)}, f32[6,5,16,128]{3,2,1,0:T(8,128)S(1)}, u32[]{:S(2)}, u32[]{:S(2)}) collective-permute-start(f32[6,5,16,128]{3,2,1,0:T(8,128)S(1)} %get-tuple-element.36), channel_id=1, source_target_pairs={{1,0},{2,1},{3,2},{4,3},{5,4},{6,5},{7,6},{8,7},{9,8},{10,9},{11,1... | collective-permute-start | bytes 737288 | tf_op jit(solution)/shard_map/ppermute | solution.py:31
  77.8 0.9 copy-start.3
  149.6 22.6 %all-to-all-start.1 = ((f32[8,1,3072]{2,1,0:T(1,128)}), f32[8,1,3072]{2,1,0:T(1,128)S(1)}, u32[]{:S(2)}, u32[]{:S(2)}) async-start(f32[8,1,3072]{2,1,0:T(1,128)} %reshape.391), calls=%async_computation.1 | async-start | bytes 196608 | tf_op jit(solution)/shard_map/all_to_all | solution.py:51
  175.3 57.5 %all-to-all-start.2 = ((f32[32,256,32]{1,2,0:T(8,128)}), f32[32,256,32]{1,2,0:T(8,128)S(1)}, u32[]{:S(2)}, u32[]{:S(2)}) async-start(f32[32,256,32]{1,2,0:T(8,128)} %broadcast_in_dim.60), calls=%async_computation.2 | async-start | bytes 2097152 | tf_op jit(solution)/shard_map/all_to_all | solution.py:63
  234.8 21.6 %all-to-all-start.3 = ((f32[16,1,768]{2,1,0:T(1,128)}), f32[16,1,768]{2,1,0:T(1,128)S(1)}, u32[]{:S(2)}, u32[]{:S(2)}) async-start(f32[16,1,768]{2,1,0:T(1,128)} %reshape.393), calls=%async_computation.3 | async-start | bytes 98304 | tf_op jit(solution)/shard_map/all_to_all | solution.py:253
  257.2 1.8 copy-start.4
  263.5 3.3 %copy-start.1 = (f32[1,5,16,16,128]{4,3,2,1,0:T(8,128)S(1)}, f32[1,5,16,16,128]{4,3,2,1,0:T(8,128)}, u32[]{:S(2)}) copy-start(f32[1,5,16,16,128]{4,3,2,1,0:T(8,128)} %bitcast_dynamic-update-slice_fusion) | copy-start | bytes 1966084
where the time goes:
time: 269 us; the launch traced here: 268 us
  waiting for transfers between devices  96.6 us (36%)
  local copies, waits for them, and re-layouts  79.5 us (30%)
  starting transfers between devices  44.8 us (17%)
  other arithmetic  33.6 us (12%)
  matrix products  9.05 us (3%)
  blocking collectives  3.45 us (1%)
    all_to_all x1, waiting for transfers between devices, copy_for_each(): return lax.all_to_all(copies, axis, split_axis=0, concat_axis=0, tiled=True)  48.1 us
    reshape x4, local copies, waits for them, and re-layouts, restrict(): field.reshape(depth // 2, 2, rows // 2, 2, cols // 2, 2)  39.7 us
    reduce_sum x6, other arithmetic, restrict(): return field.reshape(depth // 2, 2, rows // 2, 2, cols // 2, 2).mean(axis...  24.1 us
    ppermute x1, starting transfers between devices, padded_2(): before = lax.ppermute(last, axis, up)  15.4 us
    all_to_all x1, waiting for transfers between devices, shards(): lax.all_to_all(planar, SPACE, split_axis=1, concat_axis=2, tiled=True)  13.9 us
    all_to_all x1, waiting for transfers between devices, turned_blocks(): lax.all_to_all(parts, axes[k], split_axis=k, concat_axis=k, tiled=True)  13.8 us
    ppermute x1, waiting for transfers between devices, padded_2(): before = lax.ppermute(last, axis, up)  13.5 us
    add x1, local copies, waits for them, and re-layouts, shards(): inew[0] + inew[1]  9.98 us
  transfers between devices with their start and end apart: 6, of which 5 were waited for; matrix products, arithmetic and copies ran while one was open for 9% of the time, Pallas kernels for 0%

commit v1 on v0

v1 whole, which is shorter than its diff:
```python
import math

import jax
import jax.numpy as jnp
import numpy as np
from jax import lax
from jax.experimental import pallas as pl
from jax.experimental.pallas import tpu as pltpu
from jax.sharding import Mesh
from jax.sharding import PartitionSpec as P

TM = ("x", "zl")
SPACE = ("y", "zh", "c")

step_length = 0.4
diffusion = 1.0
reaction = 1.0

G_AT = (0, 4, 7, 9)
U_AT = 10
PACK = 14
REACH = 5


def basis_coefficients(nodes, chosen):
    polynomial = [1.0]
    for other, point in enumerate(nodes):
        if other == chosen:
            continue
        divisor = nodes[chosen] - point
        widened = [0.0] * (len(polynomial) + 1)
        for power, value in enumerate(polynomial):
            widened[power + 1] += value / divisor
            widened[power] -= value * point / divisor
        polynomial = widened
    return polynomial


def basis_value(nodes, chosen, where):
    result = 1.0
    for other, point in enumerate(nodes):
        if other != chosen:
            result *= (where - point) / (nodes[chosen] - point)
    return result


def node_tables():
    root = math.sqrt(3.0 / 7.0)
    fine_tau = [0.0, (1.0 - root) / 2.0, 0.5, (1.0 + root) / 2.0, 1.0]
    coarse_tau = [0.0, 0.5, 1.0]
    integ = []
    for j in range(4):
        row_values = []
        for k in range(5):
            polynomial = basis_coefficients(fine_tau, k)
            total = 0.0
            for power, value in enumerate(polynomial):
                total += (
                    value
                    * (fine_tau[j + 1] ** (power + 1) - fine_tau[j] ** (power + 1))
                    / (power + 1)
                )
            row_values.append(total)
        integ.append(row_values)
    interp = [[basis_value(coarse_tau, c, fine_tau[m]) for c in range(3)] for m in range(5)]
    spacing = [float(fine_tau[j + 1] - fine_tau[j]) for j in range(4)]
    return integ, spacing, interp


INTEG, SPACING, INTERP = node_tables()
MIX = [
    [step_length * (INTEG[j][k] - (SPACING[j] if j == k else 0.0)) for k in range(5)]
    for j in range(4)
]
QUAD = [[step_length * (INTEG[2 * c][k] + INTEG[2 * c + 1][k]) for k in range(5)] for c in range(2)]


def hartley(length):
    counter = np.arange(length)
    phase = 2.0 * np.pi * (counter[:, None] * counter[None, :] % length) / length
    return (np.cos(phase) + np.sin(phase)) / math.sqrt(length)


def block_pair(table):
    rows, cols = table.shape
    both = np.zeros((2 * rows, 2 * cols))
    both[:rows, :cols] = table
    both[rows:, cols:] = table
    return both


def tables(planes, rows, cols, depth):
    rows_c, cols_c = rows // 2, cols // 2
    hx, hy, hz = hartley(rows_c), hartley(cols_c), hartley(depth)
    down_y = 0.5 * np.repeat(hy, 2, 0)
    up_y = np.repeat(hy, 2, 0).T
    wide_x = np.repeat(hx, 2, 0)
    down_x = np.zeros((rows_c, planes, planes, rows))
    up_x = np.zeros((planes, rows, rows_c, planes))
    for p in range(planes):
        down_x[:, p, p, :] = 0.25 * wide_x.T
        up_x[p, :, :, p] = wide_x
    down_x = down_x.reshape(rows_c * planes, planes * rows)
    up_x = up_x.reshape(planes * rows, rows_c * planes)
    cos_z = np.cos(2.0 * np.pi * np.arange(depth) / depth)
    cos_y = np.cos(2.0 * np.pi * np.arange(cols_c) / cols_c)
    half = 0.5 * step_length * diffusion * 0.25
    denom = 1.0 - half * (2.0 * cos_z[:, None] + 2.0 * cos_y[None, :] - 6.0)
    denom = np.concatenate([denom, denom], 1)
    shift_x = half * 2.0 * np.cos(2.0 * np.pi * np.arange(rows_c) / rows_c)
    inverse_z = hz.reshape(4, 2, 2, planes, depth).transpose(1, 0, 2, 3, 4)
    inverse_z = inverse_z.reshape(2, 8 * planes, depth)
    f32 = lambda a: jnp.asarray(a, jnp.float32)
    return (
        f32(block_pair(down_y)), f32(down_x), f32(hz), f32(inverse_z), f32(denom), f32(shift_x),
        f32(up_x), f32(block_pair(up_y)),
    )


def dot(a, b):
    return jnp.dot(a, b, precision=lax.Precision.HIGHEST, preferred_element_type=jnp.float32)


def plane_part(f):
    near = pltpu.roll(f, 1, 0) + pltpu.roll(f, f.shape[0] - 1, 0)
    near = near + pltpu.roll(f, 1, 1) + pltpu.roll(f, f.shape[1] - 1, 1)
    return diffusion * near - f * ((6.0 * diffusion - reaction) + reaction * (f * f))


def old_kernel(place, u, g, near, far):
    planes = u.shape[1]
    core = place[1]

    for p in range(planes):
        total = [None] * 4
        for k in range(5):
            field = u[k, p]
            force = plane_part(field)
            if p > 0:
                force = force + diffusion * u[k, p - 1]
            if p < planes - 1:
                force = force + diffusion * u[k, p + 1]
            for j in range(4):
                term = MIX[j][k] * force
                total[j] = term if total[j] is None else total[j] + term
        for j in range(4):
            g[j, p] = total[j]

    def packed(out, plane_of):
        for j in range(4):
            for i in range(4 - j):
                out[G_AT[j] + i] = g[j, plane_of(i)]
            edge = plane_of(0)
            out[U_AT + j] = diffusion * sum(MIX[j][k] * u[k, edge] for k in range(5))

    top = lambda i: planes - 1 - i
    bottom = lambda i: i

    @pl.when(core == 0)
    def _():
        packed(near, top)
        packed(far, bottom)

    @pl.when(core != 0)
    def _():
        packed(near, bottom)
        packed(far, top)


def sweep_kernel(
    place, first, previous, start_near, start_far, g, own_near, own_far, got_near, got_far,
    down_y, down_x, w, send, hats, quad,
):
    planes = first.shape[0]
    coarse = planes // 2
    position, core = place[0], place[1]

    def with_sides(body):
        @pl.when(core == 0)
        def _():
            body(start_far, own_far, got_far, start_near, own_near, got_near)

        @pl.when(core != 0)
        def _():
            body(start_near, own_near, got_near, start_far, own_far, got_far)

    @pl.when(position == 0)
    def _():
        w[0, REACH : REACH + planes] = first[...]

    @pl.when(position != 0)
    def _():
        w[0, REACH : REACH + planes] = previous[...]

    def run(start_lo, own_lo, got_lo, start_hi, own_hi, got_hi):
        for i in range(REACH):
            w[0, REACH - 1 - i] = start_lo[i]
            w[0, REACH + planes + i] = start_hi[i]
        for m in range(5):
            margin = 4 - m
            held = [None, None]
            for p in range(-margin, planes + margin):
                at = p + REACH
                field = w[m, at]
                force = plane_part(field) + diffusion * (w[m, at - 1] + w[m, at + 1])
                if m < 4:
                    if p < 0:
                        source = got_lo[G_AT[m] - p - 1]
                        if p == -1:
                            source = source + own_lo[U_AT + m]
                    elif p >= planes:
                        source = got_hi[G_AT[m] + p - planes]
                        if p == planes:
                            source = source + own_hi[U_AT + m]
                    else:
                        source = g[m, p]
                        if p == 0:
                            source = source + got_lo[U_AT + m]
                        if p == planes - 1:
                            source = source + got_hi[U_AT + m]
                    w[m + 1, at] = field + step_length * SPACING[m] * force + source
                if 0 <= p < planes:
                    if p % 2 == 0:
                        held = force
                    else:
                        both = held + force
                        for c in range(2):
                            term = QUAD[c][m] * both
                            quad[c, p // 2] = term if m == 0 else quad[c, p // 2] + term

    with_sides(run)

    def paired(m):
        return jnp.concatenate(
            [w[m, REACH + 2 * i] + w[m, REACH + 2 * i + 1] for i in range(coarse)], 0
        )

    rows = coarse * first.shape[1]
    restart = paired(0)
    mask = jnp.where(position == 0, 1.0, 0.0)
    q0 = quad[0].reshape(rows, -1) + mask * restart
    q1 = quad[1].reshape(rows, -1)
    table = down_y[...]
    left = [
        dot(jnp.concatenate(pair, 1), table)
        for pair in ((q0, q1), (paired(2), paired(4)), (restart, restart))
    ]
    spectral = dot(down_x[...], jnp.concatenate(left, 1))
    width = left[0].shape[1]
    for y in range(4):
        for c in range(2):
            kx = 2 * y + c
            block = spectral[kx * coarse : (kx + 1) * coarse, : 2 * width]
            send[4 * y + c] = block
            send[4 * y + 2 + c] = block
    hats[...] = spectral[:, width:]


def lanes_swapped(a):
    return pltpu.roll(a, a.shape[1] // 2, 1)


def left_half(a):
    return lax.broadcasted_iota(jnp.int32, a.shape, 1) < a.shape[1] // 2


def spectrum_kernel(place, shift_x, got, table, denom, lifted, offset, copies):
    depth = table.shape[0]
    half = depth // 2
    d = denom[...] - shift_x[place[4]]
    inv = 1.0 / d
    spectra = dot(table[...], got[...].reshape(depth, -1))
    width = d.shape[1]
    lift = spectra[:, :width] - (1.0 - d) * spectra[:, width:]
    weighted = lift * inv
    weighted = jnp.where(left_half(d), weighted * inv, weighted)
    total = weighted + lanes_swapped(weighted)
    lifted[...] = lift
    offset[...] = total
    packed = jnp.where(left_half(total[:half]), total[:half], total[half:])
    for i in range(copies.shape[0]):
        copies[i] = packed


def scan_kernel(place, shift_x, all_offsets, lifted, offset, denom, inverse_z, out):
    zl, block, zh = place[2], place[3], place[5]
    slices = all_offsets.shape[0]
    half = all_offsets.shape[1]
    d = denom[...] - shift_x[place[4]]
    inv = 1.0 / d
    left = left_half(inv[:half])
    inv_packed = jnp.where(left, inv[:half], inv[half:])
    inv2 = inv_packed * inv_packed
    prefix = jnp.zeros_like(inv2)
    total = jnp.zeros_like(inv2)
    power = jnp.ones_like(inv2)
    whole = jnp.ones_like(inv2)
    for m in range(slices):
        piece = all_offsets[m]
        total = total * inv2 + piece
        prefix = jnp.where(m < zl, prefix * inv2 + piece, prefix)
        power = jnp.where(m < zl, power * inv2, power)
        whole = whole * inv2
    inverse = inverse_z[zh]
    weights = jnp.where(left_half(inv), inv, inv * inv)
    own = jnp.where(left_half(inv), lifted[...] * inv, offset[...])
    carried = total * power
    targets = out.shape[0] // 8
    for xp in range(targets):
        packed = jnp.where(xp == block, prefix, jnp.where(xp > block, carried, 0.0))
        carried = jnp.where(xp > block, carried * whole, carried)
        turned = lanes_swapped(packed)
        begin = jnp.concatenate(
            [jnp.where(left, packed, turned), jnp.where(left, turned, packed)], 0
        )
        later = begin * weights + jnp.where(xp == block, own, 0.0)
        planar = dot(inverse, jnp.concatenate([later, begin], 1))
        out[8 * xp : 8 * xp + 8] = planar.reshape(8, -1, planar.shape[1])


def finish_kernel(place, w, got, hats, up_x, up_y, out):
    planes = out.shape[1]
    coarse = planes // 2
    rows = out.shape[2]
    cols = out.shape[3]
    total = got[0:8] + got[8:16] + (got[16:24] + got[24:32])
    delta = total.reshape(-1, total.shape[2]) - hats[...]
    half = delta.shape[1] // 2
    later = delta[:, :half]
    begin = jnp.where(place[0] == 0, 0.0, delta[:, half:])
    spread = dot(up_x[...], jnp.concatenate([later, begin], 1))
    table = up_y[...]
    after = dot(spread[:, :half], table)
    before = dot(spread[:, half:], table[:, :cols])
    parts = [before, after[:, :cols], after[:, cols:]]
    for m in range(5):
        mixed = None
        for c in range(3):
            weight = INTERP[m][c]
            if abs(weight) < 1e-14:
                continue
            term = parts[c] if weight == 1.0 else weight * parts[c]
            mixed = term if mixed is None else mixed + term
        for i in range(coarse):
            piece = mixed[i * rows : (i + 1) * rows]
            out[m, 2 * i] = w[m, REACH + 2 * i] + piece
            out[m, 2 * i + 1] = w[m, REACH + 2 * i + 1] + piece


def call(kernel, outs, scalars, *args, scratch=()):
    smem = pl.BlockSpec(memory_space=pltpu.SMEM)
    vmem = pl.BlockSpec(memory_space=pltpu.VMEM)
    single = not isinstance(outs, list)
    shapes = [jax.ShapeDtypeStruct(s, jnp.float32) for s in ([outs] if single else outs)]
    result = pl.pallas_call(
        kernel,
        out_shape=shapes[0] if single else shapes,
        in_specs=[smem] * len(scalars) + [vmem] * len(args),
        out_specs=vmem if single else [vmem] * len(shapes),
        scratch_shapes=[pltpu.VMEM(s, jnp.float32) for s in scratch],
        compiler_params=pltpu.CompilerParams(vmem_limit_bytes=32 * 1024 * 1024),
    )(*scalars, *args)
    return result


def shards(u_old, u_init):
    planes, rows, cols = u_init.shape
    coarse, rows_c, cols_c = planes // 2, rows // 2, cols // 2
    slices = lax.axis_size(TM)
    blocks = lax.axis_size(SPACE)
    depth_c = coarse * blocks
    down_y, down_x, table_z, inverse_z, denom, shift_x, up_x, up_y = tables(
        coarse, rows, cols, depth_c
    )
    fine_old = u_old[0]
    position = lax.axis_index(TM)
    core = lax.axis_index("c")
    kx = 2 * lax.axis_index("y") + core
    place = jnp.stack(
        [position, core, lax.axis_index("zl"), lax.axis_index("x"), kx, lax.axis_index("zh")]
    ).astype(jnp.int32)

    last = fine_old[4]
    previous = lax.ppermute(last, TM, [(i, i + 1) for i in range(slices - 1)])

    def far_block(s):
        return (s + 1) % blocks if s % 2 else (s - 1) % blocks

    bottom = lambda a: a[:REACH]
    top = lambda a: a[::-1][:REACH]
    source = jnp.where(position == slices - 1, u_init, last)
    start_out = jnp.where(core == 0, bottom(source), top(source))
    across = [
        (n * blocks + s, (n + 1) % slices * blocks + far_block(s))
        for n in range(slices)
        for s in range(blocks)
    ]
    start_far = lax.ppermute(start_out, TM + SPACE, across)

    g, own_near, own_far = call(
        old_kernel,
        [(4, planes, rows, cols), (PACK, rows, cols), (PACK, rows, cols)],
        [place],
        fine_old,
    )
    got_far = lax.ppermute(own_far, SPACE, [(s, far_block(s)) for s in range(blocks)])
    start = jnp.where(position == 0, u_init, previous)
    start_edge = jnp.where(core == 0, top(start), bottom(start))
    near = lax.ppermute(jnp.concatenate([own_near, start_edge], 0), "c", [(0, 1), (1, 0)])
    got_near, start_near = near[:PACK], near[PACK:]

    w, send, hats = call(
        sweep_kernel,
        [
            (5, planes + 2 * REACH, rows, cols),
            (blocks, coarse, 4 * cols_c),
            (rows_c * coarse, 4 * cols_c),
        ],
        [place],
        u_init, previous, start_near, start_far, g, own_near, own_far, got_near, got_far,
        down_y, down_x,
        scratch=[(2, coarse, rows, cols)],
    )
    columns = lax.all_to_all(send, SPACE, 0, 0, tiled=True)
    packed = (lax.axis_size("zl"), depth_c // 2, 2 * cols_c)
    lifted, offset, copies = call(
        spectrum_kernel,
        [(depth_c, 2 * cols_c), (depth_c, 2 * cols_c), packed],
        [place, shift_x],
        columns, table_z, denom,
    )
    gathered = lax.all_to_all(copies, "zl", 0, 0, tiled=True)
    back = call(
        scan_kernel,
        (4 * rows_c, coarse, 4 * cols_c),
        [place, shift_x],
        gathered, lifted, offset, denom, inverse_z,
    )
    returned = lax.all_to_all(back, ("x", "y", "c"), 0, 0, tiled=True)
    out = call(
        finish_kernel, (5, planes, rows, cols), [place], w, returned, hats, up_x, up_y
    )
    return out[None]


def solution(mesh):
    finer = Mesh(mesh.devices.reshape(4, 8, 4, 2, 2), TM + SPACE)
    in_specs = (P(TM, None, SPACE, None, None), P(SPACE, None, None))
    out_specs = P(TM, None, SPACE, None, None)
    return jax.shard_map(
        shards, mesh=finer, in_specs=in_specs, out_specs=out_specs, check_vma=False
    )
```

time: 269 us -> 112 us (0.42)
  waiting for transfers between devices: 96.6 us -> 10 us
  local copies, waits for them, and re-layouts: 79.5 us -> 2.2 us
  blocking collectives: 3.45 us -> 65.5 us
  other arithmetic: 33.6 us -> 0.96 us
  starting transfers between devices: 44.8 us -> 25.7 us
  matrix products: 9.05 us -> 0 us
  Pallas kernels: 0 us -> 6.83 us
    all_to_all x3 -> x0, waiting for transfers between devices: 75.8 us -> none  [the longest x1 48.1 us: copy_for_each(): return lax.all_to_all(copies, axis, split_axis=0, concat_axis=0, tiled=True)]
    all_to_all x1 -> x3, blocking collectives: 3.45 us -> 65.5 us  [the longest x1 24.6 us: shards(): gathered = lax.all_to_all(copies, 'zl', 0, 0, tiled=True)]
    reshape x7 -> x0, local copies, waits for them, and re-layouts: 44.1 us -> none  [the longest x4 39.7 us: restrict(): field.reshape(depth // 2, 2, rows // 2, 2, cols // 2, 2)]
    reduce_sum x6 -> x0, other arithmetic: 24.1 us -> none  [restrict(): return field.reshape(depth // 2, 2, rows // 2, 2, cols // 2, 2).mean(axis...]
    all_to_all x3 -> x0, starting transfers between devices: 22.9 us -> none  [the longest x1 8.47 us: turned_blocks(): lax.all_to_all(parts, axes[k], split_axis=k, concat_axis=k, tiled=True)]
    add x2 -> x0, local copies, waits for them, and re-layouts: 19.7 us -> none  [the longest x1 9.98 us: shards(): inew[0] + inew[1]]
    ppermute x3 -> x4, waiting for transfers between devices: 20.9 us -> 10 us  [the longest x1 9.99 us: shards(): start_far = lax.ppermute(start_out, TM + SPACE, across)]
    dot_general x7 -> x0, matrix products: 9.05 us -> none  [the longest x1 2.59 us: shards(): jnp.einsum('fzc,cd->fzd', stacked, table_xy, precision=highest)]
  transfers between devices with their start and end apart: 6 -> 4, of which waited for: 5 -> 1; matrix products, arithmetic and copies ran while one was open for 9% -> 1% of each run, Pallas kernels for 0% -> 1%
where the time goes in v1:
time: 112 us; the launch traced here: 111 us
  blocking collectives  65.5 us (58%)
  starting transfers between devices  25.7 us (23%)
  waiting for transfers between devices  10 us (9%)
  Pallas kernels  6.83 us (6%)
  local copies, waits for them, and re-layouts  2.2 us (2%)
    all_to_all x1, blocking collectives, shards(): gathered = lax.all_to_all(copies, 'zl', 0, 0, tiled=True)  24.6 us
    all_to_all x1, blocking collectives, shards(): columns = lax.all_to_all(send, SPACE, 0, 0, tiled=True)  23 us
    all_to_all x1, blocking collectives, shards(): returned = lax.all_to_all(back, ('x', 'y', 'c'), 0, 0, tiled=True)  17.9 us
    ppermute x1, starting transfers between devices, shards(): lax.ppermute(own_far, SPACE, [(s, far_block(s)) for s in range(blocks)])  15.4 us
    ppermute x1, waiting for transfers between devices, shards(): start_far = lax.ppermute(start_out, TM + SPACE, across)  9.99 us
    pallas_call x5, Pallas kernels, call(): pl.pallas_call(kernel, out_shape=shapes[0] if single else shapes, in_spec...  6.83 us
    ppermute x1, starting transfers between devices, shards(): previous = lax.ppermute(last, TM, [(i, i + 1) for i in range(slices - 1)])  4.38 us
    ppermute x1, starting transfers between devices, shards(): lax.ppermute(jnp.concatenate([own_near, start_edge], 0), 'c', [(0, 1), (1...  3.91 us
  transfers between devices with their start and end apart: 4, of which 1 were waited for; matrix products, arithmetic and copies ran while one was open for 1% of the time, Pallas kernels for 1%

profile of v1, /device:TPU:1, one launch (start us, length us, event | category | flops | bytes accessed | tf_op | source)
XLA Modules:
  0.0 111.4 jit_solution(7514416946078345401)
XLA Ops:
  0.0 0.9 slice_bitcast_fusion
  1.0 4.4 %collective-permute-start = (f32[16,16,128]{2,1,0:T(8,128)S(1)}, f32[16,16,128]{2,1,0:T(8,128)S(1)}, u32[]{:S(2)}, u32[]{:S(2)}) collective-permute-start(f32[16,16,128]{2,1,0:T(8,128)S(1)} %slice_bitcast_fusion), channel_id=1, source_target_pairs={{0,16},{16,32},{32,48},{48,64},{64,80},{80,96},{96,112},{112,128},... | collective-permute-start | bytes 393224 | tf_op jit(solution)/shard_map/ppermute | solution.py:384
  5.4 0.1 stack.27.place
  5.4 1.1 copy-done
  6.5 1.0 shard_map.100
  7.6 15.4 %collective-permute-start.3 = (f32[14,16,128]{2,1,0:T(8,128)S(1)}, f32[14,16,128]{2,1,0:T(8,128)S(1)}, u32[]{:S(2)}, u32[]{:S(2)}) collective-permute-start(f32[14,16,128]{2,1,0:T(8,128)S(1)} %get-tuple-element.16.own_far), channel_id=1, source_target_pairs={{0,15},{1,2},{2,1},{3,4},{4,3},{5,6},{6,5},{7,8},{8,7},{9,10},{10,... | collective-permute-start | bytes 344072 | tf_op jit(solution)/shard_map/ppermute | solution.py:406
  23.0 0.0 collective-permute-done.previous
  23.0 0.9 broadcast_select_fusion
  24.0 3.9 %collective-permute-start.1 = (f32[19,16,128]{2,1,0:T(8,128)S(1)}, f32[19,16,128]{2,1,0:T(8,128)S(1)}, u32[]{:S(2)}, u32[]{:S(2)}) collective-permute-start(f32[19,16,128]{2,1,0:T(8,128)S(1)} %pad_maximum_fusion), channel_id=1, source_target_pairs={{0,1},{1,0},{2,3},{3,2},{4,5},{5,4},{6,7},{7,6},{8,9},{9,8},{10,11... | collective-permute-start | bytes 466952 | tf_op jit(solution)/shard_map/ppermute | solution.py:409
  27.9 0.0 copy-start.2
  27.9 0.0 copy-start.7
  28.0 0.0 copy-start.9
  28.0 2.1 %collective-permute-start.2 = (f32[5,16,128]{2,1,0:T(8,128)S(1)}, f32[5,16,128]{2,1,0:T(8,128)S(1)}, u32[]{:S(2)}, u32[]{:S(2)}) collective-permute-start(f32[5,16,128]{2,1,0:T(8,128)S(1)} %slice_select_fusion), channel_id=1, source_target_pairs={{0,31},{1,18},{2,17},{3,20},{4,19},{5,22},{6,21},{7,24},{8,23},{9,... | collective-permute-start | bytes 122888 | tf_op jit(solution)/shard_map/ppermute | solution.py:398
  30.0 0.0 collective-permute-done.1
  30.1 10.0 %collective-permute-done.2.start_far = f32[5,16,128]{2,1,0:T(8,128)S(1)} collective-permute-done((f32[5,16,128]{2,1,0:T(8,128)S(1)}, f32[5,16,128]{2,1,0:T(8,128)S(1)}, u32[]{:S(2)}, u32[]{:S(2)}) %collective-permute-start.2) | collective-permute-done | bytes 40992 | tf_op jit(solution)/shard_map/ppermute | solution.py:398
  40.1 1.8 %shard_map.101 = (f32[5,26,16,128]{3,2,1,0:T(8,128)S(1)}, f32[16,8,256]{2,1,0:T(8,128)S(1)}, f32[64,256]{1,0:T(8,128)S(1)}) custom-call(s32[6]{0:T(128)S(1)} %stack.27.place, f32[16,16,128]{2,1,0:T(8,128)S(1)} %copy-done.1, f32[16,16,128]{2,1,0:T(8,128)S(1)} %collective-permute-done.previous, f32[5,16,128]{2,1,0:T(8,128)S(1)} %slice.39.start_near, ...), custom_call_target="tpu_custom_call" | custom-call | tf_op jit(solution)/shard_map/pallas_call | solution.py:355
  41.9 23.0 %all_to_all.15.got = f32[16,8,256]{2,1,0:T(8,128)S(1)} all-to-all(f32[16,8,256]{2,1,0:T(8,128)S(1)} %get-tuple-element.18), channel_id=1, replica_groups=mesh['x'=4,'zl'=8,'y'=4,'zh'=2,'c'=2] {'y','zh','c'}, dimensions={0} | all-to-all | bytes 262144 | tf_op jit(solution)/shard_map/all_to_all | solution.py:424
  64.9 0.0 copy-start.3
  64.9 0.0 copy-start.5
  64.9 0.9 shard_map.102
  65.8 24.6 %all_to_all.16.all_offsets = f32[8,64,128]{2,1,0:T(8,128)S(1)} all-to-all(f32[8,64,128]{2,1,0:T(8,128)S(1)} %get-tuple-element.19), channel_id=1, replica_groups=mesh['x'=4,'zl'=8,'y'=4,'zh'=2,'c'=2] {'zl'}, dimensions={0} | all-to-all | bytes 524288 | tf_op jit(solution)/shard_map/all_to_all | solution.py:432
  90.4 1.1 shard_map.103
  91.5 17.9 %all_to_all.17.got = f32[32,8,256]{2,1,0:T(8,128)S(1)} all-to-all(f32[32,8,256]{2,1,0:T(8,128)S(1)} %shard_map.103), channel_id=1, replica_groups=mesh['x'=4,'zl'=8,'y'=4,'zh'=2,'c'=2] {'x','y','c'}, dimensions={0} | all-to-all | bytes 524288 | tf_op jit(solution)/shard_map/all_to_all | solution.py:439
  109.4 2.0 %shard_map.104 = f32[5,16,16,128]{3,2,1,0:T(8,128)} custom-call(s32[6]{0:T(128)S(1)} %stack.27.place, f32[5,26,16,128]{3,2,1,0:T(8,128)S(1)} %get-tuple-element.17.w, f32[32,8,256]{2,1,0:T(8,128)S(1)} %all_to_all.17.got, f32[64,256]{1,0:T(8,128)S(1)} %get-tuple-element.22.hats, f32[128,64]{1,0:T(8,128)S(1)} %copy-done.5, f32[128,256]{1,0:T(8,128)S(1)} %copy-done.3), custom_call_target="tpu_custom_call" | custom-call | tf_op jit(solution)/shard_map/pallas_call | solution.py:355
  (22 shorter events, 0.1 us)
Async XLA Ops:
  0.0 23.0 %copy-start.1 = (f32[16,16,128]{2,1,0:T(8,128)S(1)}, f32[16,16,128]{2,1,0:T(8,128)}, u32[]{:S(2)}) copy-start(f32[16,16,128]{2,1,0:T(8,128)} %first.1) | copy-start | bytes 393220
  1.0 22.0 %collective-permute-start = (f32[16,16,128]{2,1,0:T(8,128)S(1)}, f32[16,16,128]{2,1,0:T(8,128)S(1)}, u32[]{:S(2)}, u32[]{:S(2)}) collective-permute-start(f32[16,16,128]{2,1,0:T(8,128)S(1)} %slice_bitcast_fusion), channel_id=1, source_target_pairs={{0,16},{16,32},{32,48},{48,64},{64,80},{80,96},{96,112},{112,128},... | collective-permute-start | bytes 393224 | tf_op jit(solution)/shard_map/ppermute | solution.py:384
  5.4 1.1 copy-start
  6.5 33.5 %copy-start.4 = (f32[256,128]{1,0:T(8,128)S(1)}, f32[256,128]{1,0:T(8,128)}, u32[]{:S(2)}) copy-start(f32[256,128]{1,0:T(8,128)} %constant.44.clone.down_y) | copy-start | bytes 393220
  6.5 33.5 %copy-start.8 = (f32[64,128]{1,0:T(8,128)S(1)}, f32[64,128]{1,0:T(8,128)}, u32[]{:S(2)}) copy-start(f32[64,128]{1,0:T(8,128)} %constant.45.clone.down_x) | copy-start | bytes 98308
  7.6 22.5 %collective-permute-start.3 = (f32[14,16,128]{2,1,0:T(8,128)S(1)}, f32[14,16,128]{2,1,0:T(8,128)S(1)}, u32[]{:S(2)}, u32[]{:S(2)}) collective-permute-start(f32[14,16,128]{2,1,0:T(8,128)S(1)} %get-tuple-element.16.own_far), channel_id=1, source_target_pairs={{0,15},{1,2},{2,1},{3,4},{4,3},{5,6},{6,5},{7,8},{8,7},{9,10},{10,... | collective-permute-start | bytes 344072 | tf_op jit(solution)/shard_map/ppermute | solution.py:406
  24.0 6.0 %collective-permute-start.1 = (f32[19,16,128]{2,1,0:T(8,128)S(1)}, f32[19,16,128]{2,1,0:T(8,128)S(1)}, u32[]{:S(2)}, u32[]{:S(2)}) collective-permute-start(f32[19,16,128]{2,1,0:T(8,128)S(1)} %pad_maximum_fusion), channel_id=1, source_target_pairs={{0,1},{1,0},{2,3},{3,2},{4,5},{5,4},{6,7},{7,6},{8,9},{9,8},{10,11... | collective-permute-start | bytes 466952 | tf_op jit(solution)/shard_map/ppermute | solution.py:409
  27.9 36.9 %copy-start.2 = (f32[128,128]{1,0:T(8,128)S(1)}, f32[128,128]{1,0:T(8,128)}, u32[]{:S(2)}) copy-start(f32[128,128]{1,0:T(8,128)} %constant.48.clone.denom) | copy-start | bytes 196612
  27.9 36.9 %copy-start.7 = (f32[128,128]{1,0:T(8,128)S(1)}, f32[128,128]{1,0:T(8,128)}, u32[]{:S(2)}) copy-start(f32[128,128]{1,0:T(8,128)} %constant.46.clone.table) | copy-start | bytes 196612
  28.0 36.9 %copy-start.9 = (f32[8]{0:T(128)S(1)}, f32[8]{0:T(128)}, u32[]{:S(2)}) copy-start(f32[8]{0:T(128)} %constant.49.clone.shift_x) | copy-start | bytes 100
  28.0 12.1 %collective-permute-start.2 = (f32[5,16,128]{2,1,0:T(8,128)S(1)}, f32[5,16,128]{2,1,0:T(8,128)S(1)}, u32[]{:S(2)}, u32[]{:S(2)}) collective-permute-start(f32[5,16,128]{2,1,0:T(8,128)S(1)} %slice_select_fusion), channel_id=1, source_target_pairs={{0,31},{1,18},{2,17},{3,20},{4,19},{5,22},{6,21},{7,24},{8,23},{9,... | collective-permute-start | bytes 122888 | tf_op jit(solution)/shard_map/ppermute | solution.py:398
  40.1 50.4 %copy-start.6 = (f32[2,64,128]{2,1,0:T(8,128)S(1)}, f32[2,64,128]{2,1,0:T(8,128)}, u32[]{:S(2)}) copy-start(f32[2,64,128]{2,1,0:T(8,128)} %constant.47.clone.inverse_z) | copy-start | bytes 196612
  64.9 44.5 %copy-start.3 = (f32[128,256]{1,0:T(8,128)S(1)}, f32[128,256]{1,0:T(8,128)}, u32[]{:S(2)}) copy-start(f32[128,256]{1,0:T(8,128)} %constant.51.clone.up_y) | copy-start | bytes 393220
  64.9 44.5 %copy-start.5 = (f32[128,64]{1,0:T(8,128)S(1)}, f32[128,64]{1,0:T(8,128)}, u32[]{:S(2)}) copy-start(f32[128,64]{1,0:T(8,128)} %constant.50.clone.up_x) | copy-start | bytes 98308

commit v2 on v1

--- a/solution.py
+++ b/solution.py
@@ -167,10 +167,55 @@
         packed(far, top)
 
 
+def edge_planes(out, at, field, core, low):
+    planes = field.shape[0]
+
+    @pl.when((core == 0) == low)
+    def _():
+        for i in range(REACH):
+            out[at + i] = field[i]
+
+    @pl.when((core == 0) != low)
+    def _():
+        for i in range(REACH):
+            out[at + i] = field[planes - 1 - i]
+
+
+def last_kernel(place, u, first, last, start_out):
+    position, core, slices = place[0], place[1], place[6]
+    last[...] = u[0, 0]
+
+    @pl.when(position == slices - 1)
+    def _():
+        edge_planes(start_out, 0, first, core, True)
+
+    @pl.when(position != slices - 1)
+    def _():
+        edge_planes(start_out, 0, last, core, True)
+
+
+def relay_kernel(got, out):
+    out[...] = got[...]
+
+
+def near_kernel(place, first, previous, own_near, out):
+    position, core = place[0], place[1]
+    out[:PACK] = own_near[...]
+
+    @pl.when(position == 0)
+    def _():
+        edge_planes(out, PACK, first, core, False)
+
+    @pl.when(position != 0)
+    def _():
+        edge_planes(out, PACK, previous, core, False)
+
+
 def sweep_kernel(
-    place, first, previous, start_near, start_far, g, own_near, own_far, got_near, got_far,
+    place, first, previous, near, start_far, g, own_near, own_far, got_far,
     down_y, down_x, w, send, hats, quad,
 ):
+    got_near, start_near = near.at[:PACK], near.at[PACK:]
     planes = first.shape[0]
     coarse = planes // 2
     position, core = place[0], place[1]
@@ -347,18 +392,23 @@
             out[m, 2 * i + 1] = w[m, REACH + 2 * i + 1] + piece
 
 
-def call(kernel, outs, scalars, *args, scratch=()):
+def call(kernel, outs, scalars, *args, scratch=(), flops=0, blocked={}):
     smem = pl.BlockSpec(memory_space=pltpu.SMEM)
     vmem = pl.BlockSpec(memory_space=pltpu.VMEM)
     single = not isinstance(outs, list)
     shapes = [jax.ShapeDtypeStruct(s, jnp.float32) for s in ([outs] if single else outs)]
     result = pl.pallas_call(
         kernel,
+        grid=(1,) if blocked else (),
         out_shape=shapes[0] if single else shapes,
-        in_specs=[smem] * len(scalars) + [vmem] * len(args),
+        in_specs=[
+            smem if i < len(scalars) else blocked.get(i, vmem)
+            for i in range(len(scalars) + len(args))
+        ],
         out_specs=vmem if single else [vmem] * len(shapes),
         scratch_shapes=[pltpu.VMEM(s, jnp.float32) for s in scratch],
         compiler_params=pltpu.CompilerParams(vmem_limit_bytes=32 * 1024 * 1024),
+        cost_estimate=pl.CostEstimate(flops=flops, bytes_accessed=1 << 20, transcendentals=0),
     )(*scalars, *args)
     return result
 
@@ -372,42 +422,43 @@
     down_y, down_x, table_z, inverse_z, denom, shift_x, up_x, up_y = tables(
         coarse, rows, cols, depth_c
     )
-    fine_old = u_old[0]
     position = lax.axis_index(TM)
     core = lax.axis_index("c")
     kx = 2 * lax.axis_index("y") + core
-    place = jnp.stack(
-        [position, core, lax.axis_index("zl"), lax.axis_index("x"), kx, lax.axis_index("zh")]
-    ).astype(jnp.int32)
-
-    last = fine_old[4]
-    previous = lax.ppermute(last, TM, [(i, i + 1) for i in range(slices - 1)])
+    place = [position, core, lax.axis_index("zl"), lax.axis_index("x"), kx]
+    place = jnp.stack(place + [lax.axis_index("zh"), slices]).astype(jnp.int32)
+
+    last, start_out = call(
+        last_kernel,
+        [(planes, rows, cols), (REACH, rows, cols)],
+        [place],
+        u_old, u_init,
+        blocked={1: pl.BlockSpec((1, 1, planes, rows, cols), lambda i: (0, 4, 0, 0, 0))},
+    )
 
     def far_block(s):
         return (s + 1) % blocks if s % 2 else (s - 1) % blocks
 
-    bottom = lambda a: a[:REACH]
-    top = lambda a: a[::-1][:REACH]
-    source = jnp.where(position == slices - 1, u_init, last)
-    start_out = jnp.where(core == 0, bottom(source), top(source))
     across = [
         (n * blocks + s, (n + 1) % slices * blocks + far_block(s))
         for n in range(slices)
         for s in range(blocks)
     ]
     start_far = lax.ppermute(start_out, TM + SPACE, across)
-
+    previous = lax.ppermute(last, TM, [(i, i + 1) for i in range(slices - 1)])
     g, own_near, own_far = call(
         old_kernel,
         [(4, planes, rows, cols), (PACK, rows, cols), (PACK, rows, cols)],
         [place],
-        fine_old,
-    )
+        u_old[0],
+        flops=10**11,
+    )
+    start_far = call(relay_kernel, start_far.shape, [], start_far, flops=10**11)
     got_far = lax.ppermute(own_far, SPACE, [(s, far_block(s)) for s in range(blocks)])
-    start = jnp.where(position == 0, u_init, previous)
-    start_edge = jnp.where(core == 0, top(start), bottom(start))
-    near = lax.ppermute(jnp.concatenate([own_near, start_edge], 0), "c", [(0, 1), (1, 0)])
-    got_near, start_near = near[:PACK], near[PACK:]
+    near_out = call(
+        near_kernel, (PACK + REACH, rows, cols), [place], u_init, previous, own_near
+    )
+    near = lax.ppermute(near_out, "c", [(0, 1), (1, 0)])
 
     w, send, hats = call(
         sweep_kernel,
@@ -417,7 +468,7 @@
             (rows_c * coarse, 4 * cols_c),
         ],
         [place],
-        u_init, previous, start_near, start_far, g, own_near, own_far, got_near, got_far,
+        u_init, previous, near, start_far, g, own_near, own_far, got_far,
         down_y, down_x,
         scratch=[(2, coarse, rows, cols)],
     )

time: 112 us -> 113 us (level)
  blocking collectives: 65.5 us -> 66.9 us
    ppermute x1, starting transfers between devices: 2.05 us -> 16.4 us  [shards(): start_far = lax.ppermute(start_out, TM + SPACE, across)]
    ppermute x1, starting transfers between devices: 15.4 us -> 2.65 us  [shards(): lax.ppermute(own_far, SPACE, [(s, far_block(s)) for s in range(blocks)])]
    ppermute x1, waiting for transfers between devices: 9.99 us -> 0.01 us  [shards(): start_far = lax.ppermute(start_out, TM + SPACE, across)]
    ppermute x1, waiting for transfers between devices: 0.01 us -> 9.84 us  [shards(): lax.ppermute(own_far, SPACE, [(s, far_block(s)) for s in range(blocks)])]
    all_to_all x1, blocking collectives: 23 us -> 25.5 us  [shards(): columns = lax.all_to_all(send, SPACE, 0, 0, tiled=True)]
    all_to_all x1, blocking collectives: 24.6 us -> 22.3 us  [shards(): gathered = lax.all_to_all(copies, 'zl', 0, 0, tiled=True)]
    ppermute x1, starting transfers between devices: 4.38 us -> 2.65 us  [shards(): previous = lax.ppermute(last, TM, [(i, i + 1) for i in range(slices - 1)])]
    all_to_all x1, blocking collectives: 17.9 us -> 19.2 us  [shards(): returned = lax.all_to_all(back, ('x', 'y', 'c'), 0, 0, tiled=True)]
  transfers between devices with their start and end apart: 4 -> 4, of which waited for: 1 -> 1; matrix products, arithmetic and copies ran while one was open for 1% -> 0% of each run, Pallas kernels for 1% -> 1%
where the time goes in v2:
time: 113 us
  blocking collectives  66.9 us (59%)
  starting transfers between devices  25.7 us (23%)
  waiting for transfers between devices  9.84 us (9%)
  Pallas kernels  7.96 us (7%)
  local copies, waits for them, and re-layouts  2.14 us (2%)
    all_to_all x1, blocking collectives, shards(): columns = lax.all_to_all(send, SPACE, 0, 0, tiled=True)  25.5 us
    all_to_all x1, blocking collectives, shards(): gathered = lax.all_to_all(copies, 'zl', 0, 0, tiled=True)  22.3 us
    all_to_all x1, blocking collectives, shards(): returned = lax.all_to_all(back, ('x', 'y', 'c'), 0, 0, tiled=True)  19.2 us
    ppermute x1, starting transfers between devices, shards(): start_far = lax.ppermute(start_out, TM + SPACE, across)  16.4 us
    ppermute x1, waiting for transfers between devices, shards(): lax.ppermute(own_far, SPACE, [(s, far_block(s)) for s in range(blocks)])  9.84 us
    pallas_call x8, Pallas kernels, call(): pl.pallas_call(kernel, grid=(1,) if blocked else (), out_shape=shapes[0]...  7.96 us
    ppermute x1, starting transfers between devices, shards(): near = lax.ppermute(near_out, 'c', [(0, 1), (1, 0)])  4.04 us
    ppermute x1, starting transfers between devices, shards(): previous = lax.ppermute(last, TM, [(i, i + 1) for i in range(slices - 1)])  2.65 us
  transfers between devices with their start and end apart: 4, of which 1 were waited for; matrix products, arithmetic and copies ran while one was open for 0% of the time, Pallas kernels for 1%

profile of v2, /device:TPU:1, one launch (start us, length us, event | category | flops | bytes accessed | tf_op | source)
XLA Modules:
  0.0 112.8 jit_solution(1021051032412259929)
XLA Ops:
  0.0 0.1 stack.27.place
  0.1 0.9 copy-done
  1.0 1.1 copy-done.2
  2.1 0.6 shard_map.100
  2.6 16.4 %collective-permute-start.2 = (f32[5,16,128]{2,1,0:T(8,128)S(1)}, f32[5,16,128]{2,1,0:T(8,128)S(1)}, u32[]{:S(2)}, u32[]{:S(2)}) collective-permute-start(f32[5,16,128]{2,1,0:T(8,128)S(1)} %get-tuple-element.18), channel_id=1, source_target_pairs={{0,31},{1,18},{2,17},{3,20},{4,19},{5,22},{6,21},{7,24},{8,23},{9,... | collective-permute-start | bytes 122888 | tf_op jit(solution)/shard_map/ppermute | solution.py:447
  19.0 2.6 %collective-permute-start = (f32[16,16,128]{2,1,0:T(8,128)S(1)}, f32[16,16,128]{2,1,0:T(8,128)S(1)}, u32[]{:S(2)}, u32[]{:S(2)}) collective-permute-start(f32[16,16,128]{2,1,0:T(8,128)S(1)} %get-tuple-element.16), channel_id=1, source_target_pairs={{0,16},{16,32},{32,48},{48,64},{64,80},{80,96},{96,112},{112,128},... | collective-permute-start | bytes 393224 | tf_op jit(solution)/shard_map/ppermute | solution.py:448
  21.7 1.0 shard_map.101
  22.8 2.6 %collective-permute-start.3 = (f32[14,16,128]{2,1,0:T(8,128)S(1)}, f32[14,16,128]{2,1,0:T(8,128)S(1)}, u32[]{:S(2)}, u32[]{:S(2)}) collective-permute-start(f32[14,16,128]{2,1,0:T(8,128)S(1)} %get-tuple-element.20.own_far), channel_id=1, source_target_pairs={{0,15},{1,2},{2,1},{3,4},{4,3},{5,6},{6,5},{7,8},{8,7},{9,10},{10,... | collective-permute-start | bytes 344072 | tf_op jit(solution)/shard_map/ppermute | solution.py:457
  25.4 0.6 shard_map.102
  26.0 0.0 copy-start.9
  26.0 4.0 %collective-permute-start.1 = (f32[19,16,128]{2,1,0:T(8,128)S(1)}, f32[19,16,128]{2,1,0:T(8,128)S(1)}, u32[]{:S(2)}, u32[]{:S(2)}) collective-permute-start(f32[19,16,128]{2,1,0:T(8,128)S(1)} %shard_map.102), channel_id=1, source_target_pairs={{0,1},{1,0},{2,3},{3,2},{4,5},{5,4},{6,7},{7,6},{8,9},{9,8},{10,11... | collective-permute-start | bytes 466952 | tf_op jit(solution)/shard_map/ppermute | solution.py:461
  30.1 0.0 copy-start.3
  30.1 0.0 copy-start.10
  30.1 9.8 %collective-permute-done.3.got_far = f32[14,16,128]{2,1,0:T(8,128)S(1)} collective-permute-done((f32[14,16,128]{2,1,0:T(8,128)S(1)}, f32[14,16,128]{2,1,0:T(8,128)S(1)}, u32[]{:S(2)}, u32[]{:S(2)}) %collective-permute-start.3) | collective-permute-done | bytes 114720 | tf_op jit(solution)/shard_map/ppermute | solution.py:457
  40.0 0.0 copy-start.7
  40.0 1.8 %shard_map.104 = (f32[5,26,16,128]{3,2,1,0:T(8,128)S(1)}, f32[16,8,256]{2,1,0:T(8,128)S(1)}, f32[64,256]{1,0:T(8,128)S(1)}) custom-call(s32[7]{0:T(128)S(1)} %stack.27.place, f32[16,16,128]{2,1,0:T(8,128)S(1)} %copy-done.1, f32[16,16,128]{2,1,0:T(8,128)S(1)} %collective-permute-done.previous, f32[19,16,128]{2,1,0:T(8,128)S(1)} %collective-permute-done.1.near, ...), custom_call_target="tpu_custom_call" | custom-call | bytes 1048576 | tf_op jit(solution)/shard_map/pallas_call | solution.py:400
  41.8 25.5 %all_to_all.15.got = f32[16,8,256]{2,1,0:T(8,128)S(1)} all-to-all(f32[16,8,256]{2,1,0:T(8,128)S(1)} %get-tuple-element.22), channel_id=1, replica_groups=mesh['x'=4,'zl'=8,'y'=4,'zh'=2,'c'=2] {'y','zh','c'}, dimensions={0} | all-to-all | bytes 262144 | tf_op jit(solution)/shard_map/all_to_all | solution.py:475
  67.3 0.0 copy-start.4
  67.3 0.0 copy-start.6
  67.3 0.9 shard_map.105
  68.2 22.3 %all_to_all.16.all_offsets = f32[8,64,128]{2,1,0:T(8,128)S(1)} all-to-all(f32[8,64,128]{2,1,0:T(8,128)S(1)} %get-tuple-element.23), channel_id=1, replica_groups=mesh['x'=4,'zl'=8,'y'=4,'zh'=2,'c'=2] {'zl'}, dimensions={0} | all-to-all | bytes 524288 | tf_op jit(solution)/shard_map/all_to_all | solution.py:483
  90.6 1.1 shard_map.106
  91.6 19.2 %all_to_all.17.got = f32[32,8,256]{2,1,0:T(8,128)S(1)} all-to-all(f32[32,8,256]{2,1,0:T(8,128)S(1)} %shard_map.106), channel_id=1, replica_groups=mesh['x'=4,'zl'=8,'y'=4,'zh'=2,'c'=2] {'x','y','c'}, dimensions={0} | all-to-all | bytes 524288 | tf_op jit(solution)/shard_map/all_to_all | solution.py:490
  110.8 2.0 %shard_map.107 = f32[5,16,16,128]{3,2,1,0:T(8,128)} custom-call(s32[7]{0:T(128)S(1)} %stack.27.place, f32[5,26,16,128]{3,2,1,0:T(8,128)S(1)} %get-tuple-element.21.w, f32[32,8,256]{2,1,0:T(8,128)S(1)} %all_to_all.17.got, f32[64,256]{1,0:T(8,128)S(1)} %get-tuple-element.26.hats, f32[128,64]{1,0:T(8,128)S(1)} %copy-done.6, f32[128,256]{1,0:T(8,128)S(1)} %copy-done.4), custom_call_target="tpu_custom_call" | custom-call | bytes 1048576 | tf_op jit(solution)/shard_map/pallas_call | solution.py:400
  (18 shorter events, 0.0 us)
Async XLA Ops:
  0.1 0.9 copy-start
  1.0 1.1 copy-start.2
  2.6 27.4 %collective-permute-start.2 = (f32[5,16,128]{2,1,0:T(8,128)S(1)}, f32[5,16,128]{2,1,0:T(8,128)S(1)}, u32[]{:S(2)}, u32[]{:S(2)}) collective-permute-start(f32[5,16,128]{2,1,0:T(8,128)S(1)} %get-tuple-element.18), channel_id=1, source_target_pairs={{0,31},{1,18},{2,17},{3,20},{4,19},{5,22},{6,21},{7,24},{8,23},{9,... | collective-permute-start | bytes 122888 | tf_op jit(solution)/shard_map/ppermute | solution.py:447
  19.0 6.4 %collective-permute-start = (f32[16,16,128]{2,1,0:T(8,128)S(1)}, f32[16,16,128]{2,1,0:T(8,128)S(1)}, u32[]{:S(2)}, u32[]{:S(2)}) collective-permute-start(f32[16,16,128]{2,1,0:T(8,128)S(1)} %get-tuple-element.16), channel_id=1, source_target_pairs={{0,16},{16,32},{32,48},{48,64},{64,80},{80,96},{96,112},{112,128},... | collective-permute-start | bytes 393224 | tf_op jit(solution)/shard_map/ppermute | solution.py:448
  21.7 3.7 %copy-start.1 = (f32[16,16,128]{2,1,0:T(8,128)S(1)}, f32[16,16,128]{2,1,0:T(8,128)}, u32[]{:S(2)}) copy-start(f32[16,16,128]{2,1,0:T(8,128)} %first.5) | copy-start | bytes 393220
  22.8 17.2 %collective-permute-start.3 = (f32[14,16,128]{2,1,0:T(8,128)S(1)}, f32[14,16,128]{2,1,0:T(8,128)S(1)}, u32[]{:S(2)}, u32[]{:S(2)}) collective-permute-start(f32[14,16,128]{2,1,0:T(8,128)S(1)} %get-tuple-element.20.own_far), channel_id=1, source_target_pairs={{0,15},{1,2},{2,1},{3,4},{4,3},{5,6},{6,5},{7,8},{8,7},{9,10},{10,... | collective-permute-start | bytes 344072 | tf_op jit(solution)/shard_map/ppermute | solution.py:457
  26.0 14.0 %copy-start.5 = (f32[256,128]{1,0:T(8,128)S(1)}, f32[256,128]{1,0:T(8,128)}, u32[]{:S(2)}) copy-start(f32[256,128]{1,0:T(8,128)} %constant.42.clone.down_y) | copy-start | bytes 393220
  26.0 14.0 %copy-start.9 = (f32[64,128]{1,0:T(8,128)S(1)}, f32[64,128]{1,0:T(8,128)}, u32[]{:S(2)}) copy-start(f32[64,128]{1,0:T(8,128)} %constant.43.clone.down_x) | copy-start | bytes 98308
  26.0 14.0 %collective-permute-start.1 = (f32[19,16,128]{2,1,0:T(8,128)S(1)}, f32[19,16,128]{2,1,0:T(8,128)S(1)}, u32[]{:S(2)}, u32[]{:S(2)}) collective-permute-start(f32[19,16,128]{2,1,0:T(8,128)S(1)} %shard_map.102), channel_id=1, source_target_pairs={{0,1},{1,0},{2,3},{3,2},{4,5},{5,4},{6,7},{7,6},{8,9},{9,8},{10,11... | collective-permute-start | bytes 466952 | tf_op jit(solution)/shard_map/ppermute | solution.py:461
  30.1 37.2 %copy-start.3 = (f32[128,128]{1,0:T(8,128)S(1)}, f32[128,128]{1,0:T(8,128)}, u32[]{:S(2)}) copy-start(f32[128,128]{1,0:T(8,128)} %constant.46.clone.denom) | copy-start | bytes 196612
  30.1 37.2 %copy-start.8 = (f32[128,128]{1,0:T(8,128)S(1)}, f32[128,128]{1,0:T(8,128)}, u32[]{:S(2)}) copy-start(f32[128,128]{1,0:T(8,128)} %constant.44.clone.table) | copy-start | bytes 196612
  30.1 37.2 %copy-start.10 = (f32[8]{0:T(128)S(1)}, f32[8]{0:T(128)}, u32[]{:S(2)}) copy-start(f32[8]{0:T(128)} %constant.47.clone.shift_x) | copy-start | bytes 100
  40.0 50.6 %copy-start.7 = (f32[2,64,128]{2,1,0:T(8,128)S(1)}, f32[2,64,128]{2,1,0:T(8,128)}, u32[]{:S(2)}) copy-start(f32[2,64,128]{2,1,0:T(8,128)} %constant.45.clone.inverse_z) | copy-start | bytes 196612
  67.3 43.5 %copy-start.4 = (f32[128,256]{1,0:T(8,128)S(1)}, f32[128,256]{1,0:T(8,128)}, u32[]{:S(2)}) copy-start(f32[128,256]{1,0:T(8,128)} %constant.49.clone.up_y) | copy-start | bytes 393220
  67.3 43.5 %copy-start.6 = (f32[128,64]{1,0:T(8,128)S(1)}, f32[128,64]{1,0:T(8,128)}, u32[]{:S(2)}) copy-start(f32[128,64]{1,0:T(8,128)} %constant.48.clone.up_x) | copy-start | bytes 98308

commit v3 on v2

--- a/solution.py
+++ b/solution.py
@@ -16,10 +16,10 @@
 diffusion = 1.0
 reaction = 1.0
 
-G_AT = (0, 4, 7, 9)
-U_AT = 10
-PACK = 14
-REACH = 5
+G_AT = (0, 3, 5, 6)
+U_AT = 6
+PACK = 10
+REACH = 4
 
 
 def basis_coefficients(nodes, chosen):
@@ -72,6 +72,7 @@
     [step_length * (INTEG[j][k] - (SPACING[j] if j == k else 0.0)) for k in range(5)]
     for j in range(4)
 ]
+COUPLING = 0.5 * step_length * diffusion * 0.25
 QUAD = [[step_length * (INTEG[2 * c][k] + INTEG[2 * c + 1][k]) for k in range(5)] for c in range(2)]
 
 
@@ -104,17 +105,36 @@
     up_x = up_x.reshape(planes * rows, rows_c * planes)
     cos_z = np.cos(2.0 * np.pi * np.arange(depth) / depth)
     cos_y = np.cos(2.0 * np.pi * np.arange(cols_c) / cols_c)
-    half = 0.5 * step_length * diffusion * 0.25
+    half = COUPLING
+    cos_x = np.cos(2.0 * np.pi * np.arange(rows_c) / rows_c)
+    stencil = half * (6.0 - 2.0 * cos_x[:, None, None] - 2.0 * cos_y[None, None, :])
+    stencil = np.broadcast_to(stencil, (rows_c, planes, cols_c)).reshape(-1, cols_c)
+    stencil = np.concatenate([stencil, stencil], 1)
+    blocks = depth // planes
+    forward_z = np.zeros((depth, blocks, 2, planes))
+    forward_z[:, :, 0, :] = hz.reshape(depth, blocks, planes)
+    for s in range(blocks):
+        forward_z[:, s, 1, 0] = hz[:, (s * planes - 1) % depth]
+        forward_z[:, s, 1, planes - 1] = hz[:, (s * planes + planes) % depth]
+    forward_z = forward_z.reshape(depth, -1)
     denom = 1.0 - half * (2.0 * cos_z[:, None] + 2.0 * cos_y[None, :] - 6.0)
     denom = np.concatenate([denom, denom], 1)
-    shift_x = half * 2.0 * np.cos(2.0 * np.pi * np.arange(rows_c) / rows_c)
+    shift_x = half * 2.0 * cos_x
     inverse_z = hz.reshape(4, 2, 2, planes, depth).transpose(1, 0, 2, 3, 4)
     inverse_z = inverse_z.reshape(2, 8 * planes, depth)
     f32 = lambda a: jnp.asarray(a, jnp.float32)
     return (
-        f32(block_pair(down_y)), f32(down_x), f32(hz), f32(inverse_z), f32(denom), f32(shift_x),
-        f32(up_x), f32(block_pair(up_y)),
-    )
+        f32(block_pair(down_y)), f32(down_x), f32(stencil), f32(forward_z), f32(inverse_z),
+        f32(denom), f32(shift_x), f32(up_x), f32(block_pair(up_y)),
+    )
+
+
+def lanes_swapped(a):
+    return pltpu.roll(a, a.shape[1] // 2, 1)
+
+
+def left_half(a):
+    return lax.broadcasted_iota(jnp.int32, a.shape, 1) < a.shape[1] // 2
 
 
 def dot(a, b):
@@ -148,7 +168,7 @@
 
     def packed(out, plane_of):
         for j in range(4):
-            for i in range(4 - j):
+            for i in range(3 - j):
                 out[G_AT[j] + i] = g[j, plane_of(i)]
             edge = plane_of(0)
             out[U_AT + j] = diffusion * sum(MIX[j][k] * u[k, edge] for k in range(5))
@@ -167,31 +187,26 @@
         packed(far, top)
 
 
-def edge_planes(out, at, field, core, low):
-    planes = field.shape[0]
-
-    @pl.when((core == 0) == low)
-    def _():
-        for i in range(REACH):
-            out[at + i] = field[i]
-
-    @pl.when((core == 0) != low)
-    def _():
-        for i in range(REACH):
-            out[at + i] = field[planes - 1 - i]
-
-
-def last_kernel(place, u, first, last, start_out):
+def last_kernel(place, u, first, last, start_out, sems):
     position, core, slices = place[0], place[1], place[6]
-    last[...] = u[0, 0]
+    planes = last.shape[0]
+    edge = pl.ds(core * (planes - REACH), REACH)
+    whole = pltpu.make_async_copy(u.at[0, 4], last, sems.at[0])
+    whole.start()
 
     @pl.when(position == slices - 1)
     def _():
-        edge_planes(start_out, 0, first, core, True)
+        part = pltpu.make_async_copy(first.at[edge], start_out, sems.at[1])
+        part.start()
+        part.wait()
 
     @pl.when(position != slices - 1)
     def _():
-        edge_planes(start_out, 0, last, core, True)
+        part = pltpu.make_async_copy(u.at[0, 4, edge], start_out, sems.at[1])
+        part.start()
+        part.wait()
+
+    whole.wait()
 
 
 def relay_kernel(got, out):
@@ -200,20 +215,21 @@
 
 def near_kernel(place, first, previous, own_near, out):
     position, core = place[0], place[1]
+    edge = pl.ds((1 - core) * (first.shape[0] - REACH), REACH)
     out[:PACK] = own_near[...]
 
     @pl.when(position == 0)
     def _():
-        edge_planes(out, PACK, first, core, False)
+        out[PACK:] = first[edge]
 
     @pl.when(position != 0)
     def _():
-        edge_planes(out, PACK, previous, core, False)
+        out[PACK:] = previous[edge]
 
 
 def sweep_kernel(
     place, first, previous, near, start_far, g, own_near, own_far, got_far,
-    down_y, down_x, w, send, hats, quad,
+    down_y, down_x, stencil, w, send, hats, quad,
 ):
     got_near, start_near = near.at[:PACK], near.at[PACK:]
     planes = first.shape[0]
@@ -238,16 +254,19 @@
         w[0, REACH : REACH + planes] = previous[...]
 
     def run(start_lo, own_lo, got_lo, start_hi, own_hi, got_hi):
-        for i in range(REACH):
-            w[0, REACH - 1 - i] = start_lo[i]
-            w[0, REACH + planes + i] = start_hi[i]
+        w[0, :REACH] = start_lo[...]
+        w[0, REACH + planes :] = start_hi[...]
         for m in range(5):
-            margin = 4 - m
-            held = [None, None]
+            margin = max(3 - m, 0)
+            held = None
             for p in range(-margin, planes + margin):
                 at = p + REACH
                 field = w[m, at]
-                force = plane_part(field) + diffusion * (w[m, at - 1] + w[m, at + 1])
+                force = plane_part(field)
+                if m < 4 or p > 0:
+                    force = force + diffusion * w[m, at - 1]
+                if m < 4 or p < planes - 1:
+                    force = force + diffusion * w[m, at + 1]
                 if m < 4:
                     if p < 0:
                         source = got_lo[G_AT[m] - p - 1]
@@ -286,27 +305,35 @@
     q0 = quad[0].reshape(rows, -1) + mask * restart
     q1 = quad[1].reshape(rows, -1)
     table = down_y[...]
+    edge_rows = first.shape[1]
+    middle = jnp.zeros((rows - 2 * edge_rows, first.shape[2]), jnp.float32)
+    edges = jnp.concatenate([w[4, REACH], middle, w[4, REACH + planes - 1]], 0)
     left = [
         dot(jnp.concatenate(pair, 1), table)
-        for pair in ((q0, q1), (paired(2), paired(4)), (restart, restart))
+        for pair in ((q0, q1), (paired(2), paired(4)), (restart, edges))
     ]
     spectral = dot(down_x[...], jnp.concatenate(left, 1))
     width = left[0].shape[1]
+    states = spectral[:, width : 2 * width]
+    third = spectral[:, 2 * width :]
+    count = spectral.shape[0]
+    level = lax.broadcasted_iota(jnp.int32, states.shape, 0) % coarse
+    near_z = jnp.where(level > 0, pltpu.roll(states, 1, 0), 0.0)
+    near_z = near_z + jnp.where(level < coarse - 1, pltpu.roll(states, count - 1, 0), 0.0)
+    inside = spectral[:, :width] + stencil[...] * states - COUPLING * near_z
+    is_left = left_half(states)
+    last = jnp.where(is_left, lanes_swapped(third), third)
+    last = last * jnp.where(is_left, diffusion * QUAD[0][4], diffusion * QUAD[1][4])
+    spill = last - COUPLING * states
+    spill = jnp.where((level == 0) | (level == coarse - 1), spill, 0.0)
     for y in range(4):
         for c in range(2):
             kx = 2 * y + c
-            block = spectral[kx * coarse : (kx + 1) * coarse, : 2 * width]
-            send[4 * y + c] = block
-            send[4 * y + 2 + c] = block
+            span = slice(kx * coarse, (kx + 1) * coarse)
+            for zh in range(2):
+                send[4 * y + 2 * zh + c, :coarse] = inside[span]
+                send[4 * y + 2 * zh + c, coarse:] = spill[span]
     hats[...] = spectral[:, width:]
-
-
-def lanes_swapped(a):
-    return pltpu.roll(a, a.shape[1] // 2, 1)
-
-
-def left_half(a):
-    return lax.broadcasted_iota(jnp.int32, a.shape, 1) < a.shape[1] // 2
 
 
 def spectrum_kernel(place, shift_x, got, table, denom, lifted, offset, copies):
@@ -314,9 +341,7 @@
     half = depth // 2
     d = denom[...] - shift_x[place[4]]
     inv = 1.0 / d
-    spectra = dot(table[...], got[...].reshape(depth, -1))
-    width = d.shape[1]
-    lift = spectra[:, :width] - (1.0 - d) * spectra[:, width:]
+    lift = dot(table[...], got[...].reshape(-1, d.shape[1]))
     weighted = lift * inv
     weighted = jnp.where(left_half(d), weighted * inv, weighted)
     total = weighted + lanes_swapped(weighted)
@@ -392,22 +417,21 @@
             out[m, 2 * i + 1] = w[m, REACH + 2 * i + 1] + piece
 
 
-def call(kernel, outs, scalars, *args, scratch=(), flops=0, blocked={}):
+def call(kernel, outs, scalars, *args, scratch=(), flops=0, in_hbm=False):
     smem = pl.BlockSpec(memory_space=pltpu.SMEM)
     vmem = pl.BlockSpec(memory_space=pltpu.VMEM)
+    hbm = pl.BlockSpec(memory_space=pltpu.HBM)
     single = not isinstance(outs, list)
     shapes = [jax.ShapeDtypeStruct(s, jnp.float32) for s in ([outs] if single else outs)]
     result = pl.pallas_call(
         kernel,
-        grid=(1,) if blocked else (),
         out_shape=shapes[0] if single else shapes,
-        in_specs=[
-            smem if i < len(scalars) else blocked.get(i, vmem)
-            for i in range(len(scalars) + len(args))
-        ],
+        in_specs=[smem] * len(scalars) + [hbm if in_hbm else vmem] * len(args),
         out_specs=vmem if single else [vmem] * len(shapes),
-        scratch_shapes=[pltpu.VMEM(s, jnp.float32) for s in scratch],
-        compiler_params=pltpu.CompilerParams(vmem_limit_bytes=32 * 1024 * 1024),
+        scratch_shapes=list(scratch),
+        compiler_params=pltpu.CompilerParams(
+            vmem_limit_bytes=(63 if in_hbm else 32) * 1024 * 1024
+        ),
         cost_estimate=pl.CostEstimate(flops=flops, bytes_accessed=1 << 20, transcendentals=0),
     )(*scalars, *args)
     return result
@@ -419,7 +443,7 @@
     slices = lax.axis_size(TM)
     blocks = lax.axis_size(SPACE)
     depth_c = coarse * blocks
-    down_y, down_x, table_z, inverse_z, denom, shift_x, up_x, up_y = tables(
+    down_y, down_x, stencil, forward_z, inverse_z, denom, shift_x, up_x, up_y = tables(
         coarse, rows, cols, depth_c
     )
     position = lax.axis_index(TM)
@@ -433,7 +457,8 @@
         [(planes, rows, cols), (REACH, rows, cols)],
         [place],
         u_old, u_init,
-        blocked={1: pl.BlockSpec((1, 1, planes, rows, cols), lambda i: (0, 4, 0, 0, 0))},
+        scratch=[pltpu.SemaphoreType.DMA((2,))],
+        in_hbm=True,
     )
 
     def far_block(s):
@@ -464,13 +489,13 @@
         sweep_kernel,
         [
             (5, planes + 2 * REACH, rows, cols),
-            (blocks, coarse, 4 * cols_c),
+            (blocks, 2 * coarse, 2 * cols_c),
             (rows_c * coarse, 4 * cols_c),
         ],
         [place],
         u_init, previous, near, start_far, g, own_near, own_far, got_far,
-        down_y, down_x,
-        scratch=[(2, coarse, rows, cols)],
+        down_y, down_x, stencil,
+        scratch=[pltpu.VMEM((2, coarse, rows, cols), jnp.float32)],
     )
     columns = lax.all_to_all(send, SPACE, 0, 0, tiled=True)
     packed = (lax.axis_size("zl"), depth_c // 2, 2 * cols_c)
@@ -478,7 +503,7 @@
         spectrum_kernel,
         [(depth_c, 2 * cols_c), (depth_c, 2 * cols_c), packed],
         [place, shift_x],
-        columns, table_z, denom,
+        columns, forward_z, denom,
     )
     gathered = lax.all_to_all(copies, "zl", 0, 0, tiled=True)
     back = call(

time: 113 us -> 111 us (0.982)
  blocking collectives: 66.9 us -> 65.1 us
  Pallas kernels: 7.96 us -> 9.67 us
  local copies, waits for them, and re-layouts: 2.14 us -> 0.69 us
    unnamed x22 -> x24, local copies, waits for them, and re-layouts: 2.05 us -> 0.08 us
    pallas_call x8, Pallas kernels: 7.96 us -> 9.67 us  [call(): pl.pallas_call(kernel, out_shape=shapes[0] if single else shapes, in_spec...]
    all_to_all x1, blocking collectives: 25.5 us -> 24 us  [shards(): columns = lax.all_to_all(send, SPACE, 0, 0, tiled=True)]
where the time goes in v3:
time: 111 us; the launch traced here: 110 us
  blocking collectives  65.1 us (59%)
  starting transfers between devices  26 us (23%)
  Pallas kernels  9.67 us (9%)
  waiting for transfers between devices  8.81 us (8%)
    all_to_all x1, blocking collectives, shards(): columns = lax.all_to_all(send, SPACE, 0, 0, tiled=True)  24 us
    all_to_all x1, blocking collectives, shards(): gathered = lax.all_to_all(copies, 'zl', 0, 0, tiled=True)  22.3 us
    all_to_all x1, blocking collectives, shards(): returned = lax.all_to_all(back, ('x', 'y', 'c'), 0, 0, tiled=True)  18.8 us
    ppermute x1, starting transfers between devices, shards(): start_far = lax.ppermute(start_out, TM + SPACE, across)  16.4 us
    pallas_call x8, Pallas kernels, call(): pl.pallas_call(kernel, out_shape=shapes[0] if single else shapes, in_spec...  9.67 us
    ppermute x1, waiting for transfers between devices, shards(): lax.ppermute(own_far, SPACE, [(s, far_block(s)) for s in range(blocks)])  8.8 us
    ppermute x1, starting transfers between devices, shards(): near = lax.ppermute(near_out, 'c', [(0, 1), (1, 0)])  4.3 us
    ppermute x1, starting transfers between devices, shards(): previous = lax.ppermute(last, TM, [(i, i + 1) for i in range(slices - 1)])  2.65 us
  transfers between devices with their start and end apart: 4, of which 1 were waited for; matrix products, arithmetic and copies ran while one was open for 0% of the time, Pallas kernels for 1%

profile of v3, /device:TPU:1, one launch (start us, length us, event | category | flops | bytes accessed | tf_op | source)
XLA Modules:
  0.0 110.4 jit_solution(14902172508169844754)
XLA Ops:
  0.0 0.6 stack.27.place
  0.6 2.2 %shard_map.109 = (f32[16,16,128]{2,1,0:T(8,128)}, f32[4,16,128]{2,1,0:T(8,128)}) custom-call(s32[7]{0:T(128)} %stack.27.place, f32[1,5,16,16,128]{4,3,2,1,0:T(8,128)} %u.1, f32[16,16,128]{2,1,0:T(8,128)} %first.5), custom_call_target="tpu_custom_call" | custom-call | bytes 1048576 | tf_op jit(solution)/shard_map/pallas_call | solution.py:426
  2.9 16.4 %collective-permute-start.2 = (f32[4,16,128]{2,1,0:T(8,128)}, f32[4,16,128]{2,1,0:T(8,128)S(1)}, u32[]{:S(2)}, u32[]{:S(2)}) collective-permute-start(f32[4,16,128]{2,1,0:T(8,128)} %get-tuple-element.18), channel_id=1, source_target_pairs={{0,31},{1,18},{2,17},{3,20},{4,19},{5,22},{6,21},{7,24},{8,23},{9,... | collective-permute-start | bytes 98312 | tf_op jit(solution)/shard_map/ppermute | solution.py:472
  19.3 2.6 %collective-permute-start = (f32[16,16,128]{2,1,0:T(8,128)}, f32[16,16,128]{2,1,0:T(8,128)S(1)}, u32[]{:S(2)}, u32[]{:S(2)}) collective-permute-start(f32[16,16,128]{2,1,0:T(8,128)} %get-tuple-element.16), channel_id=1, source_target_pairs={{0,16},{16,32},{32,48},{48,64},{64,80},{80,96},{96,112},{112,128},... | collective-permute-start | bytes 393224 | tf_op jit(solution)/shard_map/ppermute | solution.py:473
  22.0 1.0 shard_map.110
  23.0 2.6 %collective-permute-start.3 = (f32[10,16,128]{2,1,0:T(8,128)S(1)}, f32[10,16,128]{2,1,0:T(8,128)S(1)}, u32[]{:S(2)}, u32[]{:S(2)}) collective-permute-start(f32[10,16,128]{2,1,0:T(8,128)S(1)} %get-tuple-element.20.own_far), channel_id=1, source_target_pairs={{0,15},{1,2},{2,1},{3,4},{4,3},{5,6},{6,5},{7,8},{8,7},{9,10},{10,... | collective-permute-start | bytes 245768 | tf_op jit(solution)/shard_map/ppermute | solution.py:482
  25.7 0.6 shard_map.111
  26.2 0.0 copy-start.4
  26.2 0.0 copy-start.8
  26.3 0.0 copy-start.9
  26.3 4.3 %collective-permute-start.1 = (f32[14,16,128]{2,1,0:T(8,128)S(1)}, f32[14,16,128]{2,1,0:T(8,128)S(1)}, u32[]{:S(2)}, u32[]{:S(2)}) collective-permute-start(f32[14,16,128]{2,1,0:T(8,128)S(1)} %shard_map.111), channel_id=1, source_target_pairs={{0,1},{1,0},{2,3},{3,2},{4,5},{5,4},{6,7},{7,6},{8,9},{9,8},{10,11... | collective-permute-start | bytes 344072 | tf_op jit(solution)/shard_map/ppermute | solution.py:486
  30.6 8.8 %collective-permute-done.3.got_far = f32[10,16,128]{2,1,0:T(8,128)S(1)} collective-permute-done((f32[10,16,128]{2,1,0:T(8,128)S(1)}, f32[10,16,128]{2,1,0:T(8,128)S(1)}, u32[]{:S(2)}, u32[]{:S(2)}) %collective-permute-start.3) | collective-permute-done | bytes 81952 | tf_op jit(solution)/shard_map/ppermute | solution.py:482
  39.4 1.9 %shard_map.113 = (f32[5,24,16,128]{3,2,1,0:T(8,128)S(1)}, f32[16,16,128]{2,1,0:T(8,128)S(1)}, f32[64,256]{1,0:T(8,128)S(1)}) custom-call(s32[7]{0:T(128)S(1)} %copy-done.10, f32[16,16,128]{2,1,0:T(8,128)S(1)} %copy-done, f32[16,16,128]{2,1,0:T(8,128)S(1)} %collective-permute-done.previous, f32[14,16,128]{2,1,0:T(8,128)S(1)} %collective-permute-done.1.near, ...), custom_call_target="tpu_custom_call" | custom-call | bytes 1048576 | tf_op jit(solution)/shard_map/pallas_call | solution.py:426
  41.3 0.0 copy-start.2
  41.3 0.0 copy-start.5
  41.3 0.0 copy-start.11
  41.3 24.0 %all_to_all.15.got = f32[16,16,128]{2,1,0:T(8,128)S(1)} all-to-all(f32[16,16,128]{2,1,0:T(8,128)S(1)} %get-tuple-element.22), channel_id=1, replica_groups=mesh['x'=4,'zl'=8,'y'=4,'zh'=2,'c'=2] {'y','zh','c'}, dimensions={0} | all-to-all | bytes 262144 | tf_op jit(solution)/shard_map/all_to_all | solution.py:500
  65.3 0.9 shard_map.114
  66.2 0.0 copy-start.7
  66.2 22.3 %all_to_all.16.all_offsets = f32[8,64,128]{2,1,0:T(8,128)S(1)} all-to-all(f32[8,64,128]{2,1,0:T(8,128)S(1)} %get-tuple-element.23), channel_id=1, replica_groups=mesh['x'=4,'zl'=8,'y'=4,'zh'=2,'c'=2] {'zl'}, dimensions={0} | all-to-all | bytes 524288 | tf_op jit(solution)/shard_map/all_to_all | solution.py:508
  88.5 1.1 shard_map.115
  89.6 0.0 copy-start.3
  89.7 18.8 %all_to_all.17.got = f32[32,8,256]{2,1,0:T(8,128)S(1)} all-to-all(f32[32,8,256]{2,1,0:T(8,128)S(1)} %shard_map.115), channel_id=1, replica_groups=mesh['x'=4,'zl'=8,'y'=4,'zh'=2,'c'=2] {'x','y','c'}, dimensions={0} | all-to-all | bytes 524288 | tf_op jit(solution)/shard_map/all_to_all | solution.py:515
  108.4 2.0 %shard_map.116 = f32[5,16,16,128]{3,2,1,0:T(8,128)} custom-call(s32[7]{0:T(128)S(1)} %copy-done.10, f32[5,24,16,128]{3,2,1,0:T(8,128)S(1)} %get-tuple-element.21.w, f32[32,8,256]{2,1,0:T(8,128)S(1)} %all_to_all.17.got, f32[64,256]{1,0:T(8,128)S(1)} %get-tuple-element.26.hats, f32[128,64]{1,0:T(8,128)S(1)} %copy-done.6, f32[128,256]{1,0:T(8,128)S(1)} %copy-done.3), custom_call_target="tpu_custom_call" | custom-call | bytes 1048576 | tf_op jit(solution)/shard_map/pallas_call | solution.py:426
  (20 shorter events, 0.1 us)
Async XLA Ops:
  0.0 21.9 %copy-start.1 = (f32[1,5,16,16,128]{4,3,2,1,0:T(8,128)S(1)}, f32[1,5,16,16,128]{4,3,2,1,0:T(8,128)}, u32[]{:S(2)}) copy-start(f32[1,5,16,16,128]{4,3,2,1,0:T(8,128)} %u.1) | copy-start | bytes 1966084
  2.9 27.7 %collective-permute-start.2 = (f32[4,16,128]{2,1,0:T(8,128)}, f32[4,16,128]{2,1,0:T(8,128)S(1)}, u32[]{:S(2)}, u32[]{:S(2)}) collective-permute-start(f32[4,16,128]{2,1,0:T(8,128)} %get-tuple-element.18), channel_id=1, source_target_pairs={{0,31},{1,18},{2,17},{3,20},{4,19},{5,22},{6,21},{7,24},{8,23},{9,... | collective-permute-start | bytes 98312 | tf_op jit(solution)/shard_map/ppermute | solution.py:472
  19.3 2.7 %copy-start.10 = (s32[7]{0:T(128)S(1)}, s32[7]{0:T(128)}, u32[]{:S(2)}) copy-start(s32[7]{0:T(128)} %stack.27.place) | copy-start | bytes 88
  19.3 6.4 %collective-permute-start = (f32[16,16,128]{2,1,0:T(8,128)}, f32[16,16,128]{2,1,0:T(8,128)S(1)}, u32[]{:S(2)}, u32[]{:S(2)}) collective-permute-start(f32[16,16,128]{2,1,0:T(8,128)} %get-tuple-element.16), channel_id=1, source_target_pairs={{0,16},{16,32},{32,48},{48,64},{64,80},{80,96},{96,112},{112,128},... | collective-permute-start | bytes 393224 | tf_op jit(solution)/shard_map/ppermute | solution.py:473
  21.9 3.7 %copy-start = (f32[16,16,128]{2,1,0:T(8,128)S(1)}, f32[16,16,128]{2,1,0:T(8,128)}, u32[]{:S(2)}) copy-start(f32[16,16,128]{2,1,0:T(8,128)} %first.5) | copy-start | bytes 393220
  23.0 16.4 %collective-permute-start.3 = (f32[10,16,128]{2,1,0:T(8,128)S(1)}, f32[10,16,128]{2,1,0:T(8,128)S(1)}, u32[]{:S(2)}, u32[]{:S(2)}) collective-permute-start(f32[10,16,128]{2,1,0:T(8,128)S(1)} %get-tuple-element.20.own_far), channel_id=1, source_target_pairs={{0,15},{1,2},{2,1},{3,4},{4,3},{5,6},{6,5},{7,8},{8,7},{9,10},{10,... | collective-permute-start | bytes 245768 | tf_op jit(solution)/shard_map/ppermute | solution.py:482
  26.2 13.2 %copy-start.4 = (f32[256,128]{1,0:T(8,128)S(1)}, f32[256,128]{1,0:T(8,128)}, u32[]{:S(2)}) copy-start(f32[256,128]{1,0:T(8,128)} %constant.44.clone.down_y) | copy-start | bytes 393220
  26.2 13.2 %copy-start.8 = (f32[64,128]{1,0:T(8,128)S(1)}, f32[64,128]{1,0:T(8,128)}, u32[]{:S(2)}) copy-start(f32[64,128]{1,0:T(8,128)} %constant.46.clone.stencil) | copy-start | bytes 98308
  26.3 13.2 %copy-start.9 = (f32[64,128]{1,0:T(8,128)S(1)}, f32[64,128]{1,0:T(8,128)}, u32[]{:S(2)}) copy-start(f32[64,128]{1,0:T(8,128)} %constant.45.clone.down_x) | copy-start | bytes 98308
  26.3 13.1 %collective-permute-start.1 = (f32[14,16,128]{2,1,0:T(8,128)S(1)}, f32[14,16,128]{2,1,0:T(8,128)S(1)}, u32[]{:S(2)}, u32[]{:S(2)}) collective-permute-start(f32[14,16,128]{2,1,0:T(8,128)S(1)} %shard_map.111), channel_id=1, source_target_pairs={{0,1},{1,0},{2,3},{3,2},{4,5},{5,4},{6,7},{7,6},{8,9},{9,8},{10,11... | collective-permute-start | bytes 344072 | tf_op jit(solution)/shard_map/ppermute | solution.py:486
  41.3 24.0 %copy-start.2 = (f32[128,128]{1,0:T(8,128)S(1)}, f32[128,128]{1,0:T(8,128)}, u32[]{:S(2)}) copy-start(f32[128,128]{1,0:T(8,128)} %constant.49.clone.denom) | copy-start | bytes 196612
  41.3 24.0 %copy-start.5 = (f32[128,256]{1,0:T(8,128)S(1)}, f32[128,256]{1,0:T(8,128)}, u32[]{:S(2)}) copy-start(f32[128,256]{1,0:T(8,128)} %constant.47.clone.table) | copy-start | bytes 393220
  41.3 24.0 %copy-start.11 = (f32[8]{0:T(128)S(1)}, f32[8]{0:T(128)}, u32[]{:S(2)}) copy-start(f32[8]{0:T(128)} %constant.50.clone.shift_x) | copy-start | bytes 100
  66.2 22.3 %copy-start.7 = (f32[2,64,128]{2,1,0:T(8,128)S(1)}, f32[2,64,128]{2,1,0:T(8,128)}, u32[]{:S(2)}) copy-start(f32[2,64,128]{2,1,0:T(8,128)} %constant.48.clone.inverse_z) | copy-start | bytes 196612
  89.6 18.8 %copy-start.3 = (f32[128,256]{1,0:T(8,128)S(1)}, f32[128,256]{1,0:T(8,128)}, u32[]{:S(2)}) copy-start(f32[128,256]{1,0:T(8,128)} %constant.52.clone.up_y) | copy-start | bytes 393220
  89.7 18.8 %copy-start.6 = (f32[128,64]{1,0:T(8,128)S(1)}, f32[128,64]{1,0:T(8,128)}, u32[]{:S(2)}) copy-start(f32[128,64]{1,0:T(8,128)} %constant.51.clone.up_x) | copy-start | bytes 98308

commit v4 on v3

--- a/solution.py
+++ b/solution.py
@@ -9,7 +9,7 @@
 from jax.sharding import Mesh
 from jax.sharding import PartitionSpec as P
 
-TM = ("x", "zl")
+TM = ("x", "zb", "za")
 SPACE = ("y", "zh", "c")
 
 step_length = 0.4
@@ -187,26 +187,17 @@
         packed(far, top)
 
 
-def last_kernel(place, u, first, last, start_out, sems):
+def edge_kernel(place, last, first, start_out):
     position, core, slices = place[0], place[1], place[6]
-    planes = last.shape[0]
-    edge = pl.ds(core * (planes - REACH), REACH)
-    whole = pltpu.make_async_copy(u.at[0, 4], last, sems.at[0])
-    whole.start()
+    edge = pl.ds(core * (first.shape[0] - REACH), REACH)
 
     @pl.when(position == slices - 1)
     def _():
-        part = pltpu.make_async_copy(first.at[edge], start_out, sems.at[1])
-        part.start()
-        part.wait()
+        start_out[...] = first[edge]
 
     @pl.when(position != slices - 1)
     def _():
-        part = pltpu.make_async_copy(u.at[0, 4, edge], start_out, sems.at[1])
-        part.start()
-        part.wait()
-
-    whole.wait()
+        start_out[...] = last[edge]
 
 
 def relay_kernel(got, out):
@@ -352,25 +343,44 @@
         copies[i] = packed
 
 
-def scan_kernel(place, shift_x, all_offsets, lifted, offset, denom, inverse_z, out):
-    zl, block, zh = place[2], place[3], place[5]
-    slices = all_offsets.shape[0]
-    half = all_offsets.shape[1]
+def packed_inverse(place, shift_x, denom):
     d = denom[...] - shift_x[place[4]]
     inv = 1.0 / d
+    half = inv.shape[0] // 2
     left = left_half(inv[:half])
-    inv_packed = jnp.where(left, inv[:half], inv[half:])
+    return inv, left, jnp.where(left, inv[:half], inv[half:])
+
+
+def group_kernel(place, shift_x, offsets, denom, total_out, prefix_out):
+    za = place[2]
+    _, _, inv = packed_inverse(place, shift_x, denom)
+    inv2 = inv * inv
+    total = jnp.zeros_like(inv2)
+    prefix = jnp.zeros_like(inv2)
+    for m in range(offsets.shape[0]):
+        piece = offsets[m]
+        total = total * inv2 + piece
+        prefix = jnp.where(m < za, prefix * inv2 + piece, prefix)
+    total_out[...] = total
+    prefix_out[...] = prefix
+
+
+def scan_kernel(
+    place, shift_x, own_total, other_total, own_prefix, lifted, offset, denom, inverse_z, out
+):
+    za, block, zh, zb = place[2], place[3], place[5], place[7]
+    inv, left, inv_packed = packed_inverse(place, shift_x, denom)
     inv2 = inv_packed * inv_packed
-    prefix = jnp.zeros_like(inv2)
-    total = jnp.zeros_like(inv2)
-    power = jnp.ones_like(inv2)
-    whole = jnp.ones_like(inv2)
-    for m in range(slices):
-        piece = all_offsets[m]
-        total = total * inv2 + piece
-        prefix = jnp.where(m < zl, prefix * inv2 + piece, prefix)
-        power = jnp.where(m < zl, power * inv2, power)
-        whole = whole * inv2
+    inv4 = inv2 * inv2
+    inv8 = inv4 * inv4
+    whole = inv8 * inv8
+    power = jnp.where(za % 2 == 1, inv2, 1.0)
+    power = jnp.where(za >= 2, power * inv4, power)
+    early = jnp.where(zb == 0, own_total[...], other_total[...])
+    late = jnp.where(zb == 0, other_total[...], own_total[...])
+    prefix = own_prefix[...] + jnp.where(zb == 0, 0.0, power * early)
+    total = early * inv8 + late
+    power = jnp.where(zb == 0, power, power * inv8)
     inverse = inverse_z[zh]
     weights = jnp.where(left_half(inv), inv, inv * inv)
     own = jnp.where(left_half(inv), lifted[...] * inv, offset[...])
@@ -417,21 +427,18 @@
             out[m, 2 * i + 1] = w[m, REACH + 2 * i + 1] + piece
 
 
-def call(kernel, outs, scalars, *args, scratch=(), flops=0, in_hbm=False):
+def call(kernel, outs, scalars, *args, scratch=(), flops=0):
     smem = pl.BlockSpec(memory_space=pltpu.SMEM)
     vmem = pl.BlockSpec(memory_space=pltpu.VMEM)
-    hbm = pl.BlockSpec(memory_space=pltpu.HBM)
     single = not isinstance(outs, list)
     shapes = [jax.ShapeDtypeStruct(s, jnp.float32) for s in ([outs] if single else outs)]
     result = pl.pallas_call(
         kernel,
         out_shape=shapes[0] if single else shapes,
-        in_specs=[smem] * len(scalars) + [hbm if in_hbm else vmem] * len(args),
+        in_specs=[smem] * len(scalars) + [vmem] * len(args),
         out_specs=vmem if single else [vmem] * len(shapes),
         scratch_shapes=list(scratch),
-        compiler_params=pltpu.CompilerParams(
-            vmem_limit_bytes=(63 if in_hbm else 32) * 1024 * 1024
-        ),
+        compiler_params=pltpu.CompilerParams(vmem_limit_bytes=32 * 1024 * 1024),
         cost_estimate=pl.CostEstimate(flops=flops, bytes_accessed=1 << 20, transcendentals=0),
     )(*scalars, *args)
     return result
@@ -449,17 +456,12 @@
     position = lax.axis_index(TM)
     core = lax.axis_index("c")
     kx = 2 * lax.axis_index("y") + core
-    place = [position, core, lax.axis_index("zl"), lax.axis_index("x"), kx]
-    place = jnp.stack(place + [lax.axis_index("zh"), slices]).astype(jnp.int32)
-
-    last, start_out = call(
-        last_kernel,
-        [(planes, rows, cols), (REACH, rows, cols)],
-        [place],
-        u_old, u_init,
-        scratch=[pltpu.SemaphoreType.DMA((2,))],
-        in_hbm=True,
-    )
+    place = [position, core, lax.axis_index("za"), lax.axis_index("x"), kx]
+    place = jnp.stack(place + [lax.axis_index("zh"), slices, lax.axis_index("zb")])
+    place = place.astype(jnp.int32)
+
+    last = u_old[0, 4]
+    start_out = call(edge_kernel, (REACH, rows, cols), [place], last, u_init, flops=10**11)
 
     def far_block(s):
         return (s + 1) % blocks if s % 2 else (s - 1) % blocks
@@ -498,19 +500,23 @@
         scratch=[pltpu.VMEM((2, coarse, rows, cols), jnp.float32)],
     )
     columns = lax.all_to_all(send, SPACE, 0, 0, tiled=True)
-    packed = (lax.axis_size("zl"), depth_c // 2, 2 * cols_c)
+    packed = (depth_c // 2, 2 * cols_c)
     lifted, offset, copies = call(
         spectrum_kernel,
-        [(depth_c, 2 * cols_c), (depth_c, 2 * cols_c), packed],
+        [(depth_c, 2 * cols_c), (depth_c, 2 * cols_c), (4, *packed)],
         [place, shift_x],
         columns, forward_z, denom,
     )
-    gathered = lax.all_to_all(copies, "zl", 0, 0, tiled=True)
+    gathered = lax.all_to_all(copies, "za", 0, 0, tiled=True)
+    own_total, own_prefix = call(
+        group_kernel, [packed, packed], [place, shift_x], gathered, denom
+    )
+    other_total = lax.ppermute(own_total, "zb", [(0, 1), (1, 0)])
     back = call(
         scan_kernel,
         (4 * rows_c, coarse, 4 * cols_c),
         [place, shift_x],
-        gathered, lifted, offset, denom, inverse_z,
+        own_total, other_total, own_prefix, lifted, offset, denom, inverse_z,
     )
     returned = lax.all_to_all(back, ("x", "y", "c"), 0, 0, tiled=True)
     out = call(
@@ -520,7 +526,7 @@
 
 
 def solution(mesh):
-    finer = Mesh(mesh.devices.reshape(4, 8, 4, 2, 2), TM + SPACE)
+    finer = Mesh(mesh.devices.reshape(4, 2, 4, 4, 2, 2), TM + SPACE)
     in_specs = (P(TM, None, SPACE, None, None), P(SPACE, None, None))
     out_specs = P(TM, None, SPACE, None, None)
     return jax.shard_map(

time: 111 us -> 106 us (0.955)
  blocking collectives: 65.1 us -> 48.4 us
  starting transfers between devices: 26 us -> 34.8 us
  waiting for transfers between devices: 8.81 us -> 10.7 us
    all_to_all x1, blocking collectives: 22.3 us -> 8.94 us  [shards(): gathered = lax.all_to_all(copies, 'za', 0, 0, tiled=True)]
    ppermute x0 -> x1, starting transfers between devices: none -> 8.43 us  [shards(): other_total = lax.ppermute(own_total, 'zb', [(0, 1), (1, 0)])]
    all_to_all x1, blocking collectives: 24 us -> 21.4 us  [shards(): columns = lax.all_to_all(send, SPACE, 0, 0, tiled=True)]
    ppermute x1, starting transfers between devices: 2.65 us -> 5.02 us  [shards(): previous = lax.ppermute(last, TM, [(i, i + 1) for i in range(slices - 1)])]
    ppermute x1, starting transfers between devices: 16.4 us -> 14.3 us  [shards(): start_far = lax.ppermute(start_out, TM + SPACE, across)]
    squeeze x0 -> x1, local copies, waits for them, and re-layouts: none -> 1.6 us  [shards(): last = u_old[0, 4]]
    ppermute x0 -> x1, waiting for transfers between devices: none -> 1.29 us  [shards(): other_total = lax.ppermute(own_total, 'zb', [(0, 1), (1, 0)])]
    pallas_call x8 -> x9, Pallas kernels: 9.67 us -> 9.71 us  [call(): pl.pallas_call(kernel, out_shape=shapes[0] if single else shapes, in_spec...]
  transfers between devices with their start and end apart: 4 -> 5, of which waited for: 1 -> 2; matrix products, arithmetic and copies ran while one was open for 0% -> 0% of each run, Pallas kernels for 1% -> 3%
where the time goes in v4:
time: 106 us
  blocking collectives  48.4 us (46%)
  starting transfers between devices  34.8 us (33%)
  waiting for transfers between devices  10.7 us (10%)
  Pallas kernels  9.71 us (9%)
  local copies, waits for them, and re-layouts  1.75 us (2%)
    all_to_all x1, blocking collectives, shards(): columns = lax.all_to_all(send, SPACE, 0, 0, tiled=True)  21.4 us
    all_to_all x1, blocking collectives, shards(): returned = lax.all_to_all(back, ('x', 'y', 'c'), 0, 0, tiled=True)  18 us
    ppermute x1, starting transfers between devices, shards(): start_far = lax.ppermute(start_out, TM + SPACE, across)  14.3 us
    pallas_call x9, Pallas kernels, call(): pl.pallas_call(kernel, out_shape=shapes[0] if single else shapes, in_spec...  9.71 us
    ppermute x1, waiting for transfers between devices, shards(): lax.ppermute(own_far, SPACE, [(s, far_block(s)) for s in range(blocks)])  9.42 us
    all_to_all x1, blocking collectives, shards(): gathered = lax.all_to_all(copies, 'za', 0, 0, tiled=True)  8.94 us
    ppermute x1, starting transfers between devices, shards(): other_total = lax.ppermute(own_total, 'zb', [(0, 1), (1, 0)])  8.43 us
    ppermute x1, starting transfers between devices, shards(): previous = lax.ppermute(last, TM, [(i, i + 1) for i in range(slices - 1)])  5.02 us
  transfers between devices with their start and end apart: 5, of which 2 were waited for; matrix products, arithmetic and copies ran while one was open for 0% of the time, Pallas kernels for 3%

profile of v4, /device:TPU:1, one launch (start us, length us, event | category | flops | bytes accessed | tf_op | source)
XLA Modules:
  0.0 105.5 jit_solution(13921906073491168136)
XLA Ops:
  0.0 1.6 %slice_bitcast_fusion.last = f32[16,16,128]{2,1,0:T(8,128)} fusion(f32[1,5,16,16,128]{4,3,2,1,0:T(8,128)} %param.11), kind=kLoop, calls=%fused_computation | loop fusion | bytes 262144 | tf_op jit(solution)/shard_map/squeeze | solution.py:463
  1.6 5.0 %collective-permute-start = (f32[16,16,128]{2,1,0:T(8,128)}, f32[16,16,128]{2,1,0:T(8,128)}, u32[]{:S(2)}, u32[]{:S(2)}) collective-permute-start(f32[16,16,128]{2,1,0:T(8,128)} %slice_bitcast_fusion.last), channel_id=1, source_target_pairs={{0,16},{16,32},{32,48},{48,64},{64,80},{80,96},{96,112},{112,128},... | collective-permute-start | bytes 393224 | tf_op jit(solution)/shard_map/ppermute | solution.py:475
  6.6 0.1 stack.31.place
  6.7 1.0 shard_map.111
  7.7 14.3 %collective-permute-start.2 = (f32[4,16,128]{2,1,0:T(8,128)S(1)}, f32[4,16,128]{2,1,0:T(8,128)S(1)}, u32[]{:S(2)}, u32[]{:S(2)}) collective-permute-start(f32[4,16,128]{2,1,0:T(8,128)S(1)} %shard_map.111), channel_id=1, source_target_pairs={{0,31},{1,18},{2,17},{3,20},{4,19},{5,22},{6,21},{7,24},{8,23},{9,... | collective-permute-start | bytes 98312 | tf_op jit(solution)/shard_map/ppermute | solution.py:474
  22.0 1.0 shard_map.109
  23.1 3.0 %collective-permute-start.3 = (f32[10,16,128]{2,1,0:T(8,128)S(1)}, f32[10,16,128]{2,1,0:T(8,128)S(1)}, u32[]{:S(2)}, u32[]{:S(2)}) collective-permute-start(f32[10,16,128]{2,1,0:T(8,128)S(1)} %get-tuple-element.18.own_far), channel_id=1, source_target_pairs={{0,15},{1,2},{2,1},{3,4},{4,3},{5,6},{6,5},{7,8},{8,7},{9,10},{10,... | collective-permute-start | bytes 245768 | tf_op jit(solution)/shard_map/ppermute | solution.py:484
  26.1 0.9 shard_map.110
  27.0 0.0 copy-start.3
  27.1 0.0 copy-start.7
  27.1 0.0 copy-start.8
  27.1 4.0 %collective-permute-start.1 = (f32[14,16,128]{2,1,0:T(8,128)S(1)}, f32[14,16,128]{2,1,0:T(8,128)S(1)}, u32[]{:S(2)}, u32[]{:S(2)}) collective-permute-start(f32[14,16,128]{2,1,0:T(8,128)S(1)} %shard_map.110), channel_id=1, source_target_pairs={{0,1},{1,0},{2,3},{3,2},{4,5},{5,4},{6,7},{7,6},{8,9},{9,8},{10,11... | collective-permute-start | bytes 344072 | tf_op jit(solution)/shard_map/ppermute | solution.py:488
  31.2 9.4 %collective-permute-done.3.got_far = f32[10,16,128]{2,1,0:T(8,128)S(1)} collective-permute-done((f32[10,16,128]{2,1,0:T(8,128)S(1)}, f32[10,16,128]{2,1,0:T(8,128)S(1)}, u32[]{:S(2)}, u32[]{:S(2)}) %collective-permute-start.3) | collective-permute-done | bytes 81952 | tf_op jit(solution)/shard_map/ppermute | solution.py:484
  40.6 2.2 %shard_map.113 = (f32[5,24,16,128]{3,2,1,0:T(8,128)S(1)}, f32[16,16,128]{2,1,0:T(8,128)S(1)}, f32[64,256]{1,0:T(8,128)S(1)}) custom-call(s32[8]{0:T(128)S(1)} %stack.31.place, f32[16,16,128]{2,1,0:T(8,128)S(1)} %copy-done.1, f32[16,16,128]{2,1,0:T(8,128)} %collective-permute-done.previous, f32[14,16,128]{2,1,0:T(8,128)S(1)} %collective-permute-done.1.near, ...), custom_call_target="tpu_custom_call" | custom-call | bytes 1048576 | tf_op jit(solution)/shard_map/pallas_call | solution.py:435
  42.8 0.0 copy-start
  42.9 21.4 %all_to_all.15.got = f32[16,16,128]{2,1,0:T(8,128)S(1)} all-to-all(f32[16,16,128]{2,1,0:T(8,128)S(1)} %get-tuple-element.20), channel_id=1, replica_groups=mesh['x'=4,'zb'=2,'za'=4,'y'=4,'zh'=2,'c'=2] {'y','zh','c'}, dimensions={0} | all-to-all | bytes 262144 | tf_op jit(solution)/shard_map/all_to_all | solution.py:502
  64.3 0.9 shard_map.114
  65.2 8.9 %all_to_all.16.offsets = f32[4,64,128]{2,1,0:T(8,128)S(1)} all-to-all(f32[4,64,128]{2,1,0:T(8,128)S(1)} %get-tuple-element.21), channel_id=1, replica_groups=mesh['x'=4,'zb'=2,'za'=4,'y'=4,'zh'=2,'c'=2] {'za'}, dimensions={0} | all-to-all | bytes 262144 | tf_op jit(solution)/shard_map/all_to_all | solution.py:510
  74.1 0.6 shard_map.115
  74.7 8.4 %collective-permute-start.4 = (f32[64,128]{1,0:T(8,128)S(1)}, f32[64,128]{1,0:T(8,128)S(1)}, u32[]{:S(2)}, u32[]{:S(2)}) collective-permute-start(f32[64,128]{1,0:T(8,128)S(1)} %get-tuple-element.22.own_total), channel_id=1, source_target_pairs={{0,64},{64,0},{1,65},{65,1},{2,66},{66,2},{3,67},{67,3},{4,68},{68... | collective-permute-start | bytes 98312 | tf_op jit(solution)/shard_map/ppermute | solution.py:514
  83.1 1.3 %collective-permute-done.4.other_total = f32[64,128]{1,0:T(8,128)S(1)} collective-permute-done((f32[64,128]{1,0:T(8,128)S(1)}, f32[64,128]{1,0:T(8,128)S(1)}, u32[]{:S(2)}, u32[]{:S(2)}) %collective-permute-start.4) | collective-permute-done | bytes 32800 | tf_op jit(solution)/shard_map/ppermute | solution.py:514
  84.4 1.0 shard_map.116
  85.5 18.0 %all_to_all.17.got = f32[32,8,256]{2,1,0:T(8,128)S(1)} all-to-all(f32[32,8,256]{2,1,0:T(8,128)S(1)} %shard_map.116), channel_id=1, replica_groups=mesh['x'=4,'zb'=2,'za'=4,'y'=4,'zh'=2,'c'=2] {'x','y','c'}, dimensions={0} | all-to-all | bytes 524288 | tf_op jit(solution)/shard_map/all_to_all | solution.py:521
  103.5 2.0 %shard_map.117 = f32[5,16,16,128]{3,2,1,0:T(8,128)} custom-call(s32[8]{0:T(128)S(1)} %stack.31.place, f32[5,24,16,128]{3,2,1,0:T(8,128)S(1)} %get-tuple-element.19.w, f32[32,8,256]{2,1,0:T(8,128)S(1)} %all_to_all.17.got, f32[64,256]{1,0:T(8,128)S(1)} %get-tuple-element.26.hats, f32[128,64]{1,0:T(8,128)S(1)} %copy-done.5, f32[128,256]{1,0:T(8,128)S(1)} %copy-done.2), custom_call_target="tpu_custom_call" | custom-call | bytes 1048576 | tf_op jit(solution)/shard_map/pallas_call | solution.py:435
  (22 shorter events, 0.1 us)
Async XLA Ops:
  0.0 6.7 %copy-start.1 = (f32[16,16,128]{2,1,0:T(8,128)S(1)}, f32[16,16,128]{2,1,0:T(8,128)}, u32[]{:S(2)}) copy-start(f32[16,16,128]{2,1,0:T(8,128)} %first.5) | copy-start | bytes 393220
  1.6 24.5 %collective-permute-start = (f32[16,16,128]{2,1,0:T(8,128)}, f32[16,16,128]{2,1,0:T(8,128)}, u32[]{:S(2)}, u32[]{:S(2)}) collective-permute-start(f32[16,16,128]{2,1,0:T(8,128)} %slice_bitcast_fusion.last), channel_id=1, source_target_pairs={{0,16},{16,32},{32,48},{48,64},{64,80},{80,96},{96,112},{112,128},... | collective-permute-start | bytes 393224 | tf_op jit(solution)/shard_map/ppermute | solution.py:475
  6.7 15.3 %copy-start.9 = (f32[1,5,16,16,128]{4,3,2,1,0:T(8,128)S(1)}, f32[1,5,16,16,128]{4,3,2,1,0:T(8,128)}, u32[]{:S(2)}) copy-start(f32[1,5,16,16,128]{4,3,2,1,0:T(8,128)} %param.11) | copy-start | bytes 1966084
  7.7 23.4 %collective-permute-start.2 = (f32[4,16,128]{2,1,0:T(8,128)S(1)}, f32[4,16,128]{2,1,0:T(8,128)S(1)}, u32[]{:S(2)}, u32[]{:S(2)}) collective-permute-start(f32[4,16,128]{2,1,0:T(8,128)S(1)} %shard_map.111), channel_id=1, source_target_pairs={{0,31},{1,18},{2,17},{3,20},{4,19},{5,22},{6,21},{7,24},{8,23},{9,... | collective-permute-start | bytes 98312 | tf_op jit(solution)/shard_map/ppermute | solution.py:474
  23.1 17.5 %collective-permute-start.3 = (f32[10,16,128]{2,1,0:T(8,128)S(1)}, f32[10,16,128]{2,1,0:T(8,128)S(1)}, u32[]{:S(2)}, u32[]{:S(2)}) collective-permute-start(f32[10,16,128]{2,1,0:T(8,128)S(1)} %get-tuple-element.18.own_far), channel_id=1, source_target_pairs={{0,15},{1,2},{2,1},{3,4},{4,3},{5,6},{6,5},{7,8},{8,7},{9,10},{10,... | collective-permute-start | bytes 245768 | tf_op jit(solution)/shard_map/ppermute | solution.py:484
  27.0 13.5 %copy-start.3 = (f32[256,128]{1,0:T(8,128)S(1)}, f32[256,128]{1,0:T(8,128)}, u32[]{:S(2)}) copy-start(f32[256,128]{1,0:T(8,128)} %constant.49.clone.down_y) | copy-start | bytes 393220
  27.1 13.5 %copy-start.7 = (f32[64,128]{1,0:T(8,128)S(1)}, f32[64,128]{1,0:T(8,128)}, u32[]{:S(2)}) copy-start(f32[64,128]{1,0:T(8,128)} %constant.51.clone.stencil) | copy-start | bytes 98308
  27.1 13.5 %copy-start.8 = (f32[64,128]{1,0:T(8,128)S(1)}, f32[64,128]{1,0:T(8,128)}, u32[]{:S(2)}) copy-start(f32[64,128]{1,0:T(8,128)} %constant.50.clone.down_x) | copy-start | bytes 98308
  27.1 13.5 %collective-permute-start.1 = (f32[14,16,128]{2,1,0:T(8,128)S(1)}, f32[14,16,128]{2,1,0:T(8,128)S(1)}, u32[]{:S(2)}, u32[]{:S(2)}) collective-permute-start(f32[14,16,128]{2,1,0:T(8,128)S(1)} %shard_map.110), channel_id=1, source_target_pairs={{0,1},{1,0},{2,3},{3,2},{4,5},{5,4},{6,7},{7,6},{8,9},{9,8},{10,11... | collective-permute-start | bytes 344072 | tf_op jit(solution)/shard_map/ppermute | solution.py:488
  42.8 21.4 %copy-start = (f32[128,128]{1,0:T(8,128)S(1)}, f32[128,128]{1,0:T(8,128)}, u32[]{:S(2)}) copy-start(f32[128,128]{1,0:T(8,128)} %constant.54.clone.denom) | copy-start | bytes 196612
  42.9 21.4 %copy-start.4 = (f32[128,256]{1,0:T(8,128)S(1)}, f32[128,256]{1,0:T(8,128)}, u32[]{:S(2)}) copy-start(f32[128,256]{1,0:T(8,128)} %constant.52.clone.table) | copy-start | bytes 393220
  42.9 21.4 %copy-start.10 = (f32[8]{0:T(128)S(1)}, f32[8]{0:T(128)}, u32[]{:S(2)}) copy-start(f32[8]{0:T(128)} %constant.55.clone.shift_x) | copy-start | bytes 100
  74.1 10.3 %copy-start.6 = (f32[2,64,128]{2,1,0:T(8,128)S(1)}, f32[2,64,128]{2,1,0:T(8,128)}, u32[]{:S(2)}) copy-start(f32[2,64,128]{2,1,0:T(8,128)} %constant.53.clone.inverse_z) | copy-start | bytes 196612
  74.7 9.7 %collective-permute-start.4 = (f32[64,128]{1,0:T(8,128)S(1)}, f32[64,128]{1,0:T(8,128)S(1)}, u32[]{:S(2)}, u32[]{:S(2)}) collective-permute-start(f32[64,128]{1,0:T(8,128)S(1)} %get-tuple-element.22.own_total), channel_id=1, source_target_pairs={{0,64},{64,0},{1,65},{65,1},{2,66},{66,2},{3,67},{67,3},{4,68},{68... | collective-permute-start | bytes 98312 | tf_op jit(solution)/shard_map/ppermute | solution.py:514
  85.5 18.0 %copy-start.2 = (f32[128,256]{1,0:T(8,128)S(1)}, f32[128,256]{1,0:T(8,128)}, u32[]{:S(2)}) copy-start(f32[128,256]{1,0:T(8,128)} %constant.57.clone.up_y) | copy-start | bytes 393220
  85.5 18.0 %copy-start.5 = (f32[128,64]{1,0:T(8,128)S(1)}, f32[128,64]{1,0:T(8,128)}, u32[]{:S(2)}) copy-start(f32[128,64]{1,0:T(8,128)} %constant.56.clone.up_x) | copy-start | bytes 98308

commit v5 on v4

--- a/solution.py
+++ b/solution.py
@@ -147,9 +147,21 @@
     return diffusion * near - f * ((6.0 * diffusion - reaction) + reaction * (f * f))
 
 
-def old_kernel(place, u, g, near, far):
+def old_kernel(place, u, first, g, near, far, edge_near, edge_far):
     planes = u.shape[1]
-    core = place[1]
+    position, core, slices = place[0], place[1], place[6]
+    far_edge = pl.ds(core * (planes - REACH), REACH)
+    near_edge = pl.ds((1 - core) * (planes - REACH), REACH)
+
+    @pl.when(position == slices - 1)
+    def _():
+        edge_far[...] = first[far_edge]
+        edge_near[...] = first[near_edge]
+
+    @pl.when(position != slices - 1)
+    def _():
+        edge_far[...] = u[4, far_edge]
+        edge_near[...] = u[4, near_edge]
 
     for p in range(planes):
         total = [None] * 4
@@ -187,42 +199,15 @@
         packed(far, top)
 
 
-def edge_kernel(place, last, first, start_out):
-    position, core, slices = place[0], place[1], place[6]
-    edge = pl.ds(core * (first.shape[0] - REACH), REACH)
-
-    @pl.when(position == slices - 1)
-    def _():
-        start_out[...] = first[edge]
-
-    @pl.when(position != slices - 1)
-    def _():
-        start_out[...] = last[edge]
-
-
-def relay_kernel(got, out):
-    out[...] = got[...]
-
-
-def near_kernel(place, first, previous, own_near, out):
-    position, core = place[0], place[1]
-    edge = pl.ds((1 - core) * (first.shape[0] - REACH), REACH)
-    out[:PACK] = own_near[...]
-
-    @pl.when(position == 0)
-    def _():
-        out[PACK:] = first[edge]
-
-    @pl.when(position != 0)
-    def _():
-        out[PACK:] = previous[edge]
+def relay_kernel(halo, edge, halo_out, edge_out):
+    halo_out[...] = halo[...]
+    edge_out[...] = edge[...]
 
 
 def sweep_kernel(
-    place, first, previous, near, start_far, g, own_near, own_far, got_far,
+    place, first, previous, start_near, start_far, g, own_near, own_far, got_near, got_far,
     down_y, down_x, stencil, w, send, hats, quad,
 ):
-    got_near, start_near = near.at[:PACK], near.at[PACK:]
     planes = first.shape[0]
     coarse = planes // 2
     position, core = place[0], place[1]
@@ -460,32 +445,31 @@
     place = jnp.stack(place + [lax.axis_index("zh"), slices, lax.axis_index("zb")])
     place = place.astype(jnp.int32)
 
-    last = u_old[0, 4]
-    start_out = call(edge_kernel, (REACH, rows, cols), [place], last, u_init, flops=10**11)
+    halo, edge = (PACK, rows, cols), (REACH, rows, cols)
+    g, own_near, own_far, edge_near, edge_far = call(
+        old_kernel,
+        [(4, planes, rows, cols), halo, halo, edge, edge],
+        [place],
+        u_old[0], u_init,
+        flops=10**11,
+    )
 
     def far_block(s):
         return (s + 1) % blocks if s % 2 else (s - 1) % blocks
 
-    across = [
-        (n * blocks + s, (n + 1) % slices * blocks + far_block(s))
-        for n in range(slices)
-        for s in range(blocks)
-    ]
-    start_far = lax.ppermute(start_out, TM + SPACE, across)
-    previous = lax.ppermute(last, TM, [(i, i + 1) for i in range(slices - 1)])
-    g, own_near, own_far = call(
-        old_kernel,
-        [(4, planes, rows, cols), (PACK, rows, cols), (PACK, rows, cols)],
-        [place],
-        u_old[0],
-        flops=10**11,
-    )
-    start_far = call(relay_kernel, start_far.shape, [], start_far, flops=10**11)
+    def from_previous(partner):
+        return [
+            (n * blocks + s, (n + 1) % slices * blocks + partner(s))
+            for n in range(slices)
+            for s in range(blocks)
+        ]
+
     got_far = lax.ppermute(own_far, SPACE, [(s, far_block(s)) for s in range(blocks)])
-    near_out = call(
-        near_kernel, (PACK + REACH, rows, cols), [place], u_init, previous, own_near
-    )
-    near = lax.ppermute(near_out, "c", [(0, 1), (1, 0)])
+    start_far = lax.ppermute(edge_far, TM + SPACE, from_previous(far_block))
+    got_far, start_far = call(relay_kernel, [halo, edge], [], got_far, start_far, flops=10**11)
+    previous = lax.ppermute(u_old[0, 4], TM, [(i, i + 1) for i in range(slices - 1)])
+    start_near = lax.ppermute(edge_near, TM + SPACE, from_previous(lambda s: s ^ 1))
+    got_near = lax.ppermute(own_near, "c", [(0, 1), (1, 0)])
 
     w, send, hats = call(
         sweep_kernel,
@@ -495,7 +479,7 @@
             (rows_c * coarse, 4 * cols_c),
         ],
         [place],
-        u_init, previous, near, start_far, g, own_near, own_far, got_far,
+        u_init, previous, start_near, start_far, g, own_near, own_far, got_near, got_far,
         down_y, down_x, stencil,
         scratch=[pltpu.VMEM((2, coarse, rows, cols), jnp.float32)],
     )

time: 106 us -> 108 us (1.019)
  blocking collectives: 48.4 us -> 53.9 us
  starting transfers between devices: 34.8 us -> 32.4 us
  Pallas kernels: 9.71 us -> 7.44 us
    all_to_all x1, blocking collectives: 21.4 us -> 30.2 us  [shards(): columns = lax.all_to_all(send, SPACE, 0, 0, tiled=True)]
    ppermute x1, starting transfers between devices: 8.43 us -> 3.86 us  [shards(): other_total = lax.ppermute(own_total, 'zb', [(0, 1), (1, 0)])]
    ppermute x1, waiting for transfers between devices: 1.29 us -> 4.7 us  [shards(): other_total = lax.ppermute(own_total, 'zb', [(0, 1), (1, 0)])]
    ppermute x3 -> x4, starting transfers between devices: 23.4 us -> 26.2 us  [the longest x1 16.4 us: shards(): start_far = lax.ppermute(edge_far, TM + SPACE, from_previous(far_block))]
    ppermute x1, waiting for transfers between devices: 9.42 us -> 6.79 us  [shards(): lax.ppermute(own_far, SPACE, [(s, far_block(s)) for s in range(blocks)])]
    pallas_call x9 -> x7, Pallas kernels: 9.71 us -> 7.44 us  [call(): pl.pallas_call(kernel, out_shape=shapes[0] if single else shapes, in_spec...]
    unnamed x22 -> x24, local copies, waits for them, and re-layouts: 0.07 us -> 2.06 us
    all_to_all x1, blocking collectives: 8.94 us -> 7.17 us  [shards(): gathered = lax.all_to_all(copies, 'za', 0, 0, tiled=True)]
  transfers between devices with their start and end apart: 5 -> 6, of which waited for: 2 -> 3; matrix products, arithmetic and copies ran while one was open for 0% -> 0% of each run, Pallas kernels for 3% -> 0%
where the time goes in v5:
time: 108 us
  blocking collectives  53.9 us (50%)
  starting transfers between devices  32.4 us (30%)
  waiting for transfers between devices  11.7 us (11%)
  Pallas kernels  7.44 us (7%)
  local copies, waits for them, and re-layouts  2.15 us (2%)
    all_to_all x1, blocking collectives, shards(): columns = lax.all_to_all(send, SPACE, 0, 0, tiled=True)  30.2 us
    all_to_all x1, blocking collectives, shards(): returned = lax.all_to_all(back, ('x', 'y', 'c'), 0, 0, tiled=True)  16.6 us
    ppermute x1, starting transfers between devices, shards(): start_far = lax.ppermute(edge_far, TM + SPACE, from_previous(far_block))  16.4 us
    pallas_call x7, Pallas kernels, call(): pl.pallas_call(kernel, out_shape=shapes[0] if single else shapes, in_spec...  7.44 us
    all_to_all x1, blocking collectives, shards(): gathered = lax.all_to_all(copies, 'za', 0, 0, tiled=True)  7.17 us
    ppermute x1, waiting for transfers between devices, shards(): lax.ppermute(own_far, SPACE, [(s, far_block(s)) for s in range(blocks)])  6.79 us
    ppermute x1, starting transfers between devices, shards(): lax.ppermute(edge_near, TM + SPACE, from_previous(lambda s: s ^ 1))  5.09 us
    ppermute x1, waiting for transfers between devices, shards(): other_total = lax.ppermute(own_total, 'zb', [(0, 1), (1, 0)])  4.7 us
  transfers between devices with their start and end apart: 6, of which 3 were waited for; matrix products, arithmetic and copies ran while one was open for 0% of the time, Pallas kernels for 0%

profile of v5, /device:TPU:1, one launch (start us, length us, event | category | flops | bytes accessed | tf_op | source)
XLA Modules:
  0.0 107.9 jit_solution(5113978944951143752)
XLA Ops:
  0.0 0.1 stack.31.place
  0.1 0.9 copy-done.1
  1.0 1.1 %copy-done.10 = f32[1,5,16,16,128]{4,3,2,1,0:T(8,128)S(1)} copy-done((f32[1,5,16,16,128]{4,3,2,1,0:T(8,128)S(1)}, f32[1,5,16,16,128]{4,3,2,1,0:T(8,128)}, u32[]{:S(2)}) %copy-start.10) | copy-done | bytes 655384
  2.1 1.0 shard_map.109
  3.1 16.4 %collective-permute-start.3 = (f32[4,16,128]{2,1,0:T(8,128)S(1)}, f32[4,16,128]{2,1,0:T(8,128)S(1)}, u32[]{:S(2)}, u32[]{:S(2)}) collective-permute-start(f32[4,16,128]{2,1,0:T(8,128)S(1)} %get-tuple-element.22), channel_id=1, source_target_pairs={{0,31},{1,18},{2,17},{3,20},{4,19},{5,22},{6,21},{7,24},{8,23},{9,... | collective-permute-start | bytes 98312 | tf_op jit(solution)/shard_map/ppermute | solution.py:468
  19.5 2.4 %collective-permute-start.2 = (f32[10,16,128]{2,1,0:T(8,128)S(1)}, f32[10,16,128]{2,1,0:T(8,128)S(1)}, u32[]{:S(2)}, u32[]{:S(2)}) collective-permute-start(f32[10,16,128]{2,1,0:T(8,128)S(1)} %get-tuple-element.21.own_far), channel_id=1, source_target_pairs={{0,15},{1,2},{2,1},{3,4},{4,3},{5,6},{6,5},{7,8},{8,7},{9,10},{10,... | collective-permute-start | bytes 245768 | tf_op jit(solution)/shard_map/ppermute | solution.py:467
  21.9 2.6 %collective-permute-start = (f32[16,16,128]{2,1,0:T(8,128)S(1)}, f32[16,16,128]{2,1,0:T(8,128)S(1)}, u32[]{:S(2)}, u32[]{:S(2)}) collective-permute-start(f32[16,16,128]{2,1,0:T(8,128)S(1)} %slice_bitcast_fusion), channel_id=1, source_target_pairs={{0,16},{16,32},{32,48},{48,64},{64,80},{80,96},{96,112},{112,128},... | collective-permute-start | bytes 393224 | tf_op jit(solution)/shard_map/ppermute | solution.py:470
  24.6 5.1 %collective-permute-start.1 = (f32[4,16,128]{2,1,0:T(8,128)S(1)}, f32[4,16,128]{2,1,0:T(8,128)S(1)}, u32[]{:S(2)}, u32[]{:S(2)}) collective-permute-start(f32[4,16,128]{2,1,0:T(8,128)S(1)} %get-tuple-element.20), channel_id=1, source_target_pairs={{0,17},{1,16},{2,19},{3,18},{4,21},{5,20},{6,23},{7,22},{8,25},{9,... | collective-permute-start | bytes 98312 | tf_op jit(solution)/shard_map/ppermute | solution.py:471
  29.7 0.0 copy-start.4
  29.7 0.0 copy-start.8
  29.7 0.0 copy-start.9
  29.7 2.1 %collective-permute-start.4 = (f32[10,16,128]{2,1,0:T(8,128)S(1)}, f32[10,16,128]{2,1,0:T(8,128)S(1)}, u32[]{:S(2)}, u32[]{:S(2)}) collective-permute-start(f32[10,16,128]{2,1,0:T(8,128)S(1)} %get-tuple-element.25.own_near), channel_id=1, source_target_pairs={{0,1},{1,0},{2,3},{3,2},{4,5},{5,4},{6,7},{7,6},{8,9},{9,8},{10,11... | collective-permute-start | bytes 245768 | tf_op jit(solution)/shard_map/ppermute | solution.py:472
  31.8 6.8 %collective-permute-done.2.halo = f32[10,16,128]{2,1,0:T(8,128)S(1)} collective-permute-done((f32[10,16,128]{2,1,0:T(8,128)S(1)}, f32[10,16,128]{2,1,0:T(8,128)S(1)}, u32[]{:S(2)}, u32[]{:S(2)}) %collective-permute-start.2) | collective-permute-done | bytes 81952 | tf_op jit(solution)/shard_map/ppermute | solution.py:467
  38.6 0.2 collective-permute-done.1.start_near
  38.9 1.9 %shard_map.111 = (f32[5,24,16,128]{3,2,1,0:T(8,128)S(1)}, f32[16,16,128]{2,1,0:T(8,128)S(1)}, f32[64,256]{1,0:T(8,128)S(1)}) custom-call(s32[8]{0:T(128)S(1)} %stack.31.place, f32[16,16,128]{2,1,0:T(8,128)S(1)} %copy-done.2, f32[16,16,128]{2,1,0:T(8,128)S(1)} %collective-permute-done.previous, f32[4,16,128]{2,1,0:T(8,128)S(1)} %collective-permute-done.1.start_near, ...), custom_call_target="tpu_custom_call" | custom-call | bytes 1048576 | tf_op jit(solution)/shard_map/pallas_call | solution.py:420
  40.8 30.2 %all_to_all.15.got = f32[16,16,128]{2,1,0:T(8,128)S(1)} all-to-all(f32[16,16,128]{2,1,0:T(8,128)S(1)} %get-tuple-element.28), channel_id=1, replica_groups=mesh['x'=4,'zb'=2,'za'=4,'y'=4,'zh'=2,'c'=2] {'y','zh','c'}, dimensions={0} | all-to-all | bytes 262144 | tf_op jit(solution)/shard_map/all_to_all | solution.py:486
  71.0 0.9 shard_map.112
  71.9 7.2 %all_to_all.16.offsets = f32[4,64,128]{2,1,0:T(8,128)S(1)} all-to-all(f32[4,64,128]{2,1,0:T(8,128)S(1)} %get-tuple-element.29), channel_id=1, replica_groups=mesh['x'=4,'zb'=2,'za'=4,'y'=4,'zh'=2,'c'=2] {'za'}, dimensions={0} | all-to-all | bytes 262144 | tf_op jit(solution)/shard_map/all_to_all | solution.py:494
  79.0 0.6 shard_map.113
  79.6 3.9 %collective-permute-start.5 = (f32[64,128]{1,0:T(8,128)S(1)}, f32[64,128]{1,0:T(8,128)S(1)}, u32[]{:S(2)}, u32[]{:S(2)}) collective-permute-start(f32[64,128]{1,0:T(8,128)S(1)} %get-tuple-element.30.own_total), channel_id=1, source_target_pairs={{0,64},{64,0},{1,65},{65,1},{2,66},{66,2},{3,67},{67,3},{4,68},{68... | collective-permute-start | bytes 98312 | tf_op jit(solution)/shard_map/ppermute | solution.py:498
  83.5 4.7 %collective-permute-done.5.other_total = f32[64,128]{1,0:T(8,128)S(1)} collective-permute-done((f32[64,128]{1,0:T(8,128)S(1)}, f32[64,128]{1,0:T(8,128)S(1)}, u32[]{:S(2)}, u32[]{:S(2)}) %collective-permute-start.5) | collective-permute-done | bytes 32800 | tf_op jit(solution)/shard_map/ppermute | solution.py:498
  88.2 1.0 shard_map.114
  89.3 16.6 %all_to_all.17.got = f32[32,8,256]{2,1,0:T(8,128)S(1)} all-to-all(f32[32,8,256]{2,1,0:T(8,128)S(1)} %shard_map.114), channel_id=1, replica_groups=mesh['x'=4,'zb'=2,'za'=4,'y'=4,'zh'=2,'c'=2] {'x','y','c'}, dimensions={0} | all-to-all | bytes 524288 | tf_op jit(solution)/shard_map/all_to_all | solution.py:505
  105.9 2.0 %shard_map.115 = f32[5,16,16,128]{3,2,1,0:T(8,128)} custom-call(s32[8]{0:T(128)S(1)} %stack.31.place, f32[5,24,16,128]{3,2,1,0:T(8,128)S(1)} %get-tuple-element.27.w, f32[32,8,256]{2,1,0:T(8,128)S(1)} %all_to_all.17.got, f32[64,256]{1,0:T(8,128)S(1)} %get-tuple-element.34.hats, f32[128,64]{1,0:T(8,128)S(1)} %copy-done.6, f32[128,256]{1,0:T(8,128)S(1)} %copy-done.3), custom_call_target="tpu_custom_call" | custom-call | bytes 1048576 | tf_op jit(solution)/shard_map/pallas_call | solution.py:420
  (24 shorter events, 0.1 us)
Async XLA Ops:
  0.1 0.9 copy-start.1
  1.0 1.1 %copy-start.10 = (f32[1,5,16,16,128]{4,3,2,1,0:T(8,128)S(1)}, f32[1,5,16,16,128]{4,3,2,1,0:T(8,128)}, u32[]{:S(2)}) copy-start(f32[1,5,16,16,128]{4,3,2,1,0:T(8,128)} %param.11) | copy-start | bytes 1966084
  3.1 28.7 %collective-permute-start.3 = (f32[4,16,128]{2,1,0:T(8,128)S(1)}, f32[4,16,128]{2,1,0:T(8,128)S(1)}, u32[]{:S(2)}, u32[]{:S(2)}) collective-permute-start(f32[4,16,128]{2,1,0:T(8,128)S(1)} %get-tuple-element.22), channel_id=1, source_target_pairs={{0,31},{1,18},{2,17},{3,20},{4,19},{5,22},{6,21},{7,24},{8,23},{9,... | collective-permute-start | bytes 98312 | tf_op jit(solution)/shard_map/ppermute | solution.py:468
  19.5 19.1 %collective-permute-start.2 = (f32[10,16,128]{2,1,0:T(8,128)S(1)}, f32[10,16,128]{2,1,0:T(8,128)S(1)}, u32[]{:S(2)}, u32[]{:S(2)}) collective-permute-start(f32[10,16,128]{2,1,0:T(8,128)S(1)} %get-tuple-element.21.own_far), channel_id=1, source_target_pairs={{0,15},{1,2},{2,1},{3,4},{4,3},{5,6},{6,5},{7,8},{8,7},{9,10},{10,... | collective-permute-start | bytes 245768 | tf_op jit(solution)/shard_map/ppermute | solution.py:467
  21.9 16.9 %collective-permute-start = (f32[16,16,128]{2,1,0:T(8,128)S(1)}, f32[16,16,128]{2,1,0:T(8,128)S(1)}, u32[]{:S(2)}, u32[]{:S(2)}) collective-permute-start(f32[16,16,128]{2,1,0:T(8,128)S(1)} %slice_bitcast_fusion), channel_id=1, source_target_pairs={{0,16},{16,32},{32,48},{48,64},{64,80},{80,96},{96,112},{112,128},... | collective-permute-start | bytes 393224 | tf_op jit(solution)/shard_map/ppermute | solution.py:470
  24.6 14.2 %collective-permute-start.1 = (f32[4,16,128]{2,1,0:T(8,128)S(1)}, f32[4,16,128]{2,1,0:T(8,128)S(1)}, u32[]{:S(2)}, u32[]{:S(2)}) collective-permute-start(f32[4,16,128]{2,1,0:T(8,128)S(1)} %get-tuple-element.20), channel_id=1, source_target_pairs={{0,17},{1,16},{2,19},{3,18},{4,21},{5,20},{6,23},{7,22},{8,25},{9,... | collective-permute-start | bytes 98312 | tf_op jit(solution)/shard_map/ppermute | solution.py:471
  29.7 9.2 %copy-start.2 = (f32[16,16,128]{2,1,0:T(8,128)S(1)}, f32[16,16,128]{2,1,0:T(8,128)}, u32[]{:S(2)}) copy-start(f32[16,16,128]{2,1,0:T(8,128)} %first.3) | copy-start | bytes 393220
  29.7 9.1 %copy-start.4 = (f32[256,128]{1,0:T(8,128)S(1)}, f32[256,128]{1,0:T(8,128)}, u32[]{:S(2)}) copy-start(f32[256,128]{1,0:T(8,128)} %constant.49.clone.down_y) | copy-start | bytes 393220
  29.7 9.1 %copy-start.8 = (f32[64,128]{1,0:T(8,128)S(1)}, f32[64,128]{1,0:T(8,128)}, u32[]{:S(2)}) copy-start(f32[64,128]{1,0:T(8,128)} %constant.51.clone.stencil) | copy-start | bytes 98308
  29.7 9.1 %copy-start.9 = (f32[64,128]{1,0:T(8,128)S(1)}, f32[64,128]{1,0:T(8,128)}, u32[]{:S(2)}) copy-start(f32[64,128]{1,0:T(8,128)} %constant.50.clone.down_x) | copy-start | bytes 98308
  29.7 9.1 %collective-permute-start.4 = (f32[10,16,128]{2,1,0:T(8,128)S(1)}, f32[10,16,128]{2,1,0:T(8,128)S(1)}, u32[]{:S(2)}, u32[]{:S(2)}) collective-permute-start(f32[10,16,128]{2,1,0:T(8,128)S(1)} %get-tuple-element.25.own_near), channel_id=1, source_target_pairs={{0,1},{1,0},{2,3},{3,2},{4,5},{5,4},{6,7},{7,6},{8,9},{9,8},{10,11... | collective-permute-start | bytes 245768 | tf_op jit(solution)/shard_map/ppermute | solution.py:472
  40.7 30.2 %copy-start = (f32[128,128]{1,0:T(8,128)S(1)}, f32[128,128]{1,0:T(8,128)}, u32[]{:S(2)}) copy-start(f32[128,128]{1,0:T(8,128)} %constant.54.clone.denom) | copy-start | bytes 196612
  40.8 30.2 %copy-start.5 = (f32[128,256]{1,0:T(8,128)S(1)}, f32[128,256]{1,0:T(8,128)}, u32[]{:S(2)}) copy-start(f32[128,256]{1,0:T(8,128)} %constant.52.clone.table) | copy-start | bytes 393220
  40.8 30.2 %copy-start.11 = (f32[8]{0:T(128)S(1)}, f32[8]{0:T(128)}, u32[]{:S(2)}) copy-start(f32[8]{0:T(128)} %constant.55.clone.shift_x) | copy-start | bytes 100
  79.0 9.2 %copy-start.7 = (f32[2,64,128]{2,1,0:T(8,128)S(1)}, f32[2,64,128]{2,1,0:T(8,128)}, u32[]{:S(2)}) copy-start(f32[2,64,128]{2,1,0:T(8,128)} %constant.53.clone.inverse_z) | copy-start | bytes 196612
  79.6 8.6 %collective-permute-start.5 = (f32[64,128]{1,0:T(8,128)S(1)}, f32[64,128]{1,0:T(8,128)S(1)}, u32[]{:S(2)}, u32[]{:S(2)}) collective-permute-start(f32[64,128]{1,0:T(8,128)S(1)} %get-tuple-element.30.own_total), channel_id=1, source_target_pairs={{0,64},{64,0},{1,65},{65,1},{2,66},{66,2},{3,67},{67,3},{4,68},{68... | collective-permute-start | bytes 98312 | tf_op jit(solution)/shard_map/ppermute | solution.py:498
  89.2 16.6 %copy-start.3 = (f32[128,256]{1,0:T(8,128)S(1)}, f32[128,256]{1,0:T(8,128)}, u32[]{:S(2)}) copy-start(f32[128,256]{1,0:T(8,128)} %constant.57.clone.up_y) | copy-start | bytes 393220
  89.2 16.6 %copy-start.6 = (f32[128,64]{1,0:T(8,128)S(1)}, f32[128,64]{1,0:T(8,128)}, u32[]{:S(2)}) copy-start(f32[128,64]{1,0:T(8,128)} %constant.56.clone.up_x) | copy-start | bytes 98308

commit v6 on v4

--- a/solution.py
+++ b/solution.py
@@ -147,9 +147,18 @@
     return diffusion * near - f * ((6.0 * diffusion - reaction) + reaction * (f * f))
 
 
-def old_kernel(place, u, g, near, far):
+def old_kernel(place, u, first, g, near, far, edge_far):
     planes = u.shape[1]
-    core = place[1]
+    position, core, slices = place[0], place[1], place[6]
+    far_edge = pl.ds(core * (planes - REACH), REACH)
+
+    @pl.when(position == slices - 1)
+    def _():
+        edge_far[...] = first[far_edge]
+
+    @pl.when(position != slices - 1)
+    def _():
+        edge_far[...] = u[4, far_edge]
 
     for p in range(planes):
         total = [None] * 4
@@ -187,23 +196,6 @@
         packed(far, top)
 
 
-def edge_kernel(place, last, first, start_out):
-    position, core, slices = place[0], place[1], place[6]
-    edge = pl.ds(core * (first.shape[0] - REACH), REACH)
-
-    @pl.when(position == slices - 1)
-    def _():
-        start_out[...] = first[edge]
-
-    @pl.when(position != slices - 1)
-    def _():
-        start_out[...] = last[edge]
-
-
-def relay_kernel(got, out):
-    out[...] = got[...]
-
-
 def near_kernel(place, first, previous, own_near, out):
     position, core = place[0], place[1]
     edge = pl.ds((1 - core) * (first.shape[0] - REACH), REACH)
@@ -216,6 +208,10 @@
     @pl.when(position != 0)
     def _():
         out[PACK:] = previous[edge]
+
+
+def relay_kernel(halo, halo_out):
+    halo_out[...] = halo[...]
 
 
 def sweep_kernel(
@@ -460,8 +456,14 @@
     place = jnp.stack(place + [lax.axis_index("zh"), slices, lax.axis_index("zb")])
     place = place.astype(jnp.int32)
 
-    last = u_old[0, 4]
-    start_out = call(edge_kernel, (REACH, rows, cols), [place], last, u_init, flops=10**11)
+    halo, edge = (PACK, rows, cols), (REACH, rows, cols)
+    g, own_near, own_far, edge_far = call(
+        old_kernel,
+        [(4, planes, rows, cols), halo, halo, edge],
+        [place],
+        u_old[0], u_init,
+        flops=10**11,
+    )
 
     def far_block(s):
         return (s + 1) % blocks if s % 2 else (s - 1) % blocks
@@ -471,17 +473,11 @@
         for n in range(slices)
         for s in range(blocks)
     ]
-    start_far = lax.ppermute(start_out, TM + SPACE, across)
-    previous = lax.ppermute(last, TM, [(i, i + 1) for i in range(slices - 1)])
-    g, own_near, own_far = call(
-        old_kernel,
-        [(4, planes, rows, cols), (PACK, rows, cols), (PACK, rows, cols)],
-        [place],
-        u_old[0],
-        flops=10**11,
-    )
-    start_far = call(relay_kernel, start_far.shape, [], start_far, flops=10**11)
+
     got_far = lax.ppermute(own_far, SPACE, [(s, far_block(s)) for s in range(blocks)])
+    start_far = lax.ppermute(edge_far, TM + SPACE, across)
+    got_far = call(relay_kernel, halo, [], got_far, flops=10**11)
+    previous = lax.ppermute(u_old[0, 4], TM, [(i, i + 1) for i in range(slices - 1)])
     near_out = call(
         near_kernel, (PACK + REACH, rows, cols), [place], u_init, previous, own_near
     )

time: 106 us -> 108 us (1.019)
  blocking collectives: 48.4 us -> 58.6 us
  starting transfers between devices: 34.8 us -> 28.8 us
  Pallas kernels: 9.71 us -> 7.97 us
  waiting for transfers between devices: 10.7 us -> 9.47 us
    ppermute x2, starting transfers between devices: 19.3 us -> 6.3 us  [the longest x1 4.38 us: shards(): lax.ppermute(u_old[0, 4], TM, [(i, i + 1) for i in range(slices - 1)])]
    ppermute x1, starting transfers between devices: 3 us -> 15.4 us  [shards(): lax.ppermute(own_far, SPACE, [(s, far_block(s)) for s in range(blocks)])]
    ppermute x1, waiting for transfers between devices: 9.42 us -> 0.01 us  [shards(): lax.ppermute(own_far, SPACE, [(s, far_block(s)) for s in range(blocks)])]
    all_to_all x1, blocking collectives: 21.4 us -> 27.3 us  [shards(): columns = lax.all_to_all(send, SPACE, 0, 0, tiled=True)]
    ppermute x1, starting transfers between devices: 8.43 us -> 3.02 us  [shards(): other_total = lax.ppermute(own_total, 'zb', [(0, 1), (1, 0)])]
    all_to_all x1, blocking collectives: 8.94 us -> 14.1 us  [shards(): gathered = lax.all_to_all(copies, 'za', 0, 0, tiled=True)]
    ppermute x1, waiting for transfers between devices: 1.29 us -> 5.53 us  [shards(): other_total = lax.ppermute(own_total, 'zb', [(0, 1), (1, 0)])]
    ppermute x2, waiting for transfers between devices: 0.01 us -> 3.93 us  [the longest x1 3.93 us: shards(): start_far = lax.ppermute(edge_far, TM + SPACE, across)]
  transfers between devices with their start and end apart: 5 -> 5, of which waited for: 2 -> 2; matrix products, arithmetic and copies ran while one was open for 0% -> 0% of each run, Pallas kernels for 3% -> 2%
where the time goes in v6:
time: 108 us; the launch traced here: 107 us
  blocking collectives  58.6 us (54%)
  starting transfers between devices  28.8 us (27%)
  waiting for transfers between devices  9.47 us (9%)
  Pallas kernels  7.97 us (7%)
  local copies, waits for them, and re-layouts  2.19 us (2%)
    all_to_all x1, blocking collectives, shards(): columns = lax.all_to_all(send, SPACE, 0, 0, tiled=True)  27.3 us
    all_to_all x1, blocking collectives, shards(): returned = lax.all_to_all(back, ('x', 'y', 'c'), 0, 0, tiled=True)  17.2 us
    ppermute x1, starting transfers between devices, shards(): lax.ppermute(own_far, SPACE, [(s, far_block(s)) for s in range(blocks)])  15.4 us
    all_to_all x1, blocking collectives, shards(): gathered = lax.all_to_all(copies, 'za', 0, 0, tiled=True)  14.1 us
    pallas_call x8, Pallas kernels, call(): pl.pallas_call(kernel, out_shape=shapes[0] if single else shapes, in_spec...  7.97 us
    ppermute x1, waiting for transfers between devices, shards(): other_total = lax.ppermute(own_total, 'zb', [(0, 1), (1, 0)])  5.53 us
    ppermute x1, starting transfers between devices, shards(): lax.ppermute(u_old[0, 4], TM, [(i, i + 1) for i in range(slices - 1)])  4.38 us
    ppermute x1, starting transfers between devices, shards(): near = lax.ppermute(near_out, 'c', [(0, 1), (1, 0)])  4.04 us
  transfers between devices with their start and end apart: 5, of which 2 were waited for; matrix products, arithmetic and copies ran while one was open for 0% of the time, Pallas kernels for 2%

profile of v6, /device:TPU:1, one launch (start us, length us, event | category | flops | bytes accessed | tf_op | source)
XLA Modules:
  0.0 107.2 jit_solution(11963292219365031810)
XLA Ops:
  0.0 0.9 slice_bitcast_fusion
  1.0 4.4 %collective-permute-start = (f32[16,16,128]{2,1,0:T(8,128)S(1)}, f32[16,16,128]{2,1,0:T(8,128)S(1)}, u32[]{:S(2)}, u32[]{:S(2)}) collective-permute-start(f32[16,16,128]{2,1,0:T(8,128)S(1)} %slice_bitcast_fusion), channel_id=1, source_target_pairs={{0,16},{16,32},{32,48},{48,64},{64,80},{80,96},{96,112},{112,128},... | collective-permute-start | bytes 393224 | tf_op jit(solution)/shard_map/ppermute | solution.py:480
  5.4 0.1 stack.31.place
  5.4 1.1 %copy-done.9 = f32[1,5,16,16,128]{4,3,2,1,0:T(8,128)S(1)} copy-done((f32[1,5,16,16,128]{4,3,2,1,0:T(8,128)S(1)}, f32[1,5,16,16,128]{4,3,2,1,0:T(8,128)}, u32[]{:S(2)}) %copy-start.9) | copy-done | bytes 655384
  6.5 1.0 shard_map.109
  7.6 15.4 %collective-permute-start.3 = (f32[10,16,128]{2,1,0:T(8,128)S(1)}, f32[10,16,128]{2,1,0:T(8,128)S(1)}, u32[]{:S(2)}, u32[]{:S(2)}) collective-permute-start(f32[10,16,128]{2,1,0:T(8,128)S(1)} %get-tuple-element.20.own_far), channel_id=1, source_target_pairs={{0,15},{1,2},{2,1},{3,4},{4,3},{5,6},{6,5},{7,8},{8,7},{9,10},{10,... | collective-permute-start | bytes 245768 | tf_op jit(solution)/shard_map/ppermute | solution.py:477
  23.0 1.9 %collective-permute-start.2 = (f32[4,16,128]{2,1,0:T(8,128)S(1)}, f32[4,16,128]{2,1,0:T(8,128)S(1)}, u32[]{:S(2)}, u32[]{:S(2)}) collective-permute-start(f32[4,16,128]{2,1,0:T(8,128)S(1)} %get-tuple-element.18), channel_id=1, source_target_pairs={{0,31},{1,18},{2,17},{3,20},{4,19},{5,22},{6,21},{7,24},{8,23},{9,... | collective-permute-start | bytes 98312 | tf_op jit(solution)/shard_map/ppermute | solution.py:478
  24.9 0.6 shard_map.110
  25.5 0.0 copy-start.3
  25.5 0.0 copy-start.7
  25.5 0.0 copy-start.8
  25.5 4.0 %collective-permute-start.1 = (f32[14,16,128]{2,1,0:T(8,128)S(1)}, f32[14,16,128]{2,1,0:T(8,128)S(1)}, u32[]{:S(2)}, u32[]{:S(2)}) collective-permute-start(f32[14,16,128]{2,1,0:T(8,128)S(1)} %shard_map.110), channel_id=1, source_target_pairs={{0,1},{1,0},{2,3},{3,2},{4,5},{5,4},{6,7},{7,6},{8,9},{9,8},{10,11... | collective-permute-start | bytes 344072 | tf_op jit(solution)/shard_map/ppermute | solution.py:484
  29.6 3.9 %collective-permute-done.2.start_far = f32[4,16,128]{2,1,0:T(8,128)S(1)} collective-permute-done((f32[4,16,128]{2,1,0:T(8,128)S(1)}, f32[4,16,128]{2,1,0:T(8,128)S(1)}, u32[]{:S(2)}, u32[]{:S(2)}) %collective-permute-start.2) | collective-permute-done | bytes 32800 | tf_op jit(solution)/shard_map/ppermute | solution.py:478
  33.5 1.9 %shard_map.112 = (f32[5,24,16,128]{3,2,1,0:T(8,128)S(1)}, f32[16,16,128]{2,1,0:T(8,128)S(1)}, f32[64,256]{1,0:T(8,128)S(1)}) custom-call(s32[8]{0:T(128)S(1)} %stack.31.place, f32[16,16,128]{2,1,0:T(8,128)S(1)} %copy-done.1, f32[16,16,128]{2,1,0:T(8,128)S(1)} %collective-permute-done.previous, f32[14,16,128]{2,1,0:T(8,128)S(1)} %collective-permute-done.1.near, ...), custom_call_target="tpu_custom_call" | custom-call | bytes 1048576 | tf_op jit(solution)/shard_map/pallas_call | solution.py:431
  35.4 0.0 copy-start.4
  35.4 27.3 %all_to_all.15.got = f32[16,16,128]{2,1,0:T(8,128)S(1)} all-to-all(f32[16,16,128]{2,1,0:T(8,128)S(1)} %get-tuple-element.22), channel_id=1, replica_groups=mesh['x'=4,'zb'=2,'za'=4,'y'=4,'zh'=2,'c'=2] {'y','zh','c'}, dimensions={0} | all-to-all | bytes 262144 | tf_op jit(solution)/shard_map/all_to_all | solution.py:498
  62.7 0.9 shard_map.113
  63.6 14.1 %all_to_all.16.offsets = f32[4,64,128]{2,1,0:T(8,128)S(1)} all-to-all(f32[4,64,128]{2,1,0:T(8,128)S(1)} %get-tuple-element.23), channel_id=1, replica_groups=mesh['x'=4,'zb'=2,'za'=4,'y'=4,'zh'=2,'c'=2] {'za'}, dimensions={0} | all-to-all | bytes 262144 | tf_op jit(solution)/shard_map/all_to_all | solution.py:506
  77.7 0.6 shard_map.114
  78.3 3.0 %collective-permute-start.4 = (f32[64,128]{1,0:T(8,128)S(1)}, f32[64,128]{1,0:T(8,128)S(1)}, u32[]{:S(2)}, u32[]{:S(2)}) collective-permute-start(f32[64,128]{1,0:T(8,128)S(1)} %get-tuple-element.24.own_total), channel_id=1, source_target_pairs={{0,64},{64,0},{1,65},{65,1},{2,66},{66,2},{3,67},{67,3},{4,68},{68... | collective-permute-start | bytes 98312 | tf_op jit(solution)/shard_map/ppermute | solution.py:510
  81.3 5.5 %collective-permute-done.4.other_total = f32[64,128]{1,0:T(8,128)S(1)} collective-permute-done((f32[64,128]{1,0:T(8,128)S(1)}, f32[64,128]{1,0:T(8,128)S(1)}, u32[]{:S(2)}, u32[]{:S(2)}) %collective-permute-start.4) | collective-permute-done | bytes 32800 | tf_op jit(solution)/shard_map/ppermute | solution.py:510
  86.9 1.0 shard_map.115
  87.9 17.2 %all_to_all.17.got = f32[32,8,256]{2,1,0:T(8,128)S(1)} all-to-all(f32[32,8,256]{2,1,0:T(8,128)S(1)} %shard_map.115), channel_id=1, replica_groups=mesh['x'=4,'zb'=2,'za'=4,'y'=4,'zh'=2,'c'=2] {'x','y','c'}, dimensions={0} | all-to-all | bytes 524288 | tf_op jit(solution)/shard_map/all_to_all | solution.py:517
  105.2 2.0 %shard_map.116 = f32[5,16,16,128]{3,2,1,0:T(8,128)} custom-call(s32[8]{0:T(128)S(1)} %stack.31.place, f32[5,24,16,128]{3,2,1,0:T(8,128)S(1)} %get-tuple-element.21.w, f32[32,8,256]{2,1,0:T(8,128)S(1)} %all_to_all.17.got, f32[64,256]{1,0:T(8,128)S(1)} %get-tuple-element.28.hats, f32[128,64]{1,0:T(8,128)S(1)} %copy-done.5, f32[128,256]{1,0:T(8,128)S(1)} %copy-done.2), custom_call_target="tpu_custom_call" | custom-call | bytes 1048576 | tf_op jit(solution)/shard_map/pallas_call | solution.py:431
  (21 shorter events, 0.1 us)
Async XLA Ops:
  0.0 5.4 %copy-start.1 = (f32[16,16,128]{2,1,0:T(8,128)S(1)}, f32[16,16,128]{2,1,0:T(8,128)}, u32[]{:S(2)}) copy-start(f32[16,16,128]{2,1,0:T(8,128)} %first.5) | copy-start | bytes 393220
  1.0 24.0 %collective-permute-start = (f32[16,16,128]{2,1,0:T(8,128)S(1)}, f32[16,16,128]{2,1,0:T(8,128)S(1)}, u32[]{:S(2)}, u32[]{:S(2)}) collective-permute-start(f32[16,16,128]{2,1,0:T(8,128)S(1)} %slice_bitcast_fusion), channel_id=1, source_target_pairs={{0,16},{16,32},{32,48},{48,64},{64,80},{80,96},{96,112},{112,128},... | collective-permute-start | bytes 393224 | tf_op jit(solution)/shard_map/ppermute | solution.py:480
  5.4 1.1 %copy-start.9 = (f32[1,5,16,16,128]{4,3,2,1,0:T(8,128)S(1)}, f32[1,5,16,16,128]{4,3,2,1,0:T(8,128)}, u32[]{:S(2)}) copy-start(f32[1,5,16,16,128]{4,3,2,1,0:T(8,128)} %param.11) | copy-start | bytes 1966084
  7.6 22.0 %collective-permute-start.3 = (f32[10,16,128]{2,1,0:T(8,128)S(1)}, f32[10,16,128]{2,1,0:T(8,128)S(1)}, u32[]{:S(2)}, u32[]{:S(2)}) collective-permute-start(f32[10,16,128]{2,1,0:T(8,128)S(1)} %get-tuple-element.20.own_far), channel_id=1, source_target_pairs={{0,15},{1,2},{2,1},{3,4},{4,3},{5,6},{6,5},{7,8},{8,7},{9,10},{10,... | collective-permute-start | bytes 245768 | tf_op jit(solution)/shard_map/ppermute | solution.py:477
  23.0 10.5 %collective-permute-start.2 = (f32[4,16,128]{2,1,0:T(8,128)S(1)}, f32[4,16,128]{2,1,0:T(8,128)S(1)}, u32[]{:S(2)}, u32[]{:S(2)}) collective-permute-start(f32[4,16,128]{2,1,0:T(8,128)S(1)} %get-tuple-element.18), channel_id=1, source_target_pairs={{0,31},{1,18},{2,17},{3,20},{4,19},{5,22},{6,21},{7,24},{8,23},{9,... | collective-permute-start | bytes 98312 | tf_op jit(solution)/shard_map/ppermute | solution.py:478
  25.5 8.1 %copy-start.3 = (f32[256,128]{1,0:T(8,128)S(1)}, f32[256,128]{1,0:T(8,128)}, u32[]{:S(2)}) copy-start(f32[256,128]{1,0:T(8,128)} %constant.49.clone.down_y) | copy-start | bytes 393220
  25.5 8.0 %copy-start.7 = (f32[64,128]{1,0:T(8,128)S(1)}, f32[64,128]{1,0:T(8,128)}, u32[]{:S(2)}) copy-start(f32[64,128]{1,0:T(8,128)} %constant.51.clone.stencil) | copy-start | bytes 98308
  25.5 8.0 %copy-start.8 = (f32[64,128]{1,0:T(8,128)S(1)}, f32[64,128]{1,0:T(8,128)}, u32[]{:S(2)}) copy-start(f32[64,128]{1,0:T(8,128)} %constant.50.clone.down_x) | copy-start | bytes 98308
  25.5 8.0 %collective-permute-start.1 = (f32[14,16,128]{2,1,0:T(8,128)S(1)}, f32[14,16,128]{2,1,0:T(8,128)S(1)}, u32[]{:S(2)}, u32[]{:S(2)}) collective-permute-start(f32[14,16,128]{2,1,0:T(8,128)S(1)} %shard_map.110), channel_id=1, source_target_pairs={{0,1},{1,0},{2,3},{3,2},{4,5},{5,4},{6,7},{7,6},{8,9},{9,8},{10,11... | collective-permute-start | bytes 344072 | tf_op jit(solution)/shard_map/ppermute | solution.py:484
  35.4 27.3 %copy-start = (f32[128,128]{1,0:T(8,128)S(1)}, f32[128,128]{1,0:T(8,128)}, u32[]{:S(2)}) copy-start(f32[128,128]{1,0:T(8,128)} %constant.54.clone.denom) | copy-start | bytes 196612
  35.4 27.3 %copy-start.4 = (f32[128,256]{1,0:T(8,128)S(1)}, f32[128,256]{1,0:T(8,128)}, u32[]{:S(2)}) copy-start(f32[128,256]{1,0:T(8,128)} %constant.52.clone.table) | copy-start | bytes 393220
  35.4 27.3 %copy-start.10 = (f32[8]{0:T(128)S(1)}, f32[8]{0:T(128)}, u32[]{:S(2)}) copy-start(f32[8]{0:T(128)} %constant.55.clone.shift_x) | copy-start | bytes 100
  77.7 9.2 %copy-start.6 = (f32[2,64,128]{2,1,0:T(8,128)S(1)}, f32[2,64,128]{2,1,0:T(8,128)}, u32[]{:S(2)}) copy-start(f32[2,64,128]{2,1,0:T(8,128)} %constant.53.clone.inverse_z) | copy-start | bytes 196612
  78.3 8.6 %collective-permute-start.4 = (f32[64,128]{1,0:T(8,128)S(1)}, f32[64,128]{1,0:T(8,128)S(1)}, u32[]{:S(2)}, u32[]{:S(2)}) collective-permute-start(f32[64,128]{1,0:T(8,128)S(1)} %get-tuple-element.24.own_total), channel_id=1, source_target_pairs={{0,64},{64,0},{1,65},{65,1},{2,66},{66,2},{3,67},{67,3},{4,68},{68... | collective-permute-start | bytes 98312 | tf_op jit(solution)/shard_map/ppermute | solution.py:510
  87.9 17.3 %copy-start.2 = (f32[128,256]{1,0:T(8,128)S(1)}, f32[128,256]{1,0:T(8,128)}, u32[]{:S(2)}) copy-start(f32[128,256]{1,0:T(8,128)} %constant.57.clone.up_y) | copy-start | bytes 393220
  87.9 17.3 %copy-start.5 = (f32[128,64]{1,0:T(8,128)S(1)}, f32[128,64]{1,0:T(8,128)}, u32[]{:S(2)}) copy-start(f32[128,64]{1,0:T(8,128)} %constant.56.clone.up_x) | copy-start | bytes 98308

commit v7 on v6

--- a/solution.py
+++ b/solution.py
@@ -11,6 +11,8 @@
 
 TM = ("x", "zb", "za")
 SPACE = ("y", "zh", "c")
+FORWARD = ("zb", "y", "zh", "c")
+ROWS = 10
 
 step_length = 0.4
 diffusion = 1.0
@@ -111,11 +113,11 @@
     stencil = np.broadcast_to(stencil, (rows_c, planes, cols_c)).reshape(-1, cols_c)
     stencil = np.concatenate([stencil, stencil], 1)
     blocks = depth // planes
-    forward_z = np.zeros((depth, blocks, 2, planes))
-    forward_z[:, :, 0, :] = hz.reshape(depth, blocks, planes)
+    forward_z = np.zeros((depth, ROWS, blocks))
     for s in range(blocks):
-        forward_z[:, s, 1, 0] = hz[:, (s * planes - 1) % depth]
-        forward_z[:, s, 1, planes - 1] = hz[:, (s * planes + planes) % depth]
+        forward_z[:, :planes, s] = hz[:, s * planes : (s + 1) * planes]
+        forward_z[:, planes, s] = hz[:, (s * planes - 1) % depth]
+        forward_z[:, planes + 1, s] = hz[:, (s * planes + planes) % depth]
     forward_z = forward_z.reshape(depth, -1)
     denom = 1.0 - half * (2.0 * cos_z[:, None] + 2.0 * cos_y[None, :] - 6.0)
     denom = np.concatenate([denom, denom], 1)
@@ -145,6 +147,10 @@
     near = pltpu.roll(f, 1, 0) + pltpu.roll(f, f.shape[0] - 1, 0)
     near = near + pltpu.roll(f, 1, 1) + pltpu.roll(f, f.shape[1] - 1, 1)
     return diffusion * near - f * ((6.0 * diffusion - reaction) + reaction * (f * f))
+
+
+def last_kernel(u, last):
+    last[...] = u[4]
 
 
 def old_kernel(place, u, first, g, near, far, edge_far):
@@ -316,27 +322,44 @@
     for y in range(4):
         for c in range(2):
             kx = 2 * y + c
-            span = slice(kx * coarse, (kx + 1) * coarse)
-            for zh in range(2):
-                send[4 * y + 2 * zh + c, :coarse] = inside[span]
-                send[4 * y + 2 * zh + c, coarse:] = spill[span]
+            at = kx * coarse
+            lines = [inside[at + p : at + p + 1] for p in range(coarse)]
+            lines += [spill[at : at + 1], spill[at + coarse - 1 : at + coarse]]
+            for zb in range(2):
+                for zh in range(2):
+                    peer = 16 * zb + 4 * y + 2 * zh + c
+                    for r in range(ROWS):
+                        send[peer, :, r * width : (r + 1) * width] = lines[r]
     hats[...] = spectral[:, width:]
 
 
-def spectrum_kernel(place, shift_x, got, table, denom, lifted, offset, copies):
+def spectrum_kernel(place, shift_x, got, table, denom, lifted, offset, copies, lines):
+    zb = place[7]
     depth = table.shape[0]
     half = depth // 2
     d = denom[...] - shift_x[place[4]]
     inv = 1.0 / d
-    lift = dot(table[...], got[...].reshape(-1, d.shape[1]))
-    weighted = lift * inv
-    weighted = jnp.where(left_half(d), weighted * inv, weighted)
-    total = weighted + lanes_swapped(weighted)
-    lifted[...] = lift
-    offset[...] = total
-    packed = jnp.where(left_half(total[:half]), total[:half], total[half:])
-    for i in range(copies.shape[0]):
-        copies[i] = packed
+    width = d.shape[1]
+    blocks = got.shape[0] // 2
+    for part in range(2):
+        for r in range(ROWS):
+            span = slice(r * width, (r + 1) * width)
+            for s in range(blocks):
+                at = r * blocks + s
+                lines[at : at + 1, part * width : (part + 1) * width] = got[part * blocks + s, :, span]
+    both = dot(table[...], lines[...])
+    totals = []
+    for part in range(2):
+        lift = both[:, part * width : (part + 1) * width]
+        weighted = lift * inv
+        weighted = jnp.where(left_half(d), weighted * inv, weighted)
+        total = weighted + lanes_swapped(weighted)
+        totals.append(total)
+        packed = jnp.where(left_half(total[:half]), total[:half], total[half:])
+        for i in range(copies.shape[0]):
+            copies[i, part * half : (part + 1) * half] = packed
+    lifted[...] = jnp.where(zb == 0, both[:, :width], both[:, width:])
+    offset[...] = jnp.where(zb == 0, totals[0], totals[1])
 
 
 def packed_inverse(place, shift_x, denom):
@@ -347,35 +370,23 @@
     return inv, left, jnp.where(left, inv[:half], inv[half:])
 
 
-def group_kernel(place, shift_x, offsets, denom, total_out, prefix_out):
-    za = place[2]
-    _, _, inv = packed_inverse(place, shift_x, denom)
-    inv2 = inv * inv
-    total = jnp.zeros_like(inv2)
-    prefix = jnp.zeros_like(inv2)
-    for m in range(offsets.shape[0]):
-        piece = offsets[m]
-        total = total * inv2 + piece
-        prefix = jnp.where(m < za, prefix * inv2 + piece, prefix)
-    total_out[...] = total
-    prefix_out[...] = prefix
-
-
-def scan_kernel(
-    place, shift_x, own_total, other_total, own_prefix, lifted, offset, denom, inverse_z, out
-):
+def scan_kernel(place, shift_x, offsets, lifted, offset, denom, inverse_z, out):
     za, block, zh, zb = place[2], place[3], place[5], place[7]
+    half = denom.shape[0] // 2
     inv, left, inv_packed = packed_inverse(place, shift_x, denom)
     inv2 = inv_packed * inv_packed
     inv4 = inv2 * inv2
     inv8 = inv4 * inv4
     whole = inv8 * inv8
+    slice_at = zb * 4 + za
+    prefix = jnp.zeros_like(inv2)
+    total = jnp.zeros_like(inv2)
+    for m in range(8):
+        piece = offsets[m % 4, (m // 4) * half : (m // 4 + 1) * half]
+        total = total * inv2 + piece
+        prefix = jnp.where(m < slice_at, prefix * inv2 + piece, prefix)
     power = jnp.where(za % 2 == 1, inv2, 1.0)
     power = jnp.where(za >= 2, power * inv4, power)
-    early = jnp.where(zb == 0, own_total[...], other_total[...])
-    late = jnp.where(zb == 0, other_total[...], own_total[...])
-    prefix = own_prefix[...] + jnp.where(zb == 0, 0.0, power * early)
-    total = early * inv8 + late
     power = jnp.where(zb == 0, power, power * inv8)
     inverse = inverse_z[zh]
     weights = jnp.where(left_half(inv), inv, inv * inv)
@@ -456,6 +467,7 @@
     place = jnp.stack(place + [lax.axis_index("zh"), slices, lax.axis_index("zb")])
     place = place.astype(jnp.int32)
 
+    last = call(last_kernel, (planes, rows, cols), [], u_old[0])
     halo, edge = (PACK, rows, cols), (REACH, rows, cols)
     g, own_near, own_far, edge_far = call(
         old_kernel,
@@ -477,7 +489,7 @@
     got_far = lax.ppermute(own_far, SPACE, [(s, far_block(s)) for s in range(blocks)])
     start_far = lax.ppermute(edge_far, TM + SPACE, across)
     got_far = call(relay_kernel, halo, [], got_far, flops=10**11)
-    previous = lax.ppermute(u_old[0, 4], TM, [(i, i + 1) for i in range(slices - 1)])
+    previous = lax.ppermute(last, TM, [(i, i + 1) for i in range(slices - 1)])
     near_out = call(
         near_kernel, (PACK + REACH, rows, cols), [place], u_init, previous, own_near
     )
@@ -487,7 +499,7 @@
         sweep_kernel,
         [
             (5, planes + 2 * REACH, rows, cols),
-            (blocks, 2 * coarse, 2 * cols_c),
+            (2 * blocks, 1, ROWS * 2 * cols_c),
             (rows_c * coarse, 4 * cols_c),
         ],
         [place],
@@ -495,24 +507,20 @@
         down_y, down_x, stencil,
         scratch=[pltpu.VMEM((2, coarse, rows, cols), jnp.float32)],
     )
-    columns = lax.all_to_all(send, SPACE, 0, 0, tiled=True)
-    packed = (depth_c // 2, 2 * cols_c)
+    columns = lax.all_to_all(send, FORWARD, 0, 0, tiled=True)
     lifted, offset, copies = call(
         spectrum_kernel,
-        [(depth_c, 2 * cols_c), (depth_c, 2 * cols_c), (4, *packed)],
+        [(depth_c, 2 * cols_c), (depth_c, 2 * cols_c), (4, depth_c, 2 * cols_c)],
         [place, shift_x],
         columns, forward_z, denom,
+        scratch=[pltpu.VMEM((ROWS * blocks, 4 * cols_c), jnp.float32)],
     )
     gathered = lax.all_to_all(copies, "za", 0, 0, tiled=True)
-    own_total, own_prefix = call(
-        group_kernel, [packed, packed], [place, shift_x], gathered, denom
-    )
-    other_total = lax.ppermute(own_total, "zb", [(0, 1), (1, 0)])
     back = call(
         scan_kernel,
         (4 * rows_c, coarse, 4 * cols_c),
         [place, shift_x],
-        own_total, other_total, own_prefix, lifted, offset, denom, inverse_z,
+        gathered, lifted, offset, denom, inverse_z,
     )
     returned = lax.all_to_all(back, ("x", "y", "c"), 0, 0, tiled=True)
     out = call(

time: 108 us -> 101 us (0.935)
  waiting for transfers between devices: 9.47 us -> 4.22 us
  starting transfers between devices: 28.8 us -> 25.9 us
  blocking collectives: 58.6 us -> 61 us
    ppermute x2 -> x1, waiting for transfers between devices: 5.54 us -> 0.01 us  [shards(): previous = lax.ppermute(last, TM, [(i, i + 1) for i in range(slices - 1)])]
    ppermute x2 -> x1, starting transfers between devices: 7.4 us -> 4.51 us  [shards(): previous = lax.ppermute(last, TM, [(i, i + 1) for i in range(slices - 1)])]
    all_to_all x1, blocking collectives: 14.1 us -> 15.5 us  [shards(): gathered = lax.all_to_all(copies, 'za', 0, 0, tiled=True)]
  transfers between devices with their start and end apart: 5 -> 4, of which waited for: 2 -> 1; matrix products, arithmetic and copies ran while one was open for 0% -> 0% of each run, Pallas kernels for 2% -> 2%
where the time goes in v7:
time: 101 us; the launch traced here: 100 us
  blocking collectives  61 us (60%)
  starting transfers between devices  25.9 us (26%)
  Pallas kernels  7.59 us (8%)
  waiting for transfers between devices  4.22 us (4%)
  local copies, waits for them, and re-layouts  1.24 us (1%)
    all_to_all x1, blocking collectives, shards(): columns = lax.all_to_all(send, FORWARD, 0, 0, tiled=True)  27.3 us
    all_to_all x1, blocking collectives, shards(): returned = lax.all_to_all(back, ('x', 'y', 'c'), 0, 0, tiled=True)  18.2 us
    all_to_all x1, blocking collectives, shards(): gathered = lax.all_to_all(copies, 'za', 0, 0, tiled=True)  15.5 us
    ppermute x1, starting transfers between devices, shards(): lax.ppermute(own_far, SPACE, [(s, far_block(s)) for s in range(blocks)])  15.4 us
    pallas_call x8, Pallas kernels, call(): pl.pallas_call(kernel, out_shape=shapes[0] if single else shapes, in_spec...  7.59 us
    ppermute x1, starting transfers between devices, shards(): previous = lax.ppermute(last, TM, [(i, i + 1) for i in range(slices - 1)])  4.51 us
    ppermute x1, waiting for transfers between devices, shards(): start_far = lax.ppermute(edge_far, TM + SPACE, across)  4.21 us
    ppermute x1, starting transfers between devices, shards(): near = lax.ppermute(near_out, 'c', [(0, 1), (1, 0)])  4.04 us
  transfers between devices with their start and end apart: 4, of which 1 were waited for; matrix products, arithmetic and copies ran while one was open for 0% of the time, Pallas kernels for 2%

profile of v7, /device:TPU:1, one launch (start us, length us, event | category | flops | bytes accessed | tf_op | source)
XLA Modules:
  0.0 100.2 jit_solution(7741466326300872703)
XLA Ops:
  0.0 1.1 %copy-done = f32[1,5,16,16,128]{4,3,2,1,0:T(8,128)S(1)} copy-done((f32[1,5,16,16,128]{4,3,2,1,0:T(8,128)S(1)}, f32[1,5,16,16,128]{4,3,2,1,0:T(8,128)}, u32[]{:S(2)}) %copy-start) | copy-done | bytes 655384
  1.1 4.5 %collective-permute-start = (f32[16,16,128]{2,1,0:T(8,128)S(1)}, f32[16,16,128]{2,1,0:T(8,128)S(1)}, u32[]{:S(2)}, u32[]{:S(2)}) collective-permute-start(f32[16,16,128]{2,1,0:T(8,128)S(1)} %shard_map.109), channel_id=1, source_target_pairs={{0,16},{16,32},{32,48},{48,64},{64,80},{80,96},{96,112},{112,128},... | collective-permute-start | bytes 393224 | tf_op jit(solution)/shard_map/ppermute | solution.py:492
  5.6 0.1 stack.31.place
  5.7 1.0 %shard_map.110 = (f32[4,16,16,128]{3,2,1,0:T(8,128)S(1)}, f32[10,16,128]{2,1,0:T(8,128)S(1)}, f32[10,16,128]{2,1,0:T(8,128)S(1)}, f32[4,16,128]{2,1,0:T(8,128)S(1)}) custom-call(s32[8]{0:T(128)S(1)} %stack.31.place, f32[5,16,16,128]{3,2,1,0:T(8,128)S(1)} %bitcast.10, f32[16,16,128]{2,1,0:T(8,128)S(1)} %copy-done.2), custom_call_target="tpu_custom_call" | custom-call | flops 99999997952 | bytes 1048576 | tf_op jit(solution)/shard_map/pallas_call | solution.py:442
  6.8 15.4 %collective-permute-start.3 = (f32[10,16,128]{2,1,0:T(8,128)S(1)}, f32[10,16,128]{2,1,0:T(8,128)S(1)}, u32[]{:S(2)}, u32[]{:S(2)}) collective-permute-start(f32[10,16,128]{2,1,0:T(8,128)S(1)} %get-tuple-element.18.own_far), channel_id=1, source_target_pairs={{0,15},{1,2},{2,1},{3,4},{4,3},{5,6},{6,5},{7,8},{8,7},{9,10},{10,... | collective-permute-start | bytes 245768 | tf_op jit(solution)/shard_map/ppermute | solution.py:489
  22.2 1.9 %collective-permute-start.2 = (f32[4,16,128]{2,1,0:T(8,128)S(1)}, f32[4,16,128]{2,1,0:T(8,128)S(1)}, u32[]{:S(2)}, u32[]{:S(2)}) collective-permute-start(f32[4,16,128]{2,1,0:T(8,128)S(1)} %get-tuple-element.16), channel_id=1, source_target_pairs={{0,31},{1,18},{2,17},{3,20},{4,19},{5,22},{6,21},{7,24},{8,23},{9,... | collective-permute-start | bytes 98312 | tf_op jit(solution)/shard_map/ppermute | solution.py:490
  24.1 0.6 shard_map.111
  24.7 0.0 copy-start.5
  24.7 0.0 copy-start.9
  24.7 0.0 copy-start.10
  24.7 4.0 %collective-permute-start.1 = (f32[14,16,128]{2,1,0:T(8,128)S(1)}, f32[14,16,128]{2,1,0:T(8,128)S(1)}, u32[]{:S(2)}, u32[]{:S(2)}) collective-permute-start(f32[14,16,128]{2,1,0:T(8,128)S(1)} %shard_map.111), channel_id=1, source_target_pairs={{0,1},{1,0},{2,3},{3,2},{4,5},{5,4},{6,7},{7,6},{8,9},{9,8},{10,11... | collective-permute-start | bytes 344072 | tf_op jit(solution)/shard_map/ppermute | solution.py:496
  28.8 4.2 %collective-permute-done.2.start_far = f32[4,16,128]{2,1,0:T(8,128)S(1)} collective-permute-done((f32[4,16,128]{2,1,0:T(8,128)S(1)}, f32[4,16,128]{2,1,0:T(8,128)S(1)}, u32[]{:S(2)}, u32[]{:S(2)}) %collective-permute-start.2) | collective-permute-done | bytes 32800 | tf_op jit(solution)/shard_map/ppermute | solution.py:490
  33.0 1.9 %shard_map.113 = (f32[5,24,16,128]{3,2,1,0:T(8,128)S(1)}, f32[32,1,1280]{2,1,0:T(1,128)S(1)}, f32[64,256]{1,0:T(8,128)S(1)}) custom-call(s32[8]{0:T(128)S(1)} %stack.31.place, f32[16,16,128]{2,1,0:T(8,128)S(1)} %copy-done.2, f32[16,16,128]{2,1,0:T(8,128)S(1)} %collective-permute-done.previous, f32[14,16,128]{2,1,0:T(8,128)S(1)} %collective-permute-done.1.near, ...), custom_call_target="tpu_custom_call" | custom-call | bytes 1048576 | tf_op jit(solution)/shard_map/pallas_call | solution.py:442
  34.9 0.0 copy-start.3
  34.9 0.0 copy-start.11
  34.9 27.3 %all_to_all.15.got = f32[32,1,1280]{2,1,0:T(1,128)S(1)} all-to-all(f32[32,1,1280]{2,1,0:T(1,128)S(1)} %get-tuple-element.20), channel_id=1, replica_groups=mesh['x'=4,'zb'=2,'za'=4,'y'=4,'zh'=2,'c'=2] {'zb','y','zh','c'}, dimensions={0} | all-to-all | bytes 327680 | tf_op jit(solution)/shard_map/all_to_all | solution.py:510
  62.2 1.0 %shard_map.114 = (f32[128,128]{1,0:T(8,128)S(1)}, f32[128,128]{1,0:T(8,128)S(1)}, f32[4,128,128]{2,1,0:T(8,128)S(1)}) custom-call(s32[8]{0:T(128)S(1)} %stack.31.place, f32[8]{0:T(128)S(1)} %copy-done.11, f32[32,1,1280]{2,1,0:T(1,128)S(1)} %all_to_all.15.got, f32[128,160]{1,0:T(8,128)S(1)} %copy-done.6, f32[128,128]{1,0:T(8,128)S(1)} %copy-done.3), custom_call_target="tpu_custom_call" | custom-call | bytes 1048576 | tf_op jit(solution)/shard_map/pallas_call | solution.py:442
  63.2 0.0 copy-start.8
  63.2 15.5 %all_to_all.16.offsets = f32[4,128,128]{2,1,0:T(8,128)S(1)} all-to-all(f32[4,128,128]{2,1,0:T(8,128)S(1)} %get-tuple-element.21), channel_id=1, replica_groups=mesh['x'=4,'zb'=2,'za'=4,'y'=4,'zh'=2,'c'=2] {'za'}, dimensions={0} | all-to-all | bytes 524288 | tf_op jit(solution)/shard_map/all_to_all | solution.py:518
  78.8 1.1 %shard_map.115 = f32[32,8,256]{2,1,0:T(8,128)S(1)} custom-call(s32[8]{0:T(128)S(1)} %stack.31.place, f32[8]{0:T(128)S(1)} %copy-done.11, f32[4,128,128]{2,1,0:T(8,128)S(1)} %all_to_all.16.offsets, f32[128,128]{1,0:T(8,128)S(1)} %get-tuple-element.22.lifted, f32[128,128]{1,0:T(8,128)S(1)} %get-tuple-element.23.offset, f32[128,128]{1,0:T(8,128)S(1)} %copy-done.3, ...), custom_call_target="tpu_custom_call" | custom-call | bytes 1048576 | tf_op jit(solution)/shard_map/pallas_call | solution.py:442
  79.9 0.0 copy-start.4
  79.9 0.0 copy-start.7
  79.9 18.2 %all_to_all.17.got = f32[32,8,256]{2,1,0:T(8,128)S(1)} all-to-all(f32[32,8,256]{2,1,0:T(8,128)S(1)} %shard_map.115), channel_id=1, replica_groups=mesh['x'=4,'zb'=2,'za'=4,'y'=4,'zh'=2,'c'=2] {'x','y','c'}, dimensions={0} | all-to-all | bytes 524288 | tf_op jit(solution)/shard_map/all_to_all | solution.py:525
  98.1 2.0 %shard_map.116 = f32[5,16,16,128]{3,2,1,0:T(8,128)} custom-call(s32[8]{0:T(128)S(1)} %stack.31.place, f32[5,24,16,128]{3,2,1,0:T(8,128)S(1)} %get-tuple-element.19.w, f32[32,8,256]{2,1,0:T(8,128)S(1)} %all_to_all.17.got, f32[64,256]{1,0:T(8,128)S(1)} %get-tuple-element.24.hats, f32[128,64]{1,0:T(8,128)S(1)} %copy-done.7, f32[128,256]{1,0:T(8,128)S(1)} %copy-done.4), custom_call_target="tpu_custom_call" | custom-call | bytes 1048576 | tf_op jit(solution)/shard_map/pallas_call | solution.py:442
  (20 shorter events, 0.1 us)
Async XLA Ops:
  0.0 1.1 %copy-start = (f32[1,5,16,16,128]{4,3,2,1,0:T(8,128)S(1)}, f32[1,5,16,16,128]{4,3,2,1,0:T(8,128)}, u32[]{:S(2)}) copy-start(f32[1,5,16,16,128]{4,3,2,1,0:T(8,128)} %param.11) | copy-start | bytes 1966084
  1.1 4.6 %copy-start.1 = (f32[1,5,16,16,128]{4,3,2,1,0:T(8,128)S(1)}, f32[1,5,16,16,128]{4,3,2,1,0:T(8,128)}, u32[]{:S(2)}) copy-start(f32[1,5,16,16,128]{4,3,2,1,0:T(8,128)} %param.11) | copy-start | bytes 1966084
  1.1 4.6 %copy-start.2 = (f32[16,16,128]{2,1,0:T(8,128)S(1)}, f32[16,16,128]{2,1,0:T(8,128)}, u32[]{:S(2)}) copy-start(f32[16,16,128]{2,1,0:T(8,128)} %first.5) | copy-start | bytes 393220
  1.1 23.0 %collective-permute-start = (f32[16,16,128]{2,1,0:T(8,128)S(1)}, f32[16,16,128]{2,1,0:T(8,128)S(1)}, u32[]{:S(2)}, u32[]{:S(2)}) collective-permute-start(f32[16,16,128]{2,1,0:T(8,128)S(1)} %shard_map.109), channel_id=1, source_target_pairs={{0,16},{16,32},{32,48},{48,64},{64,80},{80,96},{96,112},{112,128},... | collective-permute-start | bytes 393224 | tf_op jit(solution)/shard_map/ppermute | solution.py:492
  6.8 22.0 %collective-permute-start.3 = (f32[10,16,128]{2,1,0:T(8,128)S(1)}, f32[10,16,128]{2,1,0:T(8,128)S(1)}, u32[]{:S(2)}, u32[]{:S(2)}) collective-permute-start(f32[10,16,128]{2,1,0:T(8,128)S(1)} %get-tuple-element.18.own_far), channel_id=1, source_target_pairs={{0,15},{1,2},{2,1},{3,4},{4,3},{5,6},{6,5},{7,8},{8,7},{9,10},{10,... | collective-permute-start | bytes 245768 | tf_op jit(solution)/shard_map/ppermute | solution.py:489
  22.2 10.8 %collective-permute-start.2 = (f32[4,16,128]{2,1,0:T(8,128)S(1)}, f32[4,16,128]{2,1,0:T(8,128)S(1)}, u32[]{:S(2)}, u32[]{:S(2)}) collective-permute-start(f32[4,16,128]{2,1,0:T(8,128)S(1)} %get-tuple-element.16), channel_id=1, source_target_pairs={{0,31},{1,18},{2,17},{3,20},{4,19},{5,22},{6,21},{7,24},{8,23},{9,... | collective-permute-start | bytes 98312 | tf_op jit(solution)/shard_map/ppermute | solution.py:490
  24.7 8.3 %copy-start.5 = (f32[256,128]{1,0:T(8,128)S(1)}, f32[256,128]{1,0:T(8,128)}, u32[]{:S(2)}) copy-start(f32[256,128]{1,0:T(8,128)} %constant.49.clone.down_y) | copy-start | bytes 393220
  24.7 8.3 %copy-start.9 = (f32[64,128]{1,0:T(8,128)S(1)}, f32[64,128]{1,0:T(8,128)}, u32[]{:S(2)}) copy-start(f32[64,128]{1,0:T(8,128)} %constant.51.clone.stencil) | copy-start | bytes 98308
  24.7 8.3 %copy-start.10 = (f32[64,128]{1,0:T(8,128)S(1)}, f32[64,128]{1,0:T(8,128)}, u32[]{:S(2)}) copy-start(f32[64,128]{1,0:T(8,128)} %constant.50.clone.down_x) | copy-start | bytes 98308
  24.7 8.3 %collective-permute-start.1 = (f32[14,16,128]{2,1,0:T(8,128)S(1)}, f32[14,16,128]{2,1,0:T(8,128)S(1)}, u32[]{:S(2)}, u32[]{:S(2)}) collective-permute-start(f32[14,16,128]{2,1,0:T(8,128)S(1)} %shard_map.111), channel_id=1, source_target_pairs={{0,1},{1,0},{2,3},{3,2},{4,5},{5,4},{6,7},{7,6},{8,9},{9,8},{10,11... | collective-permute-start | bytes 344072 | tf_op jit(solution)/shard_map/ppermute | solution.py:496
  34.9 27.3 %copy-start.3 = (f32[128,128]{1,0:T(8,128)S(1)}, f32[128,128]{1,0:T(8,128)}, u32[]{:S(2)}) copy-start(f32[128,128]{1,0:T(8,128)} %constant.54.clone.denom) | copy-start | bytes 196612
  34.9 27.3 %copy-start.6 = (f32[128,160]{1,0:T(8,128)S(1)}, f32[128,160]{1,0:T(8,128)}, u32[]{:S(2)}) copy-start(f32[128,160]{1,0:T(8,128)} %constant.52.clone.table) | copy-start | bytes 245764
  34.9 27.3 %copy-start.11 = (f32[8]{0:T(128)S(1)}, f32[8]{0:T(128)}, u32[]{:S(2)}) copy-start(f32[8]{0:T(128)} %constant.55.clone.shift_x) | copy-start | bytes 100
  63.2 15.5 %copy-start.8 = (f32[2,64,128]{2,1,0:T(8,128)S(1)}, f32[2,64,128]{2,1,0:T(8,128)}, u32[]{:S(2)}) copy-start(f32[2,64,128]{2,1,0:T(8,128)} %constant.53.clone.inverse_z) | copy-start | bytes 196612
  79.9 18.3 %copy-start.4 = (f32[128,256]{1,0:T(8,128)S(1)}, f32[128,256]{1,0:T(8,128)}, u32[]{:S(2)}) copy-start(f32[128,256]{1,0:T(8,128)} %constant.57.clone.up_y) | copy-start | bytes 393220
  79.9 18.3 %copy-start.7 = (f32[128,64]{1,0:T(8,128)S(1)}, f32[128,64]{1,0:T(8,128)}, u32[]{:S(2)}) copy-start(f32[128,64]{1,0:T(8,128)} %constant.56.clone.up_x) | copy-start | bytes 98308

commit v8 on v7

--- a/solution.py
+++ b/solution.py
@@ -126,8 +126,9 @@
     inverse_z = inverse_z.reshape(2, 8 * planes, depth)
     f32 = lambda a: jnp.asarray(a, jnp.float32)
     return (
-        f32(block_pair(down_y)), f32(down_x), f32(stencil), f32(forward_z), f32(inverse_z),
-        f32(denom), f32(shift_x), f32(up_x), f32(block_pair(up_y)),
+        table_halves(block_pair(down_y), 0), table_halves(down_x, 1), f32(stencil),
+        table_halves(forward_z, 1), table_halves(inverse_z, 2), f32(denom), f32(shift_x),
+        table_halves(up_x, 1), table_halves(block_pair(up_y), 0),
     )
 
 
@@ -139,8 +140,28 @@
     return lax.broadcasted_iota(jnp.int32, a.shape, 1) < a.shape[1] // 2
 
 
-def dot(a, b):
-    return jnp.dot(a, b, precision=lax.Precision.HIGHEST, preferred_element_type=jnp.float32)
+def halves(a):
+    high = a.astype(jnp.bfloat16)
+    return high, (a - high.astype(jnp.float32)).astype(jnp.bfloat16)
+
+
+def table_halves(table, axis):
+    table = np.asarray(table, np.float32)
+    high = table.astype(jnp.bfloat16)
+    low = (table - high.astype(np.float32)).astype(jnp.bfloat16)
+    return jnp.asarray(np.concatenate([high, high, low], axis))
+
+
+def table_times(table, b):
+    high, low = halves(b)
+    parts = jnp.concatenate([high, low, high], 0)
+    return jnp.dot(table, parts, preferred_element_type=jnp.float32)
+
+
+def times_table(a, table):
+    high, low = halves(a)
+    parts = jnp.concatenate([high, low, high], 1)
+    return jnp.dot(parts, table, preferred_element_type=jnp.float32)
 
 
 def plane_part(f):
@@ -302,10 +323,10 @@
     middle = jnp.zeros((rows - 2 * edge_rows, first.shape[2]), jnp.float32)
     edges = jnp.concatenate([w[4, REACH], middle, w[4, REACH + planes - 1]], 0)
     left = [
-        dot(jnp.concatenate(pair, 1), table)
+        times_table(jnp.concatenate(pair, 1), table)
         for pair in ((q0, q1), (paired(2), paired(4)), (restart, edges))
     ]
-    spectral = dot(down_x[...], jnp.concatenate(left, 1))
+    spectral = table_times(down_x[...], jnp.concatenate(left, 1))
     width = left[0].shape[1]
     states = spectral[:, width : 2 * width]
     third = spectral[:, 2 * width :]
@@ -347,7 +368,7 @@
             for s in range(blocks):
                 at = r * blocks + s
                 lines[at : at + 1, part * width : (part + 1) * width] = got[part * blocks + s, :, span]
-    both = dot(table[...], lines[...])
+    both = table_times(table[...], lines[...])
     totals = []
     for part in range(2):
         lift = both[:, part * width : (part + 1) * width]
@@ -401,7 +422,7 @@
             [jnp.where(left, packed, turned), jnp.where(left, turned, packed)], 0
         )
         later = begin * weights + jnp.where(xp == block, own, 0.0)
-        planar = dot(inverse, jnp.concatenate([later, begin], 1))
+        planar = table_times(inverse, jnp.concatenate([later, begin], 1))
         out[8 * xp : 8 * xp + 8] = planar.reshape(8, -1, planar.shape[1])
 
 
@@ -415,10 +436,10 @@
     half = delta.shape[1] // 2
     later = delta[:, :half]
     begin = jnp.where(place[0] == 0, 0.0, delta[:, half:])
-    spread = dot(up_x[...], jnp.concatenate([later, begin], 1))
+    spread = table_times(up_x[...], jnp.concatenate([later, begin], 1))
     table = up_y[...]
-    after = dot(spread[:, :half], table)
-    before = dot(spread[:, half:], table[:, :cols])
+    after = times_table(spread[:, :half], table)
+    before = times_table(spread[:, half:], table[:, :cols])
     parts = [before, after[:, :cols], after[:, cols:]]
     for m in range(5):
         mixed = None

time: 101 us -> 99.9 us (0.989)
  no operation moved by 1% of the time
where the time goes in v8:
time: 99.9 us; the launch traced here: 99.5 us
  blocking collectives  61 us (61%)
  starting transfers between devices  25.9 us (26%)
  Pallas kernels  6.93 us (7%)
  waiting for transfers between devices  4.22 us (4%)
  local copies, waits for them, and re-layouts  1.24 us (1%)
    all_to_all x1, blocking collectives, shards(): columns = lax.all_to_all(send, FORWARD, 0, 0, tiled=True)  27.3 us
    all_to_all x1, blocking collectives, shards(): returned = lax.all_to_all(back, ('x', 'y', 'c'), 0, 0, tiled=True)  18.3 us
    all_to_all x1, blocking collectives, shards(): gathered = lax.all_to_all(copies, 'za', 0, 0, tiled=True)  15.5 us
    ppermute x1, starting transfers between devices, shards(): lax.ppermute(own_far, SPACE, [(s, far_block(s)) for s in range(blocks)])  15.4 us
    pallas_call x8, Pallas kernels, call(): pl.pallas_call(kernel, out_shape=shapes[0] if single else shapes, in_spec...  6.93 us
    ppermute x1, starting transfers between devices, shards(): previous = lax.ppermute(last, TM, [(i, i + 1) for i in range(slices - 1)])  4.51 us
    ppermute x1, waiting for transfers between devices, shards(): start_far = lax.ppermute(edge_far, TM + SPACE, across)  4.21 us
    ppermute x1, starting transfers between devices, shards(): near = lax.ppermute(near_out, 'c', [(0, 1), (1, 0)])  4.04 us
  transfers between devices with their start and end apart: 4, of which 1 were waited for; matrix products, arithmetic and copies ran while one was open for 0% of the time, Pallas kernels for 2%

profile of v8, /device:TPU:1, one launch (start us, length us, event | category | flops | bytes accessed | tf_op | source)
XLA Modules:
  0.0 99.5 jit_solution(7403313194610395090)
XLA Ops:
  0.0 1.1 %copy-done = f32[1,5,16,16,128]{4,3,2,1,0:T(8,128)S(1)} copy-done((f32[1,5,16,16,128]{4,3,2,1,0:T(8,128)S(1)}, f32[1,5,16,16,128]{4,3,2,1,0:T(8,128)}, u32[]{:S(2)}) %copy-start) | copy-done | bytes 655384
  1.1 4.5 %collective-permute-start = (f32[16,16,128]{2,1,0:T(8,128)S(1)}, f32[16,16,128]{2,1,0:T(8,128)S(1)}, u32[]{:S(2)}, u32[]{:S(2)}) collective-permute-start(f32[16,16,128]{2,1,0:T(8,128)S(1)} %shard_map.109), channel_id=1, source_target_pairs={{0,16},{16,32},{32,48},{48,64},{64,80},{80,96},{96,112},{112,128},... | collective-permute-start | bytes 393224 | tf_op jit(solution)/shard_map/ppermute | solution.py:513
  5.6 0.1 stack.31.place
  5.7 1.0 %shard_map.110 = (f32[4,16,16,128]{3,2,1,0:T(8,128)S(1)}, f32[10,16,128]{2,1,0:T(8,128)S(1)}, f32[10,16,128]{2,1,0:T(8,128)S(1)}, f32[4,16,128]{2,1,0:T(8,128)S(1)}) custom-call(s32[8]{0:T(128)S(1)} %stack.31.place, f32[5,16,16,128]{3,2,1,0:T(8,128)S(1)} %bitcast.10, f32[16,16,128]{2,1,0:T(8,128)S(1)} %copy-done.2), custom_call_target="tpu_custom_call" | custom-call | flops 99999997952 | bytes 1048576 | tf_op jit(solution)/shard_map/pallas_call | solution.py:463
  6.8 15.4 %collective-permute-start.3 = (f32[10,16,128]{2,1,0:T(8,128)S(1)}, f32[10,16,128]{2,1,0:T(8,128)S(1)}, u32[]{:S(2)}, u32[]{:S(2)}) collective-permute-start(f32[10,16,128]{2,1,0:T(8,128)S(1)} %get-tuple-element.18.own_far), channel_id=1, source_target_pairs={{0,15},{1,2},{2,1},{3,4},{4,3},{5,6},{6,5},{7,8},{8,7},{9,10},{10,... | collective-permute-start | bytes 245768 | tf_op jit(solution)/shard_map/ppermute | solution.py:510
  22.2 1.9 %collective-permute-start.2 = (f32[4,16,128]{2,1,0:T(8,128)S(1)}, f32[4,16,128]{2,1,0:T(8,128)S(1)}, u32[]{:S(2)}, u32[]{:S(2)}) collective-permute-start(f32[4,16,128]{2,1,0:T(8,128)S(1)} %get-tuple-element.16), channel_id=1, source_target_pairs={{0,31},{1,18},{2,17},{3,20},{4,19},{5,22},{6,21},{7,24},{8,23},{9,... | collective-permute-start | bytes 98312 | tf_op jit(solution)/shard_map/ppermute | solution.py:511
  24.1 0.6 shard_map.111
  24.7 0.0 copy-start.5
  24.7 0.0 copy-start.9
  24.7 0.0 copy-start.10
  24.7 4.0 %collective-permute-start.1 = (f32[14,16,128]{2,1,0:T(8,128)S(1)}, f32[14,16,128]{2,1,0:T(8,128)S(1)}, u32[]{:S(2)}, u32[]{:S(2)}) collective-permute-start(f32[14,16,128]{2,1,0:T(8,128)S(1)} %shard_map.111), channel_id=1, source_target_pairs={{0,1},{1,0},{2,3},{3,2},{4,5},{5,4},{6,7},{7,6},{8,9},{9,8},{10,11... | collective-permute-start | bytes 344072 | tf_op jit(solution)/shard_map/ppermute | solution.py:517
  28.8 4.2 %collective-permute-done.2.start_far = f32[4,16,128]{2,1,0:T(8,128)S(1)} collective-permute-done((f32[4,16,128]{2,1,0:T(8,128)S(1)}, f32[4,16,128]{2,1,0:T(8,128)S(1)}, u32[]{:S(2)}, u32[]{:S(2)}) %collective-permute-start.2) | collective-permute-done | bytes 32800 | tf_op jit(solution)/shard_map/ppermute | solution.py:511
  33.0 1.7 %shard_map.113 = (f32[5,24,16,128]{3,2,1,0:T(8,128)S(1)}, f32[32,1,1280]{2,1,0:T(1,128)S(1)}, f32[64,256]{1,0:T(8,128)S(1)}) custom-call(s32[8]{0:T(128)S(1)} %stack.31.place, f32[16,16,128]{2,1,0:T(8,128)S(1)} %copy-done.2, f32[16,16,128]{2,1,0:T(8,128)S(1)} %collective-permute-done.previous, f32[14,16,128]{2,1,0:T(8,128)S(1)} %collective-permute-done.1.near, ...), custom_call_target="tpu_custom_call" | custom-call | bytes 1048576 | tf_op jit(solution)/shard_map/pallas_call | solution.py:463
  34.7 0.0 copy-start.3
  34.7 0.0 copy-start.6
  34.7 0.0 copy-start.11
  34.7 27.3 %all_to_all.15.got = f32[32,1,1280]{2,1,0:T(1,128)S(1)} all-to-all(f32[32,1,1280]{2,1,0:T(1,128)S(1)} %get-tuple-element.20), channel_id=1, replica_groups=mesh['x'=4,'zb'=2,'za'=4,'y'=4,'zh'=2,'c'=2] {'zb','y','zh','c'}, dimensions={0} | all-to-all | bytes 327680 | tf_op jit(solution)/shard_map/all_to_all | solution.py:531
  62.0 1.0 shard_map.114
  62.9 0.0 copy-start.7
  63.0 15.5 %all_to_all.16.offsets = f32[4,128,128]{2,1,0:T(8,128)S(1)} all-to-all(f32[4,128,128]{2,1,0:T(8,128)S(1)} %get-tuple-element.21), channel_id=1, replica_groups=mesh['x'=4,'zb'=2,'za'=4,'y'=4,'zh'=2,'c'=2] {'za'}, dimensions={0} | all-to-all | bytes 524288 | tf_op jit(solution)/shard_map/all_to_all | solution.py:539
  78.5 1.0 shard_map.115
  79.5 0.0 copy-start.4
  79.5 18.3 %all_to_all.17.got = f32[32,8,256]{2,1,0:T(8,128)S(1)} all-to-all(f32[32,8,256]{2,1,0:T(8,128)S(1)} %shard_map.115), channel_id=1, replica_groups=mesh['x'=4,'zb'=2,'za'=4,'y'=4,'zh'=2,'c'=2] {'x','y','c'}, dimensions={0} | all-to-all | bytes 524288 | tf_op jit(solution)/shard_map/all_to_all | solution.py:546
  97.7 1.7 %shard_map.116 = f32[5,16,16,128]{3,2,1,0:T(8,128)} custom-call(s32[8]{0:T(128)S(1)} %stack.31.place, f32[5,24,16,128]{3,2,1,0:T(8,128)S(1)} %get-tuple-element.19.w, f32[32,8,256]{2,1,0:T(8,128)S(1)} %all_to_all.17.got, f32[64,256]{1,0:T(8,128)S(1)} %get-tuple-element.24.hats, bf16[128,192]{1,0:T(8,128)(2,1)S(1)} %copy-done.8, bf16[384,256]{1,0:T(8,128)(2,1)S(1)} %copy-done.4), custom_call_target="tpu_custom_call" | custom-call | bytes 1048576 | tf_op jit(solution)/shard_map/pallas_call | solution.py:463
  (20 shorter events, 0.1 us)
Async XLA Ops:
  0.0 1.1 %copy-start = (f32[1,5,16,16,128]{4,3,2,1,0:T(8,128)S(1)}, f32[1,5,16,16,128]{4,3,2,1,0:T(8,128)}, u32[]{:S(2)}) copy-start(f32[1,5,16,16,128]{4,3,2,1,0:T(8,128)} %param.11) | copy-start | bytes 1966084
  1.1 4.6 %copy-start.1 = (f32[1,5,16,16,128]{4,3,2,1,0:T(8,128)S(1)}, f32[1,5,16,16,128]{4,3,2,1,0:T(8,128)}, u32[]{:S(2)}) copy-start(f32[1,5,16,16,128]{4,3,2,1,0:T(8,128)} %param.11) | copy-start | bytes 1966084
  1.1 4.6 %copy-start.2 = (f32[16,16,128]{2,1,0:T(8,128)S(1)}, f32[16,16,128]{2,1,0:T(8,128)}, u32[]{:S(2)}) copy-start(f32[16,16,128]{2,1,0:T(8,128)} %first.5) | copy-start | bytes 393220
  1.1 23.0 %collective-permute-start = (f32[16,16,128]{2,1,0:T(8,128)S(1)}, f32[16,16,128]{2,1,0:T(8,128)S(1)}, u32[]{:S(2)}, u32[]{:S(2)}) collective-permute-start(f32[16,16,128]{2,1,0:T(8,128)S(1)} %shard_map.109), channel_id=1, source_target_pairs={{0,16},{16,32},{32,48},{48,64},{64,80},{80,96},{96,112},{112,128},... | collective-permute-start | bytes 393224 | tf_op jit(solution)/shard_map/ppermute | solution.py:513
  6.8 22.0 %collective-permute-start.3 = (f32[10,16,128]{2,1,0:T(8,128)S(1)}, f32[10,16,128]{2,1,0:T(8,128)S(1)}, u32[]{:S(2)}, u32[]{:S(2)}) collective-permute-start(f32[10,16,128]{2,1,0:T(8,128)S(1)} %get-tuple-element.18.own_far), channel_id=1, source_target_pairs={{0,15},{1,2},{2,1},{3,4},{4,3},{5,6},{6,5},{7,8},{8,7},{9,10},{10,... | collective-permute-start | bytes 245768 | tf_op jit(solution)/shard_map/ppermute | solution.py:510
  22.2 10.8 %collective-permute-start.2 = (f32[4,16,128]{2,1,0:T(8,128)S(1)}, f32[4,16,128]{2,1,0:T(8,128)S(1)}, u32[]{:S(2)}, u32[]{:S(2)}) collective-permute-start(f32[4,16,128]{2,1,0:T(8,128)S(1)} %get-tuple-element.16), channel_id=1, source_target_pairs={{0,31},{1,18},{2,17},{3,20},{4,19},{5,22},{6,21},{7,24},{8,23},{9,... | collective-permute-start | bytes 98312 | tf_op jit(solution)/shard_map/ppermute | solution.py:511
  24.7 8.3 %copy-start.5 = (bf16[768,128]{1,0:T(8,128)(2,1)S(1)}, bf16[768,128]{1,0:T(8,128)(2,1)}, u32[]{:S(2)}) copy-start(bf16[768,128]{1,0:T(8,128)(2,1)} %constant.49.clone.down_y) | copy-start | bytes 589828
  24.7 8.3 %copy-start.9 = (bf16[64,384]{1,0:T(8,128)(2,1)S(1)}, bf16[64,384]{1,0:T(8,128)(2,1)}, u32[]{:S(2)}) copy-start(bf16[64,384]{1,0:T(8,128)(2,1)} %constant.50.clone.down_x) | copy-start | bytes 147460
  24.7 8.3 %copy-start.10 = (f32[64,128]{1,0:T(8,128)S(1)}, f32[64,128]{1,0:T(8,128)}, u32[]{:S(2)}) copy-start(f32[64,128]{1,0:T(8,128)} %constant.51.clone.stencil) | copy-start | bytes 98308
  24.7 8.3 %collective-permute-start.1 = (f32[14,16,128]{2,1,0:T(8,128)S(1)}, f32[14,16,128]{2,1,0:T(8,128)S(1)}, u32[]{:S(2)}, u32[]{:S(2)}) collective-permute-start(f32[14,16,128]{2,1,0:T(8,128)S(1)} %shard_map.111), channel_id=1, source_target_pairs={{0,1},{1,0},{2,3},{3,2},{4,5},{5,4},{6,7},{7,6},{8,9},{9,8},{10,11... | collective-permute-start | bytes 344072 | tf_op jit(solution)/shard_map/ppermute | solution.py:517
  34.7 27.3 %copy-start.3 = (f32[128,128]{1,0:T(8,128)S(1)}, f32[128,128]{1,0:T(8,128)}, u32[]{:S(2)}) copy-start(f32[128,128]{1,0:T(8,128)} %constant.54.clone.denom) | copy-start | bytes 196612
  34.7 27.3 %copy-start.6 = (bf16[128,480]{1,0:T(8,128)(2,1)S(1)}, bf16[128,480]{1,0:T(8,128)(2,1)}, u32[]{:S(2)}) copy-start(bf16[128,480]{1,0:T(8,128)(2,1)} %constant.52.clone.table) | copy-start | bytes 368644
  34.7 27.3 %copy-start.11 = (f32[8]{0:T(128)S(1)}, f32[8]{0:T(128)}, u32[]{:S(2)}) copy-start(f32[8]{0:T(128)} %constant.55.clone.shift_x) | copy-start | bytes 100
  62.9 15.5 %copy-start.7 = (bf16[2,64,384]{2,1,0:T(8,128)(2,1)S(1)}, bf16[2,64,384]{2,1,0:T(8,128)(2,1)}, u32[]{:S(2)}) copy-start(bf16[2,64,384]{2,1,0:T(8,128)(2,1)} %constant.53.clone.inverse_z) | copy-start | bytes 294916
  79.5 18.3 %copy-start.4 = (bf16[384,256]{1,0:T(8,128)(2,1)S(1)}, bf16[384,256]{1,0:T(8,128)(2,1)}, u32[]{:S(2)}) copy-start(bf16[384,256]{1,0:T(8,128)(2,1)} %constant.57.clone.up_y) | copy-start | bytes 589828
  79.5 18.3 %copy-start.8 = (bf16[128,192]{1,0:T(8,128)(2,1)S(1)}, bf16[128,192]{1,0:T(8,128)(2,1)}, u32[]{:S(2)}) copy-start(bf16[128,192]{1,0:T(8,128)(2,1)} %constant.56.clone.up_x) | copy-start | bytes 147460

commit v9 on v8

--- a/solution.py
+++ b/solution.py
@@ -127,7 +127,7 @@
     f32 = lambda a: jnp.asarray(a, jnp.float32)
     return (
         table_halves(block_pair(down_y), 0), table_halves(down_x, 1), f32(stencil),
-        table_halves(forward_z, 1), table_halves(inverse_z, 2), f32(denom), f32(shift_x),
+        table_halves(forward_z, 1), table_halves(inverse_z, 2), f32(denom), ShiftTable(shift_x),
         table_halves(up_x, 1), table_halves(block_pair(up_y), 0),
     )
 
@@ -455,20 +455,40 @@
             out[m, 2 * i + 1] = w[m, REACH + 2 * i + 1] + piece
 
 
+def whereabouts():
+    x, zb, za = (lax.axis_index(a) for a in TM)
+    y, zh, core = (lax.axis_index(a) for a in SPACE)
+    return ((x * 2 + zb) * 4 + za, core, za, x, 2 * y + core, zh, 32, zb)
+
+
+class ShiftTable:
+    def __init__(self, values):
+        self.values = [float(v) for v in values]
+
+    def __getitem__(self, at):
+        found = self.values[0]
+        for i, value in enumerate(self.values[1:], 1):
+            found = jnp.where(at == i, value, found)
+        return found
+
+
 def call(kernel, outs, scalars, *args, scratch=(), flops=0):
-    smem = pl.BlockSpec(memory_space=pltpu.SMEM)
     vmem = pl.BlockSpec(memory_space=pltpu.VMEM)
     single = not isinstance(outs, list)
     shapes = [jax.ShapeDtypeStruct(s, jnp.float32) for s in ([outs] if single else outs)]
+    tables = scalars[1:]
+    inner = kernel
+    if scalars:
+        kernel = lambda *refs: inner(whereabouts(), *tables, *refs)
     result = pl.pallas_call(
         kernel,
         out_shape=shapes[0] if single else shapes,
-        in_specs=[smem] * len(scalars) + [vmem] * len(args),
+        in_specs=[vmem] * len(args),
         out_specs=vmem if single else [vmem] * len(shapes),
         scratch_shapes=list(scratch),
         compiler_params=pltpu.CompilerParams(vmem_limit_bytes=32 * 1024 * 1024),
         cost_estimate=pl.CostEstimate(flops=flops, bytes_accessed=1 << 20, transcendentals=0),
-    )(*scalars, *args)
+    )(*args)
     return result
 
 
@@ -481,13 +501,7 @@
     down_y, down_x, stencil, forward_z, inverse_z, denom, shift_x, up_x, up_y = tables(
         coarse, rows, cols, depth_c
     )
-    position = lax.axis_index(TM)
-    core = lax.axis_index("c")
-    kx = 2 * lax.axis_index("y") + core
-    place = [position, core, lax.axis_index("za"), lax.axis_index("x"), kx]
-    place = jnp.stack(place + [lax.axis_index("zh"), slices, lax.axis_index("zb")])
-    place = place.astype(jnp.int32)
-
+    place = None
     last = call(last_kernel, (planes, rows, cols), [], u_old[0])
     halo, edge = (PACK, rows, cols), (REACH, rows, cols)
     g, own_near, own_far, edge_far = call(

time: 99.9 us -> 97.1 us (0.972)
  Pallas kernels: 6.93 us -> 3.7 us
    pallas_call x8, Pallas kernels: 6.93 us -> 3.7 us  [call(): pl.pallas_call(kernel, out_shape=shapes[0] if single else shapes, in_spec...]
  transfers between devices with their start and end apart: 4 -> 4, of which waited for: 1 -> 1; matrix products, arithmetic and copies ran while one was open for 0% -> 0% of each run, Pallas kernels for 2% -> 1%
where the time goes in v9:
time: 97.1 us; the launch traced here: 96.7 us
  blocking collectives  61 us (63%)
  starting transfers between devices  25.9 us (27%)
  waiting for transfers between devices  4.83 us (5%)
  Pallas kernels  3.7 us (4%)
  local copies, waits for them, and re-layouts  1.15 us (1%)
    all_to_all x1, blocking collectives, shards(): columns = lax.all_to_all(send, FORWARD, 0, 0, tiled=True)  27 us
    all_to_all x1, blocking collectives, shards(): returned = lax.all_to_all(back, ('x', 'y', 'c'), 0, 0, tiled=True)  18.3 us
    all_to_all x1, blocking collectives, shards(): gathered = lax.all_to_all(copies, 'za', 0, 0, tiled=True)  15.7 us
    ppermute x1, starting transfers between devices, shards(): lax.ppermute(own_far, SPACE, [(s, far_block(s)) for s in range(blocks)])  15.4 us
    ppermute x1, waiting for transfers between devices, shards(): start_far = lax.ppermute(edge_far, TM + SPACE, across)  4.82 us
    ppermute x1, starting transfers between devices, shards(): previous = lax.ppermute(last, TM, [(i, i + 1) for i in range(slices - 1)])  4.51 us
    ppermute x1, starting transfers between devices, shards(): near = lax.ppermute(near_out, 'c', [(0, 1), (1, 0)])  4.04 us
    pallas_call x8, Pallas kernels, call(): pl.pallas_call(kernel, out_shape=shapes[0] if single else shapes, in_spec...  3.7 us
  transfers between devices with their start and end apart: 4, of which 1 were waited for; matrix products, arithmetic and copies ran while one was open for 0% of the time, Pallas kernels for 1%

profile of v9, /device:TPU:1, one launch (start us, length us, event | category | flops | bytes accessed | tf_op | source)
XLA Modules:
  0.0 96.7 jit_solution(6952512206445891824)
XLA Ops:
  0.0 1.1 %copy-done = f32[1,5,16,16,128]{4,3,2,1,0:T(8,128)S(1)} copy-done((f32[1,5,16,16,128]{4,3,2,1,0:T(8,128)S(1)}, f32[1,5,16,16,128]{4,3,2,1,0:T(8,128)}, u32[]{:S(2)}) %copy-start) | copy-done | bytes 655384
  1.1 4.5 %collective-permute-start = (f32[16,16,128]{2,1,0:T(8,128)S(1)}, f32[16,16,128]{2,1,0:T(8,128)S(1)}, u32[]{:S(2)}, u32[]{:S(2)}) collective-permute-start(f32[16,16,128]{2,1,0:T(8,128)S(1)} %shard_map.100), channel_id=1, source_target_pairs={{0,16},{16,32},{32,48},{48,64},{64,80},{80,96},{96,112},{112,128},... | collective-permute-start | bytes 393224 | tf_op jit(solution)/shard_map/ppermute | solution.py:527
  5.6 0.5 shard_map.101
  6.2 15.4 %collective-permute-start.3 = (f32[10,16,128]{2,1,0:T(8,128)S(1)}, f32[10,16,128]{2,1,0:T(8,128)S(1)}, u32[]{:S(2)}, u32[]{:S(2)}) collective-permute-start(f32[10,16,128]{2,1,0:T(8,128)S(1)} %get-tuple-element.18.refs_6_), channel_id=1, source_target_pairs={{0,15},{1,2},{2,1},{3,4},{4,3},{5,6},{6,5},{7,8},{8,7},{9,10},{10,... | collective-permute-start | bytes 245768 | tf_op jit(solution)/shard_map/ppermute | solution.py:524
  21.5 1.9 %collective-permute-start.2 = (f32[4,16,128]{2,1,0:T(8,128)S(1)}, f32[4,16,128]{2,1,0:T(8,128)S(1)}, u32[]{:S(2)}, u32[]{:S(2)}) collective-permute-start(f32[4,16,128]{2,1,0:T(8,128)S(1)} %get-tuple-element.16), channel_id=1, source_target_pairs={{0,31},{1,18},{2,17},{3,20},{4,19},{5,22},{6,21},{7,24},{8,23},{9,... | collective-permute-start | bytes 98312 | tf_op jit(solution)/shard_map/ppermute | solution.py:525
  23.5 0.0 collective-permute-done.refs_1_
  23.5 0.0 copy-start.4
  23.5 0.0 copy-start.8
  23.5 0.0 copy-start.9
  23.6 4.0 %collective-permute-start.1 = (f32[14,16,128]{2,1,0:T(8,128)S(1)}, f32[14,16,128]{2,1,0:T(8,128)S(1)}, u32[]{:S(2)}, u32[]{:S(2)}) collective-permute-start(f32[14,16,128]{2,1,0:T(8,128)S(1)} %shard_map.102), channel_id=1, source_target_pairs={{0,1},{1,0},{2,3},{3,2},{4,5},{5,4},{6,7},{7,6},{8,9},{9,8},{10,11... | collective-permute-start | bytes 344072 | tf_op jit(solution)/shard_map/ppermute | solution.py:531
  27.6 0.0 collective-permute-done.3.halo
  27.6 4.8 %collective-permute-done.2.refs_3_ = f32[4,16,128]{2,1,0:T(8,128)S(1)} collective-permute-done((f32[4,16,128]{2,1,0:T(8,128)S(1)}, f32[4,16,128]{2,1,0:T(8,128)S(1)}, u32[]{:S(2)}, u32[]{:S(2)}) %collective-permute-start.2) | collective-permute-done | bytes 32800 | tf_op jit(solution)/shard_map/ppermute | solution.py:525
  32.5 1.1 %shard_map.104 = (f32[5,24,16,128]{3,2,1,0:T(8,128)S(1)}, f32[32,1,1280]{2,1,0:T(1,128)S(1)}, f32[64,256]{1,0:T(8,128)S(1)}) custom-call(f32[16,16,128]{2,1,0:T(8,128)S(1)} %copy-done.1, f32[16,16,128]{2,1,0:T(8,128)S(1)} %collective-permute-done.refs_1_, f32[14,16,128]{2,1,0:T(8,128)S(1)} %collective-permute-done.1.refs_2_, ...), custom_call_target="tpu_custom_call" | custom-call | bytes 1048576 | tf_op jit(solution)/shard_map/pallas_call | solution.py:483
  33.6 0.0 copy-start.2
  33.6 0.0 copy-start.5
  33.6 27.0 %all_to_all.15.refs_0_ = f32[32,1,1280]{2,1,0:T(1,128)S(1)} all-to-all(f32[32,1,1280]{2,1,0:T(1,128)S(1)} %get-tuple-element.20), channel_id=1, replica_groups=mesh['x'=4,'zb'=2,'za'=4,'y'=4,'zh'=2,'c'=2] {'zb','y','zh','c'}, dimensions={0} | all-to-all | bytes 327680 | tf_op jit(solution)/shard_map/all_to_all | solution.py:545
  60.6 0.4 shard_map.105
  61.0 0.0 copy-start.6
  61.0 15.7 %all_to_all.16.refs_0_ = f32[4,128,128]{2,1,0:T(8,128)S(1)} all-to-all(f32[4,128,128]{2,1,0:T(8,128)S(1)} %get-tuple-element.21), channel_id=1, replica_groups=mesh['x'=4,'zb'=2,'za'=4,'y'=4,'zh'=2,'c'=2] {'za'}, dimensions={0} | all-to-all | bytes 524288 | tf_op jit(solution)/shard_map/all_to_all | solution.py:553
  76.7 0.4 shard_map.106
  77.1 0.0 copy-start.3
  77.2 0.0 copy-start.7
  77.2 18.3 %all_to_all.17.refs_1_ = f32[32,8,256]{2,1,0:T(8,128)S(1)} all-to-all(f32[32,8,256]{2,1,0:T(8,128)S(1)} %shard_map.106), channel_id=1, replica_groups=mesh['x'=4,'zb'=2,'za'=4,'y'=4,'zh'=2,'c'=2] {'x','y','c'}, dimensions={0} | all-to-all | bytes 524288 | tf_op jit(solution)/shard_map/all_to_all | solution.py:560
  95.5 1.2 %shard_map.107 = f32[5,16,16,128]{3,2,1,0:T(8,128)} custom-call(f32[5,24,16,128]{3,2,1,0:T(8,128)S(1)} %get-tuple-element.19.refs_0_, f32[32,8,256]{2,1,0:T(8,128)S(1)} %all_to_all.17.refs_1_, f32[64,256]{1,0:T(8,128)S(1)} %get-tuple-element.24.refs_2_, bf16[128,192]{1,0:T(8,128)(2,1)S(1)} %copy-done.7, bf16[384,256]{1,0:T(8,128)(2,1)S(1)} %copy-done.3), custom_call_target="tpu_custom_call" | custom-call | bytes 1048576 | tf_op jit(solution)/shard_map/pallas_call | solution.py:483
  (15 shorter events, 0.1 us)
Async XLA Ops:
  0.0 1.1 %copy-start = (f32[1,5,16,16,128]{4,3,2,1,0:T(8,128)S(1)}, f32[1,5,16,16,128]{4,3,2,1,0:T(8,128)}, u32[]{:S(2)}) copy-start(f32[1,5,16,16,128]{4,3,2,1,0:T(8,128)} %param.10) | copy-start | bytes 1966084
  1.1 4.5 %copy-start.1 = (f32[16,16,128]{2,1,0:T(8,128)S(1)}, f32[16,16,128]{2,1,0:T(8,128)}, u32[]{:S(2)}) copy-start(f32[16,16,128]{2,1,0:T(8,128)} %refs_0_.3) | copy-start | bytes 393220
  1.1 22.4 %collective-permute-start = (f32[16,16,128]{2,1,0:T(8,128)S(1)}, f32[16,16,128]{2,1,0:T(8,128)S(1)}, u32[]{:S(2)}, u32[]{:S(2)}) collective-permute-start(f32[16,16,128]{2,1,0:T(8,128)S(1)} %shard_map.100), channel_id=1, source_target_pairs={{0,16},{16,32},{32,48},{48,64},{64,80},{80,96},{96,112},{112,128},... | collective-permute-start | bytes 393224 | tf_op jit(solution)/shard_map/ppermute | solution.py:527
  6.2 21.5 %collective-permute-start.3 = (f32[10,16,128]{2,1,0:T(8,128)S(1)}, f32[10,16,128]{2,1,0:T(8,128)S(1)}, u32[]{:S(2)}, u32[]{:S(2)}) collective-permute-start(f32[10,16,128]{2,1,0:T(8,128)S(1)} %get-tuple-element.18.refs_6_), channel_id=1, source_target_pairs={{0,15},{1,2},{2,1},{3,4},{4,3},{5,6},{6,5},{7,8},{8,7},{9,10},{10,... | collective-permute-start | bytes 245768 | tf_op jit(solution)/shard_map/ppermute | solution.py:524
  21.5 10.9 %collective-permute-start.2 = (f32[4,16,128]{2,1,0:T(8,128)S(1)}, f32[4,16,128]{2,1,0:T(8,128)S(1)}, u32[]{:S(2)}, u32[]{:S(2)}) collective-permute-start(f32[4,16,128]{2,1,0:T(8,128)S(1)} %get-tuple-element.16), channel_id=1, source_target_pairs={{0,31},{1,18},{2,17},{3,20},{4,19},{5,22},{6,21},{7,24},{8,23},{9,... | collective-permute-start | bytes 98312 | tf_op jit(solution)/shard_map/ppermute | solution.py:525
  23.5 8.9 %copy-start.4 = (bf16[768,128]{1,0:T(8,128)(2,1)S(1)}, bf16[768,128]{1,0:T(8,128)(2,1)}, u32[]{:S(2)}) copy-start(bf16[768,128]{1,0:T(8,128)(2,1)} %constant.16.clone.refs_8_) | copy-start | bytes 589828
  23.5 8.9 %copy-start.8 = (bf16[64,384]{1,0:T(8,128)(2,1)S(1)}, bf16[64,384]{1,0:T(8,128)(2,1)}, u32[]{:S(2)}) copy-start(bf16[64,384]{1,0:T(8,128)(2,1)} %constant.17.clone.refs_9_) | copy-start | bytes 147460
  23.5 8.9 %copy-start.9 = (f32[64,128]{1,0:T(8,128)S(1)}, f32[64,128]{1,0:T(8,128)}, u32[]{:S(2)}) copy-start(f32[64,128]{1,0:T(8,128)} %constant.18.clone.refs_10_) | copy-start | bytes 98308
  23.6 8.9 %collective-permute-start.1 = (f32[14,16,128]{2,1,0:T(8,128)S(1)}, f32[14,16,128]{2,1,0:T(8,128)S(1)}, u32[]{:S(2)}, u32[]{:S(2)}) collective-permute-start(f32[14,16,128]{2,1,0:T(8,128)S(1)} %shard_map.102), channel_id=1, source_target_pairs={{0,1},{1,0},{2,3},{3,2},{4,5},{5,4},{6,7},{7,6},{8,9},{9,8},{10,11... | collective-permute-start | bytes 344072 | tf_op jit(solution)/shard_map/ppermute | solution.py:531
  33.6 27.0 %copy-start.2 = (f32[128,128]{1,0:T(8,128)S(1)}, f32[128,128]{1,0:T(8,128)}, u32[]{:S(2)}) copy-start(f32[128,128]{1,0:T(8,128)} %constant.21.clone.refs_2_.refs_3_) | copy-start | bytes 196612
  33.6 27.0 %copy-start.5 = (bf16[128,480]{1,0:T(8,128)(2,1)S(1)}, bf16[128,480]{1,0:T(8,128)(2,1)}, u32[]{:S(2)}) copy-start(bf16[128,480]{1,0:T(8,128)(2,1)} %constant.19.clone.refs_1_) | copy-start | bytes 368644
  61.0 15.7 %copy-start.6 = (bf16[2,64,384]{2,1,0:T(8,128)(2,1)S(1)}, bf16[2,64,384]{2,1,0:T(8,128)(2,1)}, u32[]{:S(2)}) copy-start(bf16[2,64,384]{2,1,0:T(8,128)(2,1)} %constant.20.clone.refs_4_) | copy-start | bytes 294916
  77.1 18.3 %copy-start.3 = (bf16[384,256]{1,0:T(8,128)(2,1)S(1)}, bf16[384,256]{1,0:T(8,128)(2,1)}, u32[]{:S(2)}) copy-start(bf16[384,256]{1,0:T(8,128)(2,1)} %constant.23.clone.refs_4_) | copy-start | bytes 589828
  77.2 18.3 %copy-start.7 = (bf16[128,192]{1,0:T(8,128)(2,1)S(1)}, bf16[128,192]{1,0:T(8,128)(2,1)}, u32[]{:S(2)}) copy-start(bf16[128,192]{1,0:T(8,128)(2,1)} %constant.22.clone.refs_3_) | copy-start | bytes 147460

commit v10 on v9

--- a/solution.py
+++ b/solution.py
@@ -322,12 +322,13 @@
     edge_rows = first.shape[1]
     middle = jnp.zeros((rows - 2 * edge_rows, first.shape[2]), jnp.float32)
     edges = jnp.concatenate([w[4, REACH], middle, w[4, REACH + planes - 1]], 0)
-    left = [
-        times_table(jnp.concatenate(pair, 1), table)
-        for pair in ((q0, q1), (paired(2), paired(4)), (restart, edges))
-    ]
-    spectral = table_times(down_x[...], jnp.concatenate(left, 1))
-    width = left[0].shape[1]
+    fields = jnp.concatenate([q0, q1, paired(2), paired(4), restart, edges], 1)
+    lines = table_times(down_x[...], fields)
+    pair_width = 2 * first.shape[2]
+    spectral = jnp.concatenate(
+        [times_table(lines[:, i * pair_width : (i + 1) * pair_width], table) for i in range(3)], 1
+    )
+    width = table.shape[1]
     states = spectral[:, width : 2 * width]
     third = spectral[:, 2 * width :]
     count = spectral.shape[0]

time: 97.1 us -> 97 us (level)
  no operation moved by 1% of the time
where the time goes in v10:
time: 97 us; the launch traced here: 96.6 us
  blocking collectives  61 us (63%)
  starting transfers between devices  25.9 us (27%)
  waiting for transfers between devices  4.83 us (5%)
  Pallas kernels  3.67 us (4%)
  local copies, waits for them, and re-layouts  1.15 us (1%)
    all_to_all x1, blocking collectives, shards(): columns = lax.all_to_all(send, FORWARD, 0, 0, tiled=True)  27 us
    all_to_all x1, blocking collectives, shards(): returned = lax.all_to_all(back, ('x', 'y', 'c'), 0, 0, tiled=True)  18.3 us
    all_to_all x1, blocking collectives, shards(): gathered = lax.all_to_all(copies, 'za', 0, 0, tiled=True)  15.7 us
    ppermute x1, starting transfers between devices, shards(): lax.ppermute(own_far, SPACE, [(s, far_block(s)) for s in range(blocks)])  15.4 us
    ppermute x1, waiting for transfers between devices, shards(): start_far = lax.ppermute(edge_far, TM + SPACE, across)  4.82 us
    ppermute x1, starting transfers between devices, shards(): previous = lax.ppermute(last, TM, [(i, i + 1) for i in range(slices - 1)])  4.51 us
    ppermute x1, starting transfers between devices, shards(): near = lax.ppermute(near_out, 'c', [(0, 1), (1, 0)])  4.04 us
    pallas_call x8, Pallas kernels, call(): pl.pallas_call(kernel, out_shape=shapes[0] if single else shapes, in_spec...  3.67 us
  transfers between devices with their start and end apart: 4, of which 1 were waited for; matrix products, arithmetic and copies ran while one was open for 0% of the time, Pallas kernels for 1%

profile of v10, /device:TPU:1, one launch (start us, length us, event | category | flops | bytes accessed | tf_op | source)
XLA Modules:
  0.0 96.6 jit_solution(1389980527130374395)
XLA Ops:
  0.0 1.1 %copy-done = f32[1,5,16,16,128]{4,3,2,1,0:T(8,128)S(1)} copy-done((f32[1,5,16,16,128]{4,3,2,1,0:T(8,128)S(1)}, f32[1,5,16,16,128]{4,3,2,1,0:T(8,128)}, u32[]{:S(2)}) %copy-start) | copy-done | bytes 655384
  1.1 4.5 %collective-permute-start = (f32[16,16,128]{2,1,0:T(8,128)S(1)}, f32[16,16,128]{2,1,0:T(8,128)S(1)}, u32[]{:S(2)}, u32[]{:S(2)}) collective-permute-start(f32[16,16,128]{2,1,0:T(8,128)S(1)} %shard_map.100), channel_id=1, source_target_pairs={{0,16},{16,32},{32,48},{48,64},{64,80},{80,96},{96,112},{112,128},... | collective-permute-start | bytes 393224 | tf_op jit(solution)/shard_map/ppermute | solution.py:528
  5.6 0.5 shard_map.101
  6.2 15.4 %collective-permute-start.3 = (f32[10,16,128]{2,1,0:T(8,128)S(1)}, f32[10,16,128]{2,1,0:T(8,128)S(1)}, u32[]{:S(2)}, u32[]{:S(2)}) collective-permute-start(f32[10,16,128]{2,1,0:T(8,128)S(1)} %get-tuple-element.18.refs_6_), channel_id=1, source_target_pairs={{0,15},{1,2},{2,1},{3,4},{4,3},{5,6},{6,5},{7,8},{8,7},{9,10},{10,... | collective-permute-start | bytes 245768 | tf_op jit(solution)/shard_map/ppermute | solution.py:525
  21.5 1.9 %collective-permute-start.2 = (f32[4,16,128]{2,1,0:T(8,128)S(1)}, f32[4,16,128]{2,1,0:T(8,128)S(1)}, u32[]{:S(2)}, u32[]{:S(2)}) collective-permute-start(f32[4,16,128]{2,1,0:T(8,128)S(1)} %get-tuple-element.16), channel_id=1, source_target_pairs={{0,31},{1,18},{2,17},{3,20},{4,19},{5,22},{6,21},{7,24},{8,23},{9,... | collective-permute-start | bytes 98312 | tf_op jit(solution)/shard_map/ppermute | solution.py:526
  23.5 0.0 collective-permute-done.refs_1_
  23.5 0.0 copy-start.4
  23.5 0.0 copy-start.8
  23.5 0.0 copy-start.9
  23.6 4.0 %collective-permute-start.1 = (f32[14,16,128]{2,1,0:T(8,128)S(1)}, f32[14,16,128]{2,1,0:T(8,128)S(1)}, u32[]{:S(2)}, u32[]{:S(2)}) collective-permute-start(f32[14,16,128]{2,1,0:T(8,128)S(1)} %shard_map.102), channel_id=1, source_target_pairs={{0,1},{1,0},{2,3},{3,2},{4,5},{5,4},{6,7},{7,6},{8,9},{9,8},{10,11... | collective-permute-start | bytes 344072 | tf_op jit(solution)/shard_map/ppermute | solution.py:532
  27.6 0.0 collective-permute-done.3.halo
  27.6 4.8 %collective-permute-done.2.refs_3_ = f32[4,16,128]{2,1,0:T(8,128)S(1)} collective-permute-done((f32[4,16,128]{2,1,0:T(8,128)S(1)}, f32[4,16,128]{2,1,0:T(8,128)S(1)}, u32[]{:S(2)}, u32[]{:S(2)}) %collective-permute-start.2) | collective-permute-done | bytes 32800 | tf_op jit(solution)/shard_map/ppermute | solution.py:526
  32.5 1.1 %shard_map.104 = (f32[5,24,16,128]{3,2,1,0:T(8,128)S(1)}, f32[32,1,1280]{2,1,0:T(1,128)S(1)}, f32[64,256]{1,0:T(8,128)S(1)}) custom-call(f32[16,16,128]{2,1,0:T(8,128)S(1)} %copy-done.1, f32[16,16,128]{2,1,0:T(8,128)S(1)} %collective-permute-done.refs_1_, f32[14,16,128]{2,1,0:T(8,128)S(1)} %collective-permute-done.1.refs_2_, ...), custom_call_target="tpu_custom_call" | custom-call | bytes 1048576 | tf_op jit(solution)/shard_map/pallas_call | solution.py:484
  33.5 0.0 copy-start.2
  33.6 0.0 copy-start.5
  33.6 27.0 %all_to_all.15.refs_0_ = f32[32,1,1280]{2,1,0:T(1,128)S(1)} all-to-all(f32[32,1,1280]{2,1,0:T(1,128)S(1)} %get-tuple-element.20), channel_id=1, replica_groups=mesh['x'=4,'zb'=2,'za'=4,'y'=4,'zh'=2,'c'=2] {'zb','y','zh','c'}, dimensions={0} | all-to-all | bytes 327680 | tf_op jit(solution)/shard_map/all_to_all | solution.py:546
  60.6 0.4 shard_map.105
  61.0 0.0 copy-start.6
  61.0 15.7 %all_to_all.16.refs_0_ = f32[4,128,128]{2,1,0:T(8,128)S(1)} all-to-all(f32[4,128,128]{2,1,0:T(8,128)S(1)} %get-tuple-element.21), channel_id=1, replica_groups=mesh['x'=4,'zb'=2,'za'=4,'y'=4,'zh'=2,'c'=2] {'za'}, dimensions={0} | all-to-all | bytes 524288 | tf_op jit(solution)/shard_map/all_to_all | solution.py:554
  76.7 0.4 shard_map.106
  77.1 0.0 copy-start.3
  77.1 0.0 copy-start.7
  77.1 18.3 %all_to_all.17.refs_1_ = f32[32,8,256]{2,1,0:T(8,128)S(1)} all-to-all(f32[32,8,256]{2,1,0:T(8,128)S(1)} %shard_map.106), channel_id=1, replica_groups=mesh['x'=4,'zb'=2,'za'=4,'y'=4,'zh'=2,'c'=2] {'x','y','c'}, dimensions={0} | all-to-all | bytes 524288 | tf_op jit(solution)/shard_map/all_to_all | solution.py:561
  95.4 1.2 %shard_map.107 = f32[5,16,16,128]{3,2,1,0:T(8,128)} custom-call(f32[5,24,16,128]{3,2,1,0:T(8,128)S(1)} %get-tuple-element.19.refs_0_, f32[32,8,256]{2,1,0:T(8,128)S(1)} %all_to_all.17.refs_1_, f32[64,256]{1,0:T(8,128)S(1)} %get-tuple-element.24.refs_2_, bf16[128,192]{1,0:T(8,128)(2,1)S(1)} %copy-done.7, bf16[384,256]{1,0:T(8,128)(2,1)S(1)} %copy-done.3), custom_call_target="tpu_custom_call" | custom-call | bytes 1048576 | tf_op jit(solution)/shard_map/pallas_call | solution.py:484
  (15 shorter events, 0.1 us)
Async XLA Ops:
  0.0 1.1 %copy-start = (f32[1,5,16,16,128]{4,3,2,1,0:T(8,128)S(1)}, f32[1,5,16,16,128]{4,3,2,1,0:T(8,128)}, u32[]{:S(2)}) copy-start(f32[1,5,16,16,128]{4,3,2,1,0:T(8,128)} %param.10) | copy-start | bytes 1966084
  1.1 4.5 %copy-start.1 = (f32[16,16,128]{2,1,0:T(8,128)S(1)}, f32[16,16,128]{2,1,0:T(8,128)}, u32[]{:S(2)}) copy-start(f32[16,16,128]{2,1,0:T(8,128)} %refs_0_.3) | copy-start | bytes 393220
  1.1 22.4 %collective-permute-start = (f32[16,16,128]{2,1,0:T(8,128)S(1)}, f32[16,16,128]{2,1,0:T(8,128)S(1)}, u32[]{:S(2)}, u32[]{:S(2)}) collective-permute-start(f32[16,16,128]{2,1,0:T(8,128)S(1)} %shard_map.100), channel_id=1, source_target_pairs={{0,16},{16,32},{32,48},{48,64},{64,80},{80,96},{96,112},{112,128},... | collective-permute-start | bytes 393224 | tf_op jit(solution)/shard_map/ppermute | solution.py:528
  6.2 21.5 %collective-permute-start.3 = (f32[10,16,128]{2,1,0:T(8,128)S(1)}, f32[10,16,128]{2,1,0:T(8,128)S(1)}, u32[]{:S(2)}, u32[]{:S(2)}) collective-permute-start(f32[10,16,128]{2,1,0:T(8,128)S(1)} %get-tuple-element.18.refs_6_), channel_id=1, source_target_pairs={{0,15},{1,2},{2,1},{3,4},{4,3},{5,6},{6,5},{7,8},{8,7},{9,10},{10,... | collective-permute-start | bytes 245768 | tf_op jit(solution)/shard_map/ppermute | solution.py:525
  21.5 10.9 %collective-permute-start.2 = (f32[4,16,128]{2,1,0:T(8,128)S(1)}, f32[4,16,128]{2,1,0:T(8,128)S(1)}, u32[]{:S(2)}, u32[]{:S(2)}) collective-permute-start(f32[4,16,128]{2,1,0:T(8,128)S(1)} %get-tuple-element.16), channel_id=1, source_target_pairs={{0,31},{1,18},{2,17},{3,20},{4,19},{5,22},{6,21},{7,24},{8,23},{9,... | collective-permute-start | bytes 98312 | tf_op jit(solution)/shard_map/ppermute | solution.py:526
  23.5 8.9 %copy-start.4 = (bf16[768,128]{1,0:T(8,128)(2,1)S(1)}, bf16[768,128]{1,0:T(8,128)(2,1)}, u32[]{:S(2)}) copy-start(bf16[768,128]{1,0:T(8,128)(2,1)} %constant.16.clone.refs_8_) | copy-start | bytes 589828
  23.5 8.9 %copy-start.8 = (bf16[64,384]{1,0:T(8,128)(2,1)S(1)}, bf16[64,384]{1,0:T(8,128)(2,1)}, u32[]{:S(2)}) copy-start(bf16[64,384]{1,0:T(8,128)(2,1)} %constant.17.clone.refs_9_) | copy-start | bytes 147460
  23.5 8.9 %copy-start.9 = (f32[64,128]{1,0:T(8,128)S(1)}, f32[64,128]{1,0:T(8,128)}, u32[]{:S(2)}) copy-start(f32[64,128]{1,0:T(8,128)} %constant.18.clone.refs_10_) | copy-start | bytes 98308
  23.6 8.9 %collective-permute-start.1 = (f32[14,16,128]{2,1,0:T(8,128)S(1)}, f32[14,16,128]{2,1,0:T(8,128)S(1)}, u32[]{:S(2)}, u32[]{:S(2)}) collective-permute-start(f32[14,16,128]{2,1,0:T(8,128)S(1)} %shard_map.102), channel_id=1, source_target_pairs={{0,1},{1,0},{2,3},{3,2},{4,5},{5,4},{6,7},{7,6},{8,9},{9,8},{10,11... | collective-permute-start | bytes 344072 | tf_op jit(solution)/shard_map/ppermute | solution.py:532
  33.5 27.0 %copy-start.2 = (f32[128,128]{1,0:T(8,128)S(1)}, f32[128,128]{1,0:T(8,128)}, u32[]{:S(2)}) copy-start(f32[128,128]{1,0:T(8,128)} %constant.21.clone.refs_2_.refs_3_) | copy-start | bytes 196612
  33.6 27.0 %copy-start.5 = (bf16[128,480]{1,0:T(8,128)(2,1)S(1)}, bf16[128,480]{1,0:T(8,128)(2,1)}, u32[]{:S(2)}) copy-start(bf16[128,480]{1,0:T(8,128)(2,1)} %constant.19.clone.refs_1_) | copy-start | bytes 368644
  61.0 15.7 %copy-start.6 = (bf16[2,64,384]{2,1,0:T(8,128)(2,1)S(1)}, bf16[2,64,384]{2,1,0:T(8,128)(2,1)}, u32[]{:S(2)}) copy-start(bf16[2,64,384]{2,1,0:T(8,128)(2,1)} %constant.20.clone.refs_4_) | copy-start | bytes 294916
  77.1 18.3 %copy-start.3 = (bf16[384,256]{1,0:T(8,128)(2,1)S(1)}, bf16[384,256]{1,0:T(8,128)(2,1)}, u32[]{:S(2)}) copy-start(bf16[384,256]{1,0:T(8,128)(2,1)} %constant.23.clone.refs_4_) | copy-start | bytes 589828
  77.1 18.3 %copy-start.7 = (bf16[128,192]{1,0:T(8,128)(2,1)S(1)}, bf16[128,192]{1,0:T(8,128)(2,1)}, u32[]{:S(2)}) copy-start(bf16[128,192]{1,0:T(8,128)(2,1)} %constant.22.clone.refs_3_) | copy-start | bytes 147460
